TPU v7x, 512 devices: a whole 4x8x8 slice. The times are simulated.
512 devices in a mesh: seq: 128 (over z_hi, y, x), mp: 4 (over z_lo, core).
Axes of the slice: x: 4, y: 8, z: 8 (z_hi: 4, z_lo: 2; z = z_hi * 2 + z_lo), core: 2. Of those that a mesh axis runs over, the one named last changes fastest.
Arguments:
- queries: bfloat16 [65536, 2048], P('seq', 'mp'), may hold values from -24 to 24
- keys: bfloat16 [65536, 2048], P('seq', 'mp'), may hold values from -24 to 24
- values: bfloat16 [65536, 2048], P('seq', 'mp'), may hold values from -6 to 6
- out_weight: bfloat16 [2048, 4096], P('mp', 'seq'), may hold values from -0.125 to 0.125
Outputs:
- layer_out: bfloat16 [65536, 4096], P('seq', 'mp')
All inputs are finite; a program needn't handle non-finite values.
Results may differ from a plain program's by a relative error of at most 0.013.
Values may be sent and summed in bfloat16 or wider, within the bound.
No kernel may reach another device: no remote copies, remote signals or barrier semaphores. Data moves between devices by JAX's collectives and lax.ppermute only.
A program may use at most 64 MiB of HBM per device.

v0:
```python
import jax
import jax.numpy as jnp
from jax import lax
from jax.sharding import PartitionSpec as P

DH = 128


def shifted(value, axis, steps):
    count = lax.axis_size(axis)
    first, last = (max(0, -steps), min(count, count - steps))
    return lax.ppermute(value, axis, [(source, source + steps) for source in range(first, last)])


def column_attend(arrays):
    query_col, key_col, value_col = arrays
    spread, parts, groups, size = query_col.shape
    row_count = parts // 2
    factor = size ** (-0.5)
    query_five = query_col.reshape(spread, row_count, 2, groups, size)
    key_five = key_col.reshape(spread, row_count, 2, groups, size)
    value_five = value_col.reshape(spread, row_count, 2, groups, size)
    scores = (
        jnp.einsum("arxgd,asxgd->arxgs", query_five, key_five, preferred_element_type=jnp.float32)
        * factor
    )
    earlier_row = jnp.arange(row_count)[None, :] < jnp.arange(row_count)[:, None]
    visible = earlier_row[None, :, None, None, :]
    col_max = jnp.max(jnp.where(visible, scores, jnp.float32(-1e30)), axis=-1)
    col_exp = jnp.where(visible, jnp.exp(scores - col_max[..., None]), jnp.float32(0.0))
    col_total = jnp.sum(col_exp, axis=-1)
    col_out = jnp.einsum(
        "arxgs,asxgd->arxgd",
        col_exp.astype(jnp.bfloat16),
        value_five,
        preferred_element_type=jnp.float32,
    )
    return (
        col_out.reshape(spread, parts, groups, size),
        col_max.reshape(spread, parts, groups),
        col_total.reshape(spread, parts, groups),
    )


def body(queries, keys, values, out_weight):
    rows_here, width_here = queries.shape
    local_heads = width_here // DH
    parts = lax.axis_size("seq")
    spread = rows_here // parts
    parity = lax.axis_index("seq") % 2
    factor = DH ** (-0.5)
    stacked = jnp.stack([keys, values])
    earlier = shifted(stacked, "seq", 1)
    key_rows = jnp.concatenate([earlier[0], keys], axis=0).reshape(2 * rows_here, local_heads, DH)
    value_rows = jnp.concatenate([earlier[1], values], axis=0).reshape(
        2 * rows_here, local_heads, DH
    )
    query_heads = queries.reshape(rows_here, local_heads, DH)
    scores = (
        jnp.einsum("qhd,khd->qhk", query_heads, key_rows, preferred_element_type=jnp.float32)
        * factor
    )
    own_place = jnp.arange(rows_here)
    query_place = parity * rows_here + own_place
    key_place = jnp.concatenate([own_place, parity * rows_here + own_place])
    key_live = jnp.concatenate(
        [jnp.broadcast_to(parity == 1, (rows_here,)), jnp.ones((rows_here,), bool)]
    )
    visible = (key_live[None, :] & (key_place[None, :] <= query_place[:, None]))[:, None, :]
    row_max = jnp.max(jnp.where(visible, scores, jnp.float32(-1e30)), axis=-1)
    row_exp = jnp.where(visible, jnp.exp(scores - row_max[..., None]), jnp.float32(0.0))
    row_total = jnp.sum(row_exp, axis=-1)
    row_out = jnp.einsum(
        "qhk,khd->qhd", row_exp.astype(jnp.bfloat16), value_rows, preferred_element_type=jnp.float32
    )
    query_cols = queries.reshape(spread, parts, local_heads, DH)
    key_cols = keys.reshape(spread, parts, local_heads, DH)
    value_cols = values.reshape(spread, parts, local_heads, DH)
    arrived = (
        lax.all_to_all(query_cols, "seq", split_axis=1, concat_axis=1, tiled=True),
        lax.all_to_all(key_cols, "seq", split_axis=1, concat_axis=1, tiled=True),
        lax.all_to_all(value_cols, "seq", split_axis=1, concat_axis=1, tiled=True),
    )
    result = column_attend(arrived)
    col_out, col_max, col_total = (
        lax.all_to_all(result[0], "seq", split_axis=1, concat_axis=1, tiled=True),
        lax.all_to_all(result[1], "seq", split_axis=1, concat_axis=1, tiled=True),
        lax.all_to_all(result[2], "seq", split_axis=1, concat_axis=1, tiled=True),
    )
    col_out = col_out.reshape(rows_here, local_heads, DH)
    col_max = col_max.reshape(rows_here, local_heads)
    col_total = col_total.reshape(rows_here, local_heads)
    highest = jnp.maximum(row_max, col_max)
    row_factor = jnp.exp(row_max - highest)
    col_factor = jnp.exp(col_max - highest)
    mixed = (row_factor[..., None] * row_out + col_factor[..., None] * col_out) / (
        row_factor * row_total + col_factor * col_total
    )[..., None]
    attended = mixed.astype(jnp.bfloat16).reshape(rows_here, width_here)
    partial_value = jnp.dot(
        attended,
        lax.all_gather(out_weight, "seq", axis=1, tiled=True),
        preferred_element_type=jnp.float32,
    )
    return lax.psum_scatter(
        partial_value.astype(jnp.bfloat16), "mp", scatter_dimension=1, tiled=True
    )


def solution(mesh):
    placed = (P("seq", "mp"), P("seq", "mp"), P("seq", "mp"), P("mp", "seq"))
    return jax.shard_map(
        body, mesh=mesh, in_specs=placed, out_specs=P("seq", "mp"), check_vma=False
    )
```

profile of v0, /device:TPU:1, one launch (start us, length us, event | category | flops | bytes accessed | tf_op | source)
XLA Modules:
  0.0 289.4 jit_solution(16924456530860799502)
XLA Ops:
  6.5 0.0 copy-start.1
  6.5 0.0 copy-start.2
  6.5 0.0 all-gather.2.cloned.1.call-start
  6.5 0.7 all-gather.2.cloned.1.call-update
  7.3 1.2 reshape.139
  8.4 1.0 copy.80
  9.4 20.8 %all-to-all-start = ((bf16[4,128,4,128]{3,2,0,1:T(4,128)(2,1)}), bf16[4,128,4,128]{3,2,0,1:T(4,128)(2,1)S(1)}, u32[]{:S(2)}, u32[]{:S(2)}) async-start(bf16[4,128,4,128]{3,2,0,1:T(4,128)(2,1)} %copy.80), calls=%async_computation | async-start | bytes 1048576 | tf_op jit(solution)/shard_map/all_to_all | solution.py:81
  30.2 1.2 reshape.141
  31.4 1.0 copy.82
  32.4 16.6 %all-to-all-done = bf16[4,128,4,128]{3,2,0,1:T(4,128)(2,1)S(1)} async-done(((bf16[4,128,4,128]{3,2,0,1:T(4,128)(2,1)}), bf16[4,128,4,128]{3,2,0,1:T(4,128)(2,1)S(1)}, u32[]{:S(2)}, u32[]{:S(2)}) %all-to-all-start) | async-done | bytes 524320 | tf_op jit(solution)/shard_map/all_to_all | solution.py:81
  49.0 9.8 %all-to-all-start.1 = ((bf16[4,128,4,128]{3,2,0,1:T(4,128)(2,1)}), bf16[4,128,4,128]{3,2,0,1:T(4,128)(2,1)}, u32[]{:S(2)}, u32[]{:S(2)}) async-start(bf16[4,128,4,128]{3,2,0,1:T(4,128)(2,1)} %copy.82), calls=%async_computation.1 | async-start | bytes 1048576 | tf_op jit(solution)/shard_map/all_to_all | solution.py:80
  58.8 1.2 reshape.145
  60.0 1.0 copy.91
  61.0 15.5 %all-to-all-done.1 = bf16[4,128,4,128]{3,2,0,1:T(4,128)(2,1)} async-done(((bf16[4,128,4,128]{3,2,0,1:T(4,128)(2,1)}), bf16[4,128,4,128]{3,2,0,1:T(4,128)(2,1)}, u32[]{:S(2)}, u32[]{:S(2)}) %all-to-all-start.1) | async-done | bytes 524320 | tf_op jit(solution)/shard_map/all_to_all | solution.py:80
  76.4 9.3 %all-to-all-start.3 = ((bf16[4,128,4,128]{3,2,0,1:T(4,128)(2,1)}), bf16[4,128,4,128]{3,2,0,1:T(4,128)(2,1)S(1)}, u32[]{:S(2)}, u32[]{:S(2)}) async-start(bf16[4,128,4,128]{3,2,0,1:T(4,128)(2,1)} %copy.91), calls=%async_computation.3 | async-start | bytes 1048576 | tf_op jit(solution)/shard_map/all_to_all | solution.py:82
  85.7 0.0 copy-done.1
  85.7 0.2 copy.74
  85.9 0.0 copy-done.2
  86.0 0.2 copy.75
  86.2 1.1 pad_maximum_fusion
  87.3 3.4 %collective-permute-start = (bf16[2,512,512]{1,2,0:T(8,128)(2,1)}, bf16[2,512,512]{1,2,0:T(8,128)(2,1)}, u32[]{:S(2)}, u32[]{:S(2)}) collective-permute-start(bf16[2,512,512]{1,2,0:T(8,128)(2,1)} %pad_maximum_fusion), channel_id=1, source_target_pairs={{0,4},{4,8},{8,12},{12,16},{16,20},{20,24},{24,28},{28,32},{32,36}... | collective-permute-start | bytes 3145736 | tf_op jit(solution)/shard_map/ppermute | solution.py:12
  90.7 1.6 select_reduce_fusion
  92.4 0.3 fusion.29
  92.6 0.2 copy.98
  92.8 0.9 copy.99
  93.7 11.7 %all-to-all-done.3 = bf16[4,128,4,128]{3,2,0,1:T(4,128)(2,1)S(1)} async-done(((bf16[4,128,4,128]{3,2,0,1:T(4,128)(2,1)}), bf16[4,128,4,128]{3,2,0,1:T(4,128)(2,1)S(1)}, u32[]{:S(2)}, u32[]{:S(2)}) %all-to-all-start.3) | async-done | bytes 524320 | tf_op jit(solution)/shard_map/all_to_all | solution.py:82
  105.4 8.8 %all-to-all-start.5 = ((f32[4,128,4]{2,0,1:T(4,128)}), f32[4,128,4]{2,0,1:T(4,128)S(1)}, u32[]{:S(2)}, u32[]{:S(2)}) async-start(f32[4,128,4]{2,0,1:T(4,128)} %copy.99), calls=%async_computation.5 | async-start | bytes 524288 | tf_op jit(solution)/shard_map/all_to_all | solution.py:88
  114.3 0.2 copy.86
  114.4 0.9 copy.87
  115.3 43.3 %all-to-all-done.5 = f32[4,128,4]{2,0,1:T(4,128)S(1)} async-done(((f32[4,128,4]{2,0,1:T(4,128)}), f32[4,128,4]{2,0,1:T(4,128)S(1)}, u32[]{:S(2)}, u32[]{:S(2)}) %all-to-all-start.5) | async-done | bytes 8224 | tf_op jit(solution)/shard_map/all_to_all | solution.py:88
  158.7 6.3 %all-to-all-start.2 = ((f32[4,128,4]{2,0,1:T(4,128)}), f32[4,128,4]{2,0,1:T(4,128)S(1)}, u32[]{:S(2)}, u32[]{:S(2)}) async-start(f32[4,128,4]{2,0,1:T(4,128)} %copy.87), calls=%async_computation.2 | async-start | bytes 524288 | tf_op jit(solution)/shard_map/all_to_all | solution.py:87
  165.0 0.4 convolution_bitcast_fusion
  165.5 0.8 copy.95
  166.3 1.6 copy.96
  167.9 13.1 %all-to-all-done.2 = f32[4,128,4]{2,0,1:T(4,128)S(1)} async-done(((f32[4,128,4]{2,0,1:T(4,128)}), f32[4,128,4]{2,0,1:T(4,128)S(1)}, u32[]{:S(2)}, u32[]{:S(2)}) %all-to-all-start.2) | async-done | bytes 8224 | tf_op jit(solution)/shard_map/all_to_all | solution.py:87
  181.0 8.2 %all-to-all-start.4 = ((f32[4,128,4,128]{3,2,0,1:T(4,128)}), f32[4,128,4,128]{3,2,0,1:T(4,128)S(1)}, u32[]{:S(2)}, u32[]{:S(2)}) async-start(f32[4,128,4,128]{3,2,0,1:T(4,128)} %copy.96), calls=%async_computation.4 | async-start | bytes 2097152 | tf_op jit(solution)/shard_map/all_to_all | solution.py:86
  189.2 0.0 reduce-scatter.2.cloned.1.call-start
  189.3 1.0 copy.78
  190.3 0.8 compare_and_fusion
  191.1 0.0 collective-permute-done
  191.2 2.1 fusion.50
  193.2 1.0 copy.77
  194.2 2.9 %fusion = (f32[512,4]{0,1:T(4,128)S(1)}, f32[4,1024,512]{2,1,0:T(8,128)S(1)}) fusion(pred[512,1024]{0,1:T(8,128)(4,1)S(1)} %compare_and_fusion, bf16[512,4,128]{2,0,1:T(8,128)(2,1)} %copy.78, bf16[512,4,128]{2,0,1:T(8,128)(2,1)} %copy.77, bf16[512,512]{1,0:T(8,128)(2,1)} %param.4), kind=kOutput, calls=%fused_computation.2 | convolution fusion | flops 545257472 | bytes 10493952 | tf_op jit(solution)/shard_map/qhd,khd->qhk/dot_general | solution.py:60
  197.2 0.0 copy-start
  197.2 3.2 %copy-done = f32[4,1024,512]{2,1,0:T(8,128)} copy-done((f32[4,1024,512]{2,1,0:T(8,128)}, f32[4,1024,512]{2,1,0:T(8,128)S(1)}, u32[]{:S(2)}) %copy-start) | copy-done | bytes 8388632
  200.4 1.8 fusion.3
  202.2 0.1 copy.100
  202.3 0.1 copy.88
  202.5 15.0 %all-to-all-done.4 = f32[4,128,4,128]{3,2,0,1:T(4,128)S(1)} async-done(((f32[4,128,4,128]{3,2,0,1:T(4,128)}), f32[4,128,4,128]{3,2,0,1:T(4,128)S(1)}, u32[]{:S(2)}, u32[]{:S(2)}) %all-to-all-start.4) | async-done | bytes 1048608 | tf_op jit(solution)/shard_map/all_to_all | solution.py:86
  217.5 0.5 copy.97
  218.0 0.4 reshape.148
  218.4 5.6 %divide_convert_fusion = bf16[512,4,128]{0,2,1:T(8,128)(2,1)S(1)} fusion(f32[512,4,128]{0,2,1:T(8,128)S(1)} %reshape.148, f32[4,1024,512]{2,1,0:T(8,128)} %copy-done, f32[512,4]{0,1:T(4,128)S(1)} %get-tuple-element.12, pred[512,1024]{0,1:T(8,128)(4,1)S(1)} %compare_and_fusion, bf16[512,4,128]{0,2,1:T(8,128)(2,1)S(1)} %bitcast.74, ...), kind=kOutput, calls=%fused_computation.25 | convolution fusion | flops 548667392 | bytes 11567104 | tf_op jit(solution)/shard_map/qhk,khd->qhd/dot_general | solution.py:73
  224.1 0.0 all-gather.2.cloned.1.call-done
  224.1 6.5 %convolution_convert_fusion = bf16[512,4096]{1,0:T(8,128)(2,1)} fusion(bf16[512,512]{0,1:T(8,128)(2,1)S(1)} %bitcast.80, bf16[512,4096]{0,1:T(8,128)(2,1)} %all-gather.2.cloned.1.call-done), kind=kOutput, calls=%fused_computation.7 | convolution fusion | flops 2149580800 | bytes 8912896 | tf_op jit(solution)/shard_map/dot_general | solution.py:100
  230.6 0.0 reduce-scatter.2.cloned.1.call-update
  230.7 51.9 %reduce-scatter.2.cloned.1.call-done = bf16[512,1024]{1,0:T(8,128)(2,1)} async-done(((bf16[512,4096]{1,0:T(8,128)(2,1)}), bf16[512,1024]{1,0:T(8,128)(2,1)}) %reduce-scatter.2.cloned.1.call-update) | async-done | bytes 1048592 | tf_op jit(solution)/shard_map/reduce_scatter | solution.py:105
  (7 shorter events, 0.1 us)
Async XLA Ops:
  6.5 79.2 %copy-start.1 = (bf16[512,512]{1,0:T(8,128)(2,1)S(1)}, bf16[512,512]{1,0:T(8,128)(2,1)}, u32[]{:S(2)}) copy-start(bf16[512,512]{1,0:T(8,128)(2,1)} %param.5) | copy-start | bytes 1572868
  6.5 79.4 %copy-start.2 = (bf16[512,512]{1,0:T(8,128)(2,1)S(1)}, bf16[512,512]{1,0:T(8,128)(2,1)}, u32[]{:S(2)}) copy-start(bf16[512,512]{1,0:T(8,128)(2,1)} %param.6) | copy-start | bytes 1572868
  6.5 217.6 %all-gather.2.cloned.1.call-start = ((), (), s32[]{:S(2)}) async-start(), calls=%async_computation.7 | async-start | bytes 4227072 | tf_op jit(solution)/shard_map/all_gather | solution.py:102
  9.4 39.6 %all-to-all-start = ((bf16[4,128,4,128]{3,2,0,1:T(4,128)(2,1)}), bf16[4,128,4,128]{3,2,0,1:T(4,128)(2,1)S(1)}, u32[]{:S(2)}, u32[]{:S(2)}) async-start(bf16[4,128,4,128]{3,2,0,1:T(4,128)(2,1)} %copy.80), calls=%async_computation | async-start | bytes 1048576 | tf_op jit(solution)/shard_map/all_to_all | solution.py:81
  49.0 27.4 %all-to-all-start.1 = ((bf16[4,128,4,128]{3,2,0,1:T(4,128)(2,1)}), bf16[4,128,4,128]{3,2,0,1:T(4,128)(2,1)}, u32[]{:S(2)}, u32[]{:S(2)}) async-start(bf16[4,128,4,128]{3,2,0,1:T(4,128)(2,1)} %copy.82), calls=%async_computation.1 | async-start | bytes 1048576 | tf_op jit(solution)/shard_map/all_to_all | solution.py:80
  76.4 29.0 %all-to-all-start.3 = ((bf16[4,128,4,128]{3,2,0,1:T(4,128)(2,1)}), bf16[4,128,4,128]{3,2,0,1:T(4,128)(2,1)S(1)}, u32[]{:S(2)}, u32[]{:S(2)}) async-start(bf16[4,128,4,128]{3,2,0,1:T(4,128)(2,1)} %copy.91), calls=%async_computation.3 | async-start | bytes 1048576 | tf_op jit(solution)/shard_map/all_to_all | solution.py:82
  87.3 103.9 %collective-permute-start = (bf16[2,512,512]{1,2,0:T(8,128)(2,1)}, bf16[2,512,512]{1,2,0:T(8,128)(2,1)}, u32[]{:S(2)}, u32[]{:S(2)}) collective-permute-start(bf16[2,512,512]{1,2,0:T(8,128)(2,1)} %pad_maximum_fusion), channel_id=1, source_target_pairs={{0,4},{4,8},{8,12},{12,16},{16,20},{20,24},{24,28},{28,32},{32,36}... | collective-permute-start | bytes 3145736 | tf_op jit(solution)/shard_map/ppermute | solution.py:12
  105.4 53.3 %all-to-all-start.5 = ((f32[4,128,4]{2,0,1:T(4,128)}), f32[4,128,4]{2,0,1:T(4,128)S(1)}, u32[]{:S(2)}, u32[]{:S(2)}) async-start(f32[4,128,4]{2,0,1:T(4,128)} %copy.99), calls=%async_computation.5 | async-start | bytes 524288 | tf_op jit(solution)/shard_map/all_to_all | solution.py:88
  158.7 22.4 %all-to-all-start.2 = ((f32[4,128,4]{2,0,1:T(4,128)}), f32[4,128,4]{2,0,1:T(4,128)S(1)}, u32[]{:S(2)}, u32[]{:S(2)}) async-start(f32[4,128,4]{2,0,1:T(4,128)} %copy.87), calls=%async_computation.2 | async-start | bytes 524288 | tf_op jit(solution)/shard_map/all_to_all | solution.py:87
  181.0 36.5 %all-to-all-start.4 = ((f32[4,128,4,128]{3,2,0,1:T(4,128)}), f32[4,128,4,128]{3,2,0,1:T(4,128)S(1)}, u32[]{:S(2)}, u32[]{:S(2)}) async-start(f32[4,128,4,128]{3,2,0,1:T(4,128)} %copy.96), calls=%async_computation.4 | async-start | bytes 2097152 | tf_op jit(solution)/shard_map/all_to_all | solution.py:86
  189.2 93.3 %reduce-scatter.2.cloned.1.call-start = ((), (), s32[]{:S(2)}) async-start(), calls=%async_computation.8 | async-start | bytes 5242880 | tf_op jit(solution)/shard_map/reduce_scatter | solution.py:105
  197.2 3.2 %copy-start = (f32[4,1024,512]{2,1,0:T(8,128)}, f32[4,1024,512]{2,1,0:T(8,128)S(1)}, u32[]{:S(2)}) copy-start(f32[4,1024,512]{2,1,0:T(8,128)S(1)} %get-tuple-element.13) | copy-start | bytes 25165828
Sparse Core Ops, SparseCore 0:
  11.9 165.4 all-gather.1
  230.8 51.6 reduce-scatter.1
where the time goes:
time: 290 us; the launch traced here: 289 us
  waiting for transfers between devices  168 us (58%)
  starting transfers between devices  66.7 us (23%)
  local copies, waits for them, and re-layouts  19.9 us (7%)
  matrix products  17.2 us (6%)
  between operations  13.6 us (5%)
  other arithmetic  4.07 us (1%)
    reduce_scatter x1, waiting for transfers between devices, body(): lax.psum_scatter(partial_value.astype(jnp.bfloat16), 'mp', scatter_dimens...  51.9 us
    all_to_all x1, waiting for transfers between devices, body(): lax.all_to_all(result[2], 'seq', split_axis=1, concat_axis=1, tiled=True)  43.3 us
    all_to_all x1, starting transfers between devices, body(): lax.all_to_all(key_cols, 'seq', split_axis=1, concat_axis=1, tiled=True)  20.8 us
    all_to_all x1, waiting for transfers between devices, body(): lax.all_to_all(key_cols, 'seq', split_axis=1, concat_axis=1, tiled=True)  16.6 us
    all_to_all x1, waiting for transfers between devices, body(): lax.all_to_all(query_cols, 'seq', split_axis=1, concat_axis=1, tiled=True)  15.5 us
    all_to_all x1, waiting for transfers between devices, body(): lax.all_to_all(result[0], 'seq', split_axis=1, concat_axis=1, tiled=True)  15 us
    all_to_all x1, waiting for transfers between devices, body(): lax.all_to_all(result[1], 'seq', split_axis=1, concat_axis=1, tiled=True)  13.1 us
    all_to_all x1, waiting for transfers between devices, body(): lax.all_to_all(value_cols, 'seq', split_axis=1, concat_axis=1, tiled=True)  11.7 us
  transfers between devices with their start and end apart: 9, of which 7 were waited for; matrix products, arithmetic and copies ran while one was open for 11% of the time, Pallas kernels for 0%

commit v1 on v0

v1 whole, which is shorter than its diff:
```python
import functools

import jax
import jax.numpy as jnp
from jax import lax
from jax.experimental import pallas as pl
from jax.experimental.pallas import tpu as pltpu
from jax.sharding import PartitionSpec as P

DH = 128
HEADS_HERE = 4
ROWS = 512
WIDTH = HEADS_HERE * DH
N_MP = 4
N_SEQ = 128
PLANE = 32
COLS = 8
NEG = -1e30
FACTOR = DH ** (-0.5)
VMEM = 40 * 1024 * 1024

NT = (((1,), (1,)), ((), ()))


def nt_dot(a, b):
    return lax.dot_general(a, b, NT, preferred_element_type=jnp.float32)


def three_parts(x):
    hi = x.astype(jnp.bfloat16).astype(jnp.float32)
    rest = x - hi
    mid = rest.astype(jnp.bfloat16).astype(jnp.float32)
    return hi, mid, rest - mid


def stat_lanes(old, head, largest, total):
    lane = lax.broadcasted_iota(jnp.int32, old.shape, 1)
    out = old
    for place, part in enumerate(three_parts(largest) + three_parts(total)):
        out = jnp.where(lane == head + 4 * place, part, out)
    return out


def spread_stats(stats):
    lane = lax.broadcasted_iota(jnp.int32, (128, WIDTH), 0)
    head = lax.broadcasted_iota(jnp.int32, (128, WIDTH), 1) // DH
    mine = (lane % 4) == head
    pick_max = jnp.where(mine & (lane < 12), 1.0, 0.0).astype(jnp.bfloat16)
    pick_total = jnp.where(mine & (lane >= 12) & (lane < 24), 1.0, 0.0).astype(jnp.bfloat16)
    largest = jnp.dot(stats, pick_max, preferred_element_type=jnp.float32)
    total = jnp.dot(stats, pick_total, preferred_element_type=jnp.float32)
    return largest, total


def row_kernel(parity_ref, q_ref, k_ref, v_ref, kp_ref, vp_ref, out_ref, stat_ref):
    head = pl.program_id(0)
    odd = parity_ref[0] == 1
    block = 128

    @pl.when(head == 0)
    def _():
        stat_ref[...] = jnp.zeros_like(stat_ref)

    for b in range(ROWS // block):
        here = slice(b * block, (b + 1) * block)
        seen = (b + 1) * block
        q = q_ref[here, :]
        own = nt_dot(q, k_ref[:seen, :]) * FACTOR
        place = lax.broadcasted_iota(jnp.int32, (block, seen), 0) + b * block
        other = lax.broadcasted_iota(jnp.int32, (block, seen), 1)
        own = jnp.where(other <= place, own, NEG)
        before = nt_dot(q, kp_ref[...]) * FACTOR
        before = jnp.where(odd, before, NEG)
        largest = jnp.maximum(
            jnp.max(own, axis=1, keepdims=True), jnp.max(before, axis=1, keepdims=True)
        )
        own = jnp.exp(own - largest)
        before = jnp.exp(before - largest)
        total = jnp.sum(own, axis=1, keepdims=True) + jnp.sum(before, axis=1, keepdims=True)
        out_ref[here, :] = jnp.dot(
            own.astype(jnp.bfloat16), v_ref[:seen, :], preferred_element_type=jnp.float32
        ) + jnp.dot(before.astype(jnp.bfloat16), vp_ref[...], preferred_element_type=jnp.float32)
        stat_ref[here, :] = stat_lanes(
            stat_ref[here, :].astype(jnp.float32), head, largest, total
        ).astype(jnp.bfloat16)


def row_attend(parity, q, k, v, kp, vp):
    per_head = pl.BlockSpec((ROWS, DH), lambda h, s: (0, h))
    return pl.pallas_call(
        row_kernel,
        out_shape=(
            jax.ShapeDtypeStruct((ROWS, WIDTH), jnp.float32),
            jax.ShapeDtypeStruct((ROWS, 128), jnp.bfloat16),
        ),
        grid_spec=pltpu.PrefetchScalarGridSpec(
            num_scalar_prefetch=1,
            grid=(HEADS_HERE,),
            in_specs=[per_head] * 5,
            out_specs=(per_head, pl.BlockSpec((ROWS, 128), lambda h, s: (0, 0))),
        ),
        compiler_params=pltpu.CompilerParams(vmem_limit_bytes=VMEM),
        cost_estimate=pl.CostEstimate(
            flops=2 * 2 * 4 * ROWS * 2 * ROWS * DH,
            bytes_accessed=5 * 1024 * 1024,
            transcendentals=4 * ROWS * 2 * ROWS,
        ),
        name="row_attend",
    )(parity, q, k, v, kp, vp)


def col_kernel(q_ref, k_ref, v_ref, out_ref):
    head = pl.program_id(0)
    block = 128
    stat_place = slice(WIDTH, WIDTH + 128)

    @pl.when(head == 0)
    def _():
        out_ref[:, stat_place] = jnp.zeros((ROWS, 128), jnp.bfloat16)

    for b in range(ROWS // block):
        here = slice(b * block, (b + 1) * block)
        seen = (b + 1) * block
        scores = nt_dot(q_ref[here, :], k_ref[:seen, :]) * FACTOR
        token = lax.broadcasted_iota(jnp.int32, (block, seen), 0) + b * block
        other = lax.broadcasted_iota(jnp.int32, (block, seen), 1)
        visible = (other < token) & ((token & (COLS - 1)) == (other & (COLS - 1)))
        largest = jnp.max(jnp.where(visible, scores, NEG), axis=1, keepdims=True)
        weights = jnp.where(visible, jnp.exp(scores - largest), 0.0)
        total = jnp.sum(weights, axis=1, keepdims=True)
        out = jnp.dot(
            weights.astype(jnp.bfloat16), v_ref[:seen, :], preferred_element_type=jnp.float32
        )
        out_ref[here, pl.ds(pl.multiple_of(head * DH, DH), DH)] = out.astype(jnp.bfloat16)
        out_ref[here, stat_place] = stat_lanes(
            out_ref[here, stat_place].astype(jnp.float32), head, largest, total
        ).astype(jnp.bfloat16)


def col_attend(qkv):
    def third(n):
        return pl.BlockSpec((ROWS, DH), lambda h: (0, HEADS_HERE * n + h))

    return pl.pallas_call(
        col_kernel,
        out_shape=jax.ShapeDtypeStruct((ROWS, WIDTH + 128), jnp.bfloat16),
        grid=(HEADS_HERE,),
        in_specs=[third(0), third(1), third(2)],
        out_specs=pl.BlockSpec((ROWS, WIDTH + 128), lambda h: (0, 0)),
        compiler_params=pltpu.CompilerParams(vmem_limit_bytes=VMEM),
        cost_estimate=pl.CostEstimate(
            flops=2 * 2 * 4 * ROWS * ROWS * DH,
            bytes_accessed=2 * 1024 * 1024,
            transcendentals=4 * ROWS * ROWS,
        ),
        name="col_attend",
    )(qkv, qkv, qkv)


def mix_kernel(row_ref, row_stat_ref, col_ref, out_ref):
    row_max, row_total = spread_stats(row_stat_ref[...])
    col_max, col_total = spread_stats(col_ref[:, WIDTH : WIDTH + 128])
    highest = jnp.maximum(row_max, col_max)
    row_factor = jnp.exp(row_max - highest)
    col_factor = jnp.exp(col_max - highest)
    mixed = row_factor * row_ref[...] + col_factor * col_ref[:, :WIDTH].astype(jnp.float32)
    out_ref[...] = (mixed / (row_factor * row_total + col_factor * col_total)).astype(jnp.bfloat16)


def mix(row_out, row_stat, col):
    block = 128

    def rows(width):
        return pl.BlockSpec((block, width), lambda i: (i, 0))

    return pl.pallas_call(
        mix_kernel,
        out_shape=jax.ShapeDtypeStruct((ROWS, WIDTH), jnp.bfloat16),
        grid=(ROWS // block,),
        in_specs=[rows(WIDTH), rows(128), rows(WIDTH + 128)],
        out_specs=rows(WIDTH),
        compiler_params=pltpu.CompilerParams(vmem_limit_bytes=VMEM),
        cost_estimate=pl.CostEstimate(
            flops=4 * 2 * ROWS * 128 * WIDTH,
            bytes_accessed=3 * 1024 * 1024,
            transcendentals=2 * ROWS * WIDTH,
        ),
        name="mix",
    )(row_out, row_stat, col)


def project_kernel(order_ref, a0, a1, a2, a3, w0, w1, w2, w3, out_ref):
    total = None
    for a_ref, w_ref in ((a0, w0), (a1, w1), (a2, w2), (a3, w3)):
        weight = w_ref[...].reshape(out_ref.shape[1], WIDTH)
        term = nt_dot(a_ref[...], weight)
        total = term if total is None else total + term
    out_ref[...] = total.astype(jnp.bfloat16)


def project(order, attended, gathered):
    steps = 4
    here = PLANE // steps
    whole = pl.BlockSpec((ROWS, WIDTH), lambda i, s: (0, 0))

    def weight(j):
        return pl.BlockSpec((here, 1, 32, WIDTH), lambda i, s: (i, s[j], 0, 0))

    return pl.pallas_call(
        project_kernel,
        out_shape=jax.ShapeDtypeStruct((ROWS, PLANE * 32), jnp.bfloat16),
        grid_spec=pltpu.PrefetchScalarGridSpec(
            num_scalar_prefetch=1,
            grid=(steps,),
            in_specs=[whole] * 4 + [weight(j) for j in range(4)],
            out_specs=pl.BlockSpec((ROWS, here * 32), lambda i, s: (0, i)),
        ),
        compiler_params=pltpu.CompilerParams(vmem_limit_bytes=VMEM),
        cost_estimate=pl.CostEstimate(
            flops=2 * ROWS * 4 * WIDTH * PLANE * 32,
            bytes_accessed=7 * 1024 * 1024,
            transcendentals=0,
        ),
        name="project",
    )(order, *attended, gathered, gathered, gathered, gathered)


def same_parity():
    return [[i for i in range(N_SEQ) if i % 2 == p] for p in range(2)]


def swap_columns(value):
    return lax.all_to_all(
        value, "seq", split_axis=0, concat_axis=0, axis_index_groups=same_parity(), tiled=True
    )


def gather_weight(out_weight):
    mine = out_weight.T
    slots = []
    for k in range(N_MP):
        pairs = []
        for seq in range(N_SEQ):
            for mp in range(N_MP):
                z, place = divmod(seq, PLANE)
                target = ((mp + k) % N_MP) * PLANE + place
                pairs.append((seq * N_MP + mp, target * N_MP + z))
        slots.append(lax.ppermute(mine, ("seq", "mp"), pairs))
    stacked = jnp.concatenate(slots, axis=0)
    planes = [[z * PLANE + i for i in range(PLANE)] for z in range(N_MP)]
    gathered = lax.all_gather(stacked, "seq", axis=0, axis_index_groups=planes, tiled=True)
    return gathered.reshape(PLANE, N_MP, 32, WIDTH)


def body(queries, keys, values, out_weight):
    seq, mp = lax.axis_index("seq"), lax.axis_index("mp")
    arrived = swap_columns(jnp.concatenate([queries, keys, values], axis=1))
    gathered = gather_weight(out_weight)

    to_odd = [(i, i + 1) for i in range(0, N_SEQ, 2)]
    keys_before = lax.ppermute(keys, "seq", to_odd)
    values_before = lax.ppermute(values, "seq", to_odd)
    row_out, row_stat = row_attend(
        (seq % 2).astype(jnp.int32).reshape(1), queries, keys, values, keys_before, values_before
    )

    col = swap_columns(col_attend(arrived))
    attended = mix(row_out, row_stat, col)

    near = [(i, i ^ 1) for i in range(N_MP)]
    far = [(i, i ^ 2) for i in range(N_MP)]
    across = lax.ppermute(attended, "mp", far)
    beside = lax.ppermute(attended, "mp", near)
    last = lax.ppermute(across, "mp", near)
    z = seq // PLANE
    order = jnp.stack([(z - (mp ^ j)) % N_MP for j in range(N_MP)]).astype(jnp.int32)
    return project(order, (attended, beside, across, last), gathered)


def solution(mesh):
    placed = (P("seq", "mp"), P("seq", "mp"), P("seq", "mp"), P("mp", "seq"))
    return jax.shard_map(
        body, mesh=mesh, in_specs=placed, out_specs=P("seq", "mp"), check_vma=False
    )
```

time: 290 us -> 190 us (0.66)
  waiting for transfers between devices: 168 us -> 45.7 us
  blocking collectives: 0 us -> 63.3 us
  starting transfers between devices: 66.7 us -> 39.2 us
  Pallas kernels: 0 us -> 19 us
  matrix products: 17.2 us -> 0 us
  local copies, waits for them, and re-layouts: 19.9 us -> 5.88 us
    all_to_all x6 -> x1, waiting for transfers between devices: 115 us -> 0.01 us  [swap_columns(): lax.all_to_all(value, 'seq', split_axis=0, concat_axis=0, axis_index_grou...]
    all_to_all x0 -> x1, blocking collectives: none -> 63.3 us  [swap_columns(): lax.all_to_all(value, 'seq', split_axis=0, concat_axis=0, axis_index_grou...]
    all_to_all x6 -> x1, starting transfers between devices: 63.2 us -> 5.59 us  [swap_columns(): lax.all_to_all(value, 'seq', split_axis=0, concat_axis=0, axis_index_grou...]
    reduce_scatter x1 -> x0, waiting for transfers between devices: 51.9 us -> none  [body(): lax.psum_scatter(partial_value.astype(jnp.bfloat16), 'mp', scatter_dimens...]
    ppermute x1 -> x9, waiting for transfers between devices: 0.01 us -> 45.7 us  [the longest x1 18.9 us: body(): keys_before = lax.ppermute(keys, 'seq', to_odd)]
    ppermute x1 -> x9, starting transfers between devices: 3.44 us -> 33.6 us  [the longest x4 22 us: gather_weight(): slots.append(lax.ppermute(mine, ('seq', 'mp'), pairs))]
    pallas_call x0 -> x4, Pallas kernels: none -> 19 us  [the longest x1 6.74 us: row_attend(): pl.pallas_call(row_kernel, out_shape=(jax.ShapeDtypeStruct((ROWS, WIDTH),...]
    dot_general x5 -> x0, matrix products: 17.2 us -> none  [the longest x1 6.55 us: body(): jnp.dot(attended, lax.all_gather(out_weight, 'seq', axis=1, tiled=True),...]
  transfers between devices with their start and end apart: 9 -> 11, of which waited for: 7 -> 5; matrix products, arithmetic and copies ran while one was open for 11% -> 1% of each run, Pallas kernels for 0% -> 8%
where the time goes in v1:
time: 190 us; the launch traced here: 189 us
  blocking collectives  63.3 us (33%)
  waiting for transfers between devices  45.7 us (24%)
  starting transfers between devices  39.2 us (21%)
  Pallas kernels  19 us (10%)
  between operations  13.6 us (7%)
  local copies, waits for them, and re-layouts  5.88 us (3%)
  other arithmetic  2.23 us (1%)
    all_to_all x1, blocking collectives, swap_columns(): lax.all_to_all(value, 'seq', split_axis=0, concat_axis=0, axis_index_grou...  63.3 us
    ppermute x4, starting transfers between devices, gather_weight(): slots.append(lax.ppermute(mine, ('seq', 'mp'), pairs))  22 us
    ppermute x1, waiting for transfers between devices, body(): keys_before = lax.ppermute(keys, 'seq', to_odd)  18.9 us
    ppermute x1, waiting for transfers between devices, body(): values_before = lax.ppermute(values, 'seq', to_odd)  11.6 us
    ppermute x1, waiting for transfers between devices, body(): across = lax.ppermute(attended, 'mp', far)  10 us
    pallas_call x1, Pallas kernels, row_attend(): pl.pallas_call(row_kernel, out_shape=(jax.ShapeDtypeStruct((ROWS, WIDTH),...  6.74 us
    pallas_call x1, Pallas kernels, col_attend(): pl.pallas_call(col_kernel, out_shape=jax.ShapeDtypeStruct((ROWS, WIDTH +...  6.11 us
    unnamed x16, local copies, waits for them, and re-layouts  5.88 us
  transfers between devices with their start and end apart: 11, of which 5 were waited for; matrix products, arithmetic and copies ran while one was open for 1% of the time, Pallas kernels for 8%

profile of v1, /device:TPU:1, one launch (start us, length us, event | category | flops | bytes accessed | tf_op | source)
XLA Modules:
  0.0 188.9 jit_solution(12380257360582848835)
XLA Ops:
  6.5 0.0 all-gather.2.cloned.1.call-start
  6.5 7.2 %collective-permute-start.5 = (bf16[32,512]{1,0:T(8,128)(2,1)}, bf16[32,512]{1,0:T(8,128)(2,1)S(1)}, u32[]{:S(2)}, u32[]{:S(2)}) collective-permute-start(bf16[32,512]{1,0:T(8,128)(2,1)} %bitcast.20), channel_id=1, source_target_pairs={{0,0},{1,128},{2,256},{3,384},{4,4},{5,132},{6,260},{7,388},{8,8},... | collective-permute-start | bytes 98312 | tf_op jit(solution)/shard_map/ppermute | solution.py:248
  13.7 6.7 %collective-permute-start.6 = (bf16[32,512]{1,0:T(8,128)(2,1)}, bf16[32,512]{1,0:T(8,128)(2,1)S(1)}, u32[]{:S(2)}, u32[]{:S(2)}) collective-permute-start(bf16[32,512]{1,0:T(8,128)(2,1)} %bitcast.21), channel_id=1, source_target_pairs={{0,128},{1,256},{2,384},{3,0},{4,132},{5,260},{6,388},{7,4},{8,136... | collective-permute-start | bytes 98312 | tf_op jit(solution)/shard_map/ppermute | solution.py:248
  20.5 6.1 %collective-permute-start.7 = (bf16[32,512]{1,0:T(8,128)(2,1)}, bf16[32,512]{1,0:T(8,128)(2,1)S(1)}, u32[]{:S(2)}, u32[]{:S(2)}) collective-permute-start(bf16[32,512]{1,0:T(8,128)(2,1)} %bitcast.22), channel_id=1, source_target_pairs={{0,256},{1,384},{2,0},{3,128},{4,260},{5,388},{6,4},{7,132},{8,264... | collective-permute-start | bytes 98312 | tf_op jit(solution)/shard_map/ppermute | solution.py:248
  26.6 1.9 %collective-permute-start.8 = (bf16[32,512]{1,0:T(8,128)(2,1)}, bf16[32,512]{1,0:T(8,128)(2,1)S(1)}, u32[]{:S(2)}, u32[]{:S(2)}) collective-permute-start(bf16[32,512]{1,0:T(8,128)(2,1)} %bitcast.23), channel_id=1, source_target_pairs={{0,384},{1,0},{2,128},{3,256},{4,388},{5,4},{6,132},{7,260},{8,392... | collective-permute-start | bytes 98312 | tf_op jit(solution)/shard_map/ppermute | solution.py:248
  28.5 0.0 collective-permute-done.5
  28.5 0.0 collective-permute-done.6
  28.6 0.0 collective-permute-done.7
  28.6 3.8 %collective-permute-done.8 = bf16[32,512]{1,0:T(8,128)(2,1)S(1)} collective-permute-done((bf16[32,512]{1,0:T(8,128)(2,1)}, bf16[32,512]{1,0:T(8,128)(2,1)S(1)}, u32[]{:S(2)}, u32[]{:S(2)}) %collective-permute-start.8) | collective-permute-done | bytes 32800 | tf_op jit(solution)/shard_map/ppermute | solution.py:248
  32.4 0.7 pad_maximum_fusion
  33.1 0.0 all-gather.2.cloned.1.call-update
  33.1 1.5 maximum_bitcast_fusion
  34.5 63.3 %all_to_all.22 = bf16[64,8,1536]{2,1,0:T(8,128)(2,1)S(1)} all-to-all(bf16[64,8,1536]{2,1,0:T(8,128)(2,1)S(1)} %maximum_bitcast_fusion), channel_id=1, replica_groups={{0,8,16,24,32,40,48,56,64,72,80,88,96,104,112,120,128,136,144,152,160,1..., dimensions={0} | all-to-all | bytes 3145728 | tf_op jit(solution)/shard_map/all_to_all | solution.py:233
  97.8 0.0 copy-start.2
  97.8 0.0 copy-start.3
  97.8 0.0 copy-start.1
  97.8 6.1 %col_attend.1 = bf16[512,640]{1,0:T(8,128)(2,1)} custom-call(bf16[512,1536]{1,0:T(8,128)(2,1)S(1)} %bitcast.16, bf16[512,1536]{1,0:T(8,128)(2,1)S(1)} %bitcast.17, bf16[512,1536]{1,0:T(8,128)(2,1)S(1)} %bitcast.18), custom_call_target="tpu_custom_call" | custom-call | flops 536870912 | bytes 2097152 | tf_op jit(solution)/shard_map/col_attend/pallas_call | solution.py:144
  103.9 5.6 %all-to-all-start.1 = ((bf16[64,8,640]{2,1,0:T(8,128)(2,1)}), bf16[64,8,640]{2,1,0:T(8,128)(2,1)S(1)}, u32[]{:S(2)}, u32[]{:S(2)}) async-start(bf16[64,8,640]{2,1,0:T(8,128)(2,1)} %bitcast.7), calls=%async_computation.1 | async-start | bytes 1310720 | tf_op jit(solution)/shard_map/all_to_all | solution.py:233
  109.5 0.0 copy-done.2
  109.5 2.2 %collective-permute-start = (bf16[512,512]{1,0:T(8,128)(2,1)S(1)}, bf16[512,512]{1,0:T(8,128)(2,1)S(1)}, u32[]{:S(2)}, u32[]{:S(2)}) collective-permute-start(bf16[512,512]{1,0:T(8,128)(2,1)S(1)} %copy-done.2), channel_id=1, source_target_pairs={{0,4},{8,12},{16,20},{24,28},{32,36},{40,44},{48,52},{56,60},{64,6... | collective-permute-start | bytes 1572872 | tf_op jit(solution)/shard_map/ppermute | solution.py:261
  111.8 0.0 copy-done.3
  111.8 1.3 collective-permute-start.1
  113.1 18.9 %collective-permute-done.kp_ref = bf16[512,512]{1,0:T(8,128)(2,1)S(1)} collective-permute-done((bf16[512,512]{1,0:T(8,128)(2,1)S(1)}, bf16[512,512]{1,0:T(8,128)(2,1)S(1)}, u32[]{:S(2)}, u32[]{:S(2)}) %collective-permute-start) | collective-permute-done | bytes 524320 | tf_op jit(solution)/shard_map/ppermute | solution.py:261
  132.0 0.0 copy-start.4
  132.0 0.8 copy-done.4
  132.8 11.6 %collective-permute-done.1.vp_ref = bf16[512,512]{1,0:T(8,128)(2,1)S(1)} collective-permute-done((bf16[512,512]{1,0:T(8,128)(2,1)S(1)}, bf16[512,512]{1,0:T(8,128)(2,1)S(1)}, u32[]{:S(2)}, u32[]{:S(2)}) %collective-permute-start.1) | collective-permute-done | bytes 524320 | tf_op jit(solution)/shard_map/ppermute | solution.py:262
  144.4 0.0 copy-start.6
  144.4 0.8 copy-done.6
  145.2 0.0 copy-done.1
  145.2 0.0 copy-start.5
  145.2 1.0 copy-done.5
  146.3 0.0 copy-start.7
  146.3 1.0 copy-done.7
  147.3 6.7 %row_attend.1 = (f32[512,512]{1,0:T(8,128)S(1)}, bf16[512,128]{1,0:T(8,128)(2,1)S(1)}) custom-call(s32[1]{0:T(128)} %bitcast.4.parity_ref, bf16[512,512]{1,0:T(8,128)(2,1)S(1)} %copy-done.1, bf16[512,512]{1,0:T(8,128)(2,1)S(1)} %copy-done.2, bf16[512,512]{1,0:T(8,128)(2,1)S(1)} %copy-done.3, bf16[512,512]{1,0:T(8,128)(2,1)S(1)} %copy-done.5, ...), custom_call_target="tpu_custom_call" | custom-call | flops 1073741824 | bytes 5242880 | tf_op jit(solution)/shard_map/row_attend/pallas_call | solution.py:90
  154.0 0.0 all-to-all-done.1
  154.1 1.5 mix.1.a0
  155.5 1.9 %collective-permute-start.3 = (bf16[512,512]{1,0:T(8,128)(2,1)S(1)}, bf16[512,512]{1,0:T(8,128)(2,1)S(1)}, u32[]{:S(2)}, u32[]{:S(2)}) collective-permute-start(bf16[512,512]{1,0:T(8,128)(2,1)S(1)} %mix.1.a0), channel_id=1, source_target_pairs={{0,2},{1,3},{2,0},{3,1},{4,6},{5,7},{6,4},{7,5},{8,10},{9,11},{10,... | collective-permute-start | bytes 1572872 | tf_op jit(solution)/shard_map/ppermute | solution.py:272
  157.5 2.6 %collective-permute-start.2 = (bf16[512,512]{1,0:T(8,128)(2,1)S(1)}, bf16[512,512]{1,0:T(8,128)(2,1)S(1)}, u32[]{:S(2)}, u32[]{:S(2)}) collective-permute-start(bf16[512,512]{1,0:T(8,128)(2,1)S(1)} %mix.1.a0), channel_id=1, source_target_pairs={{0,1},{1,0},{2,3},{3,2},{4,5},{5,4},{6,7},{7,6},{8,9},{9,8},{10,11... | collective-permute-start | bytes 1572872 | tf_op jit(solution)/shard_map/ppermute | solution.py:273
  160.1 10.0 %collective-permute-done.3.a2 = bf16[512,512]{1,0:T(8,128)(2,1)S(1)} collective-permute-done((bf16[512,512]{1,0:T(8,128)(2,1)S(1)}, bf16[512,512]{1,0:T(8,128)(2,1)S(1)}, u32[]{:S(2)}, u32[]{:S(2)}) %collective-permute-start.3) | collective-permute-done | bytes 524320 | tf_op jit(solution)/shard_map/ppermute | solution.py:272
  170.1 3.5 %collective-permute-start.4 = (bf16[512,512]{1,0:T(8,128)(2,1)S(1)}, bf16[512,512]{1,0:T(8,128)(2,1)S(1)}, u32[]{:S(2)}, u32[]{:S(2)}) collective-permute-start(bf16[512,512]{1,0:T(8,128)(2,1)S(1)} %collective-permute-done.3.a2), channel_id=1, source_target_pairs={{0,1},{1,0},{2,3},{3,2},{4,5},{5,4},{6,7},{7,6},{8,9},{9,8},{10,11... | collective-permute-start | bytes 1572872 | tf_op jit(solution)/shard_map/ppermute | solution.py:274
  173.8 0.1 pad_add_fusion.order_ref
  173.8 0.0 collective-permute-done.2.a1
  173.8 1.4 collective-permute-done.4.a3
  175.2 0.0 all-gather.2.cloned.1.call-done
  175.2 0.0 copy-start
  175.2 2.2 %copy-done = bf16[4096,512]{1,0:T(8,128)(2,1)S(1)} copy-done((bf16[4096,512]{1,0:T(8,128)(2,1)S(1)}, bf16[4096,512]{1,0:T(8,128)(2,1)}, u32[]{:S(2)}) %copy-start) | copy-done | bytes 4194328
  177.4 4.7 %project.1 = bf16[512,1024]{1,0:T(8,128)(2,1)} custom-call(s32[4]{0:T(128)S(1)} %pad_add_fusion.order_ref, bf16[512,512]{1,0:T(8,128)(2,1)S(1)} %mix.1.a0, bf16[512,512]{1,0:T(8,128)(2,1)S(1)} %collective-permute-done.2.a1, bf16[512,512]{1,0:T(8,128)(2,1)S(1)} %collective-permute-done.3.a2, bf16[512,512]{1,0:T(8,128)(2,1)S(1)} %collective-permute-done.4.a3, ...), custom_call_target="tpu_custom_call" | custom-call | flops 2147483648 | bytes 7340032 | tf_op jit(solution)/shard_map/project/pallas_call | solution.py:209
Async XLA Ops:
  6.5 168.7 %all-gather.2.cloned.1.call-start = ((), (), s32[]{:S(2)}) async-start(), calls=%async_computation.2 | async-start | bytes 4325376 | tf_op jit(solution)/shard_map/all_gather | solution.py:251
  6.5 22.0 %collective-permute-start.5 = (bf16[32,512]{1,0:T(8,128)(2,1)}, bf16[32,512]{1,0:T(8,128)(2,1)S(1)}, u32[]{:S(2)}, u32[]{:S(2)}) collective-permute-start(bf16[32,512]{1,0:T(8,128)(2,1)} %bitcast.20), channel_id=1, source_target_pairs={{0,0},{1,128},{2,256},{3,384},{4,4},{5,132},{6,260},{7,388},{8,8},... | collective-permute-start | bytes 98312 | tf_op jit(solution)/shard_map/ppermute | solution.py:248
  13.7 14.8 %collective-permute-start.6 = (bf16[32,512]{1,0:T(8,128)(2,1)}, bf16[32,512]{1,0:T(8,128)(2,1)S(1)}, u32[]{:S(2)}, u32[]{:S(2)}) collective-permute-start(bf16[32,512]{1,0:T(8,128)(2,1)} %bitcast.21), channel_id=1, source_target_pairs={{0,128},{1,256},{2,384},{3,0},{4,132},{5,260},{6,388},{7,4},{8,136... | collective-permute-start | bytes 98312 | tf_op jit(solution)/shard_map/ppermute | solution.py:248
  20.5 8.1 %collective-permute-start.7 = (bf16[32,512]{1,0:T(8,128)(2,1)}, bf16[32,512]{1,0:T(8,128)(2,1)S(1)}, u32[]{:S(2)}, u32[]{:S(2)}) collective-permute-start(bf16[32,512]{1,0:T(8,128)(2,1)} %bitcast.22), channel_id=1, source_target_pairs={{0,256},{1,384},{2,0},{3,128},{4,260},{5,388},{6,4},{7,132},{8,264... | collective-permute-start | bytes 98312 | tf_op jit(solution)/shard_map/ppermute | solution.py:248
  26.6 5.8 %collective-permute-start.8 = (bf16[32,512]{1,0:T(8,128)(2,1)}, bf16[32,512]{1,0:T(8,128)(2,1)S(1)}, u32[]{:S(2)}, u32[]{:S(2)}) collective-permute-start(bf16[32,512]{1,0:T(8,128)(2,1)} %bitcast.23), channel_id=1, source_target_pairs={{0,384},{1,0},{2,128},{3,256},{4,388},{5,4},{6,132},{7,260},{8,392... | collective-permute-start | bytes 98312 | tf_op jit(solution)/shard_map/ppermute | solution.py:248
  97.8 11.7 %copy-start.2 = (bf16[512,512]{1,0:T(8,128)(2,1)S(1)}, bf16[512,512]{1,0:T(8,128)(2,1)}, u32[]{:S(2)}) copy-start(bf16[512,512]{1,0:T(8,128)(2,1)} %k_ref.1) | copy-start | bytes 1572868
  97.8 14.0 %copy-start.3 = (bf16[512,512]{1,0:T(8,128)(2,1)S(1)}, bf16[512,512]{1,0:T(8,128)(2,1)}, u32[]{:S(2)}) copy-start(bf16[512,512]{1,0:T(8,128)(2,1)} %v_ref.1) | copy-start | bytes 1572868
  97.8 47.4 %copy-start.1 = (bf16[512,512]{1,0:T(8,128)(2,1)S(1)}, bf16[512,512]{1,0:T(8,128)(2,1)}, u32[]{:S(2)}) copy-start(bf16[512,512]{1,0:T(8,128)(2,1)} %q_ref.1) | copy-start | bytes 1572868
  103.9 50.1 %all-to-all-start.1 = ((bf16[64,8,640]{2,1,0:T(8,128)(2,1)}), bf16[64,8,640]{2,1,0:T(8,128)(2,1)S(1)}, u32[]{:S(2)}, u32[]{:S(2)}) async-start(bf16[64,8,640]{2,1,0:T(8,128)(2,1)} %bitcast.7), calls=%async_computation.1 | async-start | bytes 1310720 | tf_op jit(solution)/shard_map/all_to_all | solution.py:233
  109.5 22.5 %collective-permute-start = (bf16[512,512]{1,0:T(8,128)(2,1)S(1)}, bf16[512,512]{1,0:T(8,128)(2,1)S(1)}, u32[]{:S(2)}, u32[]{:S(2)}) collective-permute-start(bf16[512,512]{1,0:T(8,128)(2,1)S(1)} %copy-done.2), channel_id=1, source_target_pairs={{0,4},{8,12},{16,20},{24,28},{32,36},{40,44},{48,52},{56,60},{64,6... | collective-permute-start | bytes 1572872 | tf_op jit(solution)/shard_map/ppermute | solution.py:261
  111.8 32.6 %collective-permute-start.1 = (bf16[512,512]{1,0:T(8,128)(2,1)S(1)}, bf16[512,512]{1,0:T(8,128)(2,1)S(1)}, u32[]{:S(2)}, u32[]{:S(2)}) collective-permute-start(bf16[512,512]{1,0:T(8,128)(2,1)S(1)} %copy-done.3), channel_id=1, source_target_pairs={{0,4},{8,12},{16,20},{24,28},{32,36},{40,44},{48,52},{56,60},{64,6... | collective-permute-start | bytes 1572872 | tf_op jit(solution)/shard_map/ppermute | solution.py:262
  132.0 0.8 copy-start.4
  144.4 0.8 copy-start.6
  145.2 1.0 copy-start.5
  146.3 1.0 copy-start.7
  155.5 14.6 %collective-permute-start.3 = (bf16[512,512]{1,0:T(8,128)(2,1)S(1)}, bf16[512,512]{1,0:T(8,128)(2,1)S(1)}, u32[]{:S(2)}, u32[]{:S(2)}) collective-permute-start(bf16[512,512]{1,0:T(8,128)(2,1)S(1)} %mix.1.a0), channel_id=1, source_target_pairs={{0,2},{1,3},{2,0},{3,1},{4,6},{5,7},{6,4},{7,5},{8,10},{9,11},{10,... | collective-permute-start | bytes 1572872 | tf_op jit(solution)/shard_map/ppermute | solution.py:272
  157.5 16.4 %collective-permute-start.2 = (bf16[512,512]{1,0:T(8,128)(2,1)S(1)}, bf16[512,512]{1,0:T(8,128)(2,1)S(1)}, u32[]{:S(2)}, u32[]{:S(2)}) collective-permute-start(bf16[512,512]{1,0:T(8,128)(2,1)S(1)} %mix.1.a0), channel_id=1, source_target_pairs={{0,1},{1,0},{2,3},{3,2},{4,5},{5,4},{6,7},{7,6},{8,9},{9,8},{10,11... | collective-permute-start | bytes 1572872 | tf_op jit(solution)/shard_map/ppermute | solution.py:273
  170.1 5.0 %collective-permute-start.4 = (bf16[512,512]{1,0:T(8,128)(2,1)S(1)}, bf16[512,512]{1,0:T(8,128)(2,1)S(1)}, u32[]{:S(2)}, u32[]{:S(2)}) collective-permute-start(bf16[512,512]{1,0:T(8,128)(2,1)S(1)} %collective-permute-done.3.a2), channel_id=1, source_target_pairs={{0,1},{1,0},{2,3},{3,2},{4,5},{5,4},{6,7},{7,6},{8,9},{9,8},{10,11... | collective-permute-start | bytes 1572872 | tf_op jit(solution)/shard_map/ppermute | solution.py:274
  175.2 2.2 %copy-start = (bf16[4096,512]{1,0:T(8,128)(2,1)S(1)}, bf16[4096,512]{1,0:T(8,128)(2,1)}, u32[]{:S(2)}) copy-start(bf16[4096,512]{1,0:T(8,128)(2,1)} %all-gather.2.cloned.1.call-done) | copy-start | bytes 12582916
Sparse Core Ops, SparseCore 0:
  33.2 103.6 all-gather.1

commit v2 on v1

v2 whole, which is shorter than its diff:
```python
import functools

import jax
import jax.numpy as jnp
from jax import lax
from jax.experimental import pallas as pl
from jax.experimental.pallas import tpu as pltpu
from jax.sharding import PartitionSpec as P

DH = 128
HEADS_HERE = 4
ROWS = 512
WIDTH = HEADS_HERE * DH
N_MP = 4
N_SEQ = 128
PLANE = 32
COLS = 8
NEG = -1e30
NONE = -1e29
FACTOR = DH ** (-0.5) * 1.4426950408889634
VMEM = 40 * 1024 * 1024
SMALL = pl.CostEstimate(flops=1024, bytes_accessed=1024, transcendentals=0)

NT = (((1,), (1,)), ((), ()))


def nt_dot(a, b):
    return lax.dot_general(a, b, NT, preferred_element_type=jnp.float32)


def stat_lanes(old, head, largest, total):
    lane = lax.broadcasted_iota(jnp.int32, old.shape, 1)
    return jnp.where(lane == head, largest, jnp.where(lane == 4 + head, total, old))


def three_parts(stats):
    high = stats.astype(jnp.bfloat16).astype(jnp.float32)
    rest = stats - high
    middle = rest.astype(jnp.bfloat16).astype(jnp.float32)
    low = rest - middle
    parts = high + pltpu.roll(middle, 8, 1) + pltpu.roll(low, 16, 1)
    return parts.astype(jnp.bfloat16)


def spread_stats(stats):
    lane = lax.broadcasted_iota(jnp.int32, (128, WIDTH), 0)
    head = lax.broadcasted_iota(jnp.int32, (128, WIDTH), 1) // DH
    kept = lane < 24
    pick_max = jnp.where(kept & ((lane & 7) == head), 1.0, 0.0).astype(jnp.bfloat16)
    pick_total = jnp.where(kept & ((lane & 7) == head + 4), 1.0, 0.0).astype(jnp.bfloat16)
    largest = jnp.dot(stats, pick_max, preferred_element_type=jnp.float32)
    total = jnp.dot(stats, pick_total, preferred_element_type=jnp.float32)
    return largest, total


def row_kernel(parity_ref, q_ref, k_ref, v_ref, kp_ref, vp_ref, out_ref, packed_ref, stat_ref):
    head = pl.program_id(0)
    odd = parity_ref[0] == 1
    block = 128

    @pl.when(head == 0)
    def _():
        stat_ref[...] = jnp.zeros_like(stat_ref)

    for b in range(ROWS // block):
        here = slice(b * block, (b + 1) * block)
        seen = (b + 1) * block
        q = q_ref[here, :]
        own = nt_dot(q, k_ref[:seen, :]) * FACTOR
        place = lax.broadcasted_iota(jnp.int32, (block, seen), 0) + b * block
        other = lax.broadcasted_iota(jnp.int32, (block, seen), 1)
        own = jnp.where(other <= place, own, NEG)
        before = nt_dot(q, kp_ref[...]) * FACTOR
        before = jnp.where(odd, before, NEG)
        largest = jnp.maximum(
            jnp.max(own, axis=1, keepdims=True), jnp.max(before, axis=1, keepdims=True)
        )
        own = jnp.exp2(own - largest)
        before = jnp.exp2(before - largest)
        total = jnp.sum(own, axis=1, keepdims=True) + jnp.sum(before, axis=1, keepdims=True)
        out_ref[here, :] = jnp.dot(
            own.astype(jnp.bfloat16), v_ref[:seen, :], preferred_element_type=jnp.float32
        ) + jnp.dot(before.astype(jnp.bfloat16), vp_ref[...], preferred_element_type=jnp.float32)
        stat_ref[here, :] = stat_lanes(stat_ref[here, :], head, largest, total)

    @pl.when(head == HEADS_HERE - 1)
    def _():
        packed_ref[...] = three_parts(stat_ref[...])


def row_attend(parity, q, k, v, kp, vp):
    per_head = pl.BlockSpec((ROWS, DH), lambda h, s: (0, h))
    return pl.pallas_call(
        row_kernel,
        out_shape=(
            jax.ShapeDtypeStruct((ROWS, WIDTH), jnp.float32),
            jax.ShapeDtypeStruct((ROWS, 128), jnp.bfloat16),
        ),
        grid_spec=pltpu.PrefetchScalarGridSpec(
            num_scalar_prefetch=1,
            grid=(HEADS_HERE,),
            in_specs=[per_head] * 5,
            out_specs=(per_head, pl.BlockSpec((ROWS, 128), lambda h, s: (0, 0))),
            scratch_shapes=[pltpu.VMEM((ROWS, 128), jnp.float32)],
        ),
        compiler_params=pltpu.CompilerParams(vmem_limit_bytes=VMEM),
        cost_estimate=SMALL,
        name="row_attend",
    )(parity, q, k, v, kp, vp)


def col_kernel(qkv_ref, out_ref):
    block = 128
    token = lax.broadcasted_iota(jnp.int32, (block, block), 0)
    other = lax.broadcasted_iota(jnp.int32, (block, block), 1)
    same = (token & (COLS - 1)) == (other & (COLS - 1))
    earlier = same & (other < token)
    for b in range(ROWS // block):
        here = slice(b * block, (b + 1) * block)
        stats = jnp.zeros((block, 128), jnp.float32)
        for head in range(HEADS_HERE):
            q_lanes, k_lanes, v_lanes = (
                slice(n * WIDTH + head * DH, n * WIDTH + (head + 1) * DH) for n in range(3)
            )
            q = qkv_ref[here, q_lanes]
            scores = []
            for c in range(b + 1):
                score = nt_dot(q, qkv_ref[c * block : (c + 1) * block, k_lanes]) * FACTOR
                scores.append(jnp.where(same if c < b else earlier, score, NEG))
            largest = functools.reduce(jnp.maximum, scores)
            largest = jnp.maximum(jnp.max(largest, axis=1, keepdims=True), NONE)
            weights = [jnp.exp2(score - largest) for score in scores]
            total = jnp.sum(functools.reduce(jnp.add, weights), axis=1, keepdims=True)
            out = jnp.dot(
                jnp.concatenate([w.astype(jnp.bfloat16) for w in weights], axis=1),
                qkv_ref[: (b + 1) * block, v_lanes],
                preferred_element_type=jnp.float32,
            )
            out_ref[here, head * DH : (head + 1) * DH] = out.astype(jnp.bfloat16)
            stats = stat_lanes(stats, head, largest, total)
        out_ref[here, WIDTH:] = three_parts(stats)


def col_attend(qkv):
    return pl.pallas_call(
        col_kernel,
        out_shape=jax.ShapeDtypeStruct((ROWS, WIDTH + 128), jnp.bfloat16),
        in_specs=[pl.BlockSpec(memory_space=pltpu.VMEM)],
        out_specs=pl.BlockSpec(memory_space=pltpu.VMEM),
        compiler_params=pltpu.CompilerParams(vmem_limit_bytes=VMEM),
        cost_estimate=SMALL,
        name="col_attend",
    )(qkv)


def mix_kernel(row_ref, row_stat_ref, col_ref, out_ref):
    row_max, row_total = spread_stats(row_stat_ref[...])
    col_max, col_total = spread_stats(col_ref[:, WIDTH : WIDTH + 128])
    highest = jnp.maximum(row_max, col_max)
    row_factor = jnp.exp2(row_max - highest)
    col_factor = jnp.exp2(col_max - highest)
    mixed = row_factor * row_ref[...] + col_factor * col_ref[:, :WIDTH].astype(jnp.float32)
    out_ref[...] = (mixed / (row_factor * row_total + col_factor * col_total)).astype(jnp.bfloat16)


def mix(row_out, row_stat, col):
    block = 128

    def rows(width):
        return pl.BlockSpec((block, width), lambda i: (i, 0))

    return pl.pallas_call(
        mix_kernel,
        out_shape=jax.ShapeDtypeStruct((ROWS, WIDTH), jnp.bfloat16),
        grid=(ROWS // block,),
        in_specs=[rows(WIDTH), rows(128), rows(WIDTH + 128)],
        out_specs=rows(WIDTH),
        compiler_params=pltpu.CompilerParams(vmem_limit_bytes=VMEM),
        cost_estimate=SMALL,
        name="mix",
    )(row_out, row_stat, col)


def arrange_kernel(place_ref, *refs):
    *pieces, out_ref = refs
    y, x, mp = place_ref[0], place_ref[1], place_ref[2]
    spots = []
    for i, piece in enumerate(pieces):
        there = (x + i // 2) & 3
        head = 2 * ((y + i % 2) & 1) + there // 2
        spots.append((piece, (there & 1) * 32, pl.multiple_of(head * DH, DH)))

    def step(i, carry):
        for piece, row, lane in spots:
            start = pl.multiple_of(i * 64 + row, 32)
            for group in range(N_MP):
                out_ref[group ^ mp, pl.ds(start, 32), pl.ds(lane, DH)] = piece[group, i]
        return carry

    lax.fori_loop(0, 16, step, 0)


def arrange(place, *pieces):
    vmem = pl.BlockSpec(memory_space=pltpu.VMEM)
    return pl.pallas_call(
        arrange_kernel,
        out_shape=jax.ShapeDtypeStruct((N_MP, PLANE * 32, WIDTH), jnp.bfloat16),
        in_specs=[pl.BlockSpec(memory_space=pltpu.SMEM)] + [vmem] * len(pieces),
        out_specs=vmem,
        compiler_params=pltpu.CompilerParams(vmem_limit_bytes=VMEM),
        cost_estimate=SMALL,
        name="arrange",
    )(place, *pieces)


def project_kernel(first, blocks, *refs):
    *refs, weight_ref, out_ref = refs
    step = 256
    for i in range(out_ref.shape[1] // step):
        here = slice(i * step, (i + 1) * step)
        total = refs[blocks][:, here] if len(refs) > blocks else None
        for j in range(blocks):
            term = nt_dot(refs[j][...], weight_ref[first + j, here, :])
            total = term if total is None else total + term
        out_ref[:, here] = total.astype(out_ref.dtype)


def project(before, blocks, weight, first, kind):
    operands = [*blocks] + ([] if before is None else [before]) + [weight]
    vmem = pl.BlockSpec(memory_space=pltpu.VMEM)
    return pl.pallas_call(
        functools.partial(project_kernel, first, len(blocks)),
        out_shape=jax.ShapeDtypeStruct((ROWS, PLANE * 32), kind),
        in_specs=[vmem] * len(operands),
        out_specs=vmem,
        compiler_params=pltpu.CompilerParams(vmem_limit_bytes=VMEM),
        cost_estimate=SMALL,
        name="project",
    )(*operands)


def same_parity():
    return [[i for i in range(N_SEQ) if i % 2 == p] for p in range(2)]


def swap_columns(value):
    return lax.all_to_all(
        value, "seq", split_axis=0, concat_axis=0, axis_index_groups=same_parity(), tiled=True
    )


def along(step, stride, size):
    pairs = []
    for i in range(N_SEQ):
        place = i // stride % size
        pairs.append((i, i + ((place + step) % size - place) * stride))
    return pairs


def turn(mine):
    pairs = []
    for seq in range(N_SEQ):
        z, place = divmod(seq, PLANE)
        for mp in range(N_MP):
            pairs.append((seq * N_MP + mp, (mp * PLANE + place) * N_MP + z))
    return lax.ppermute(mine, ("seq", "mp"), pairs)


def weight_messages(turned):
    heads = turned.reshape(4, 8, HEADS_HERE, DH).transpose(2, 1, 0, 3).reshape(1, 4 * 8, WIDTH)
    return jnp.broadcast_to(heads, (16, 4 * 8, WIDTH)).reshape(ROWS, WIDTH)


def weight_piece(received):
    tiles = received.reshape(64, 8, 4, DH).transpose(0, 2, 1, 3)
    return tiles.reshape(N_MP, 16, 32, DH)


def body(queries, keys, values, out_weight):
    seq, mp = lax.axis_index("seq"), lax.axis_index("mp")
    barrier = lax.optimization_barrier
    x_up, x_down = along(1, 1, 4), along(-1, 1, 4)
    y_pair = [(i, i ^ 4) for i in range(N_SEQ)]

    blank = jnp.zeros((ROWS, WIDTH), jnp.bfloat16)
    turned, together = barrier(
        (turn(out_weight.T), jnp.concatenate([queries, keys, values, blank], axis=1))
    )
    together = lax.dynamic_update_slice(together, weight_messages(turned), (0, 3 * WIDTH))
    arrived = swap_columns(together)

    to_odd = [(i, i + 1) for i in range(0, N_SEQ, 2)]
    keys_before = lax.ppermute(keys, "seq", to_odd)
    values_before = lax.ppermute(values, "seq", to_odd)

    own_0 = weight_piece(arrived[:, 3 * WIDTH :])
    own_1 = lax.ppermute(own_0, "seq", y_pair)
    less_0 = lax.ppermute(own_0, "seq", x_up)
    more_0 = lax.ppermute(own_0, "seq", x_down)

    row_out, row_stat = row_attend(
        (seq % 2).astype(jnp.int32).reshape(1), queries, keys, values, keys_before, values_before
    )
    arrived, row_out, row_stat = barrier((arrived, row_out, row_stat))

    col_own = col_attend(arrived)
    col_own, own_1, less_0, more_0 = barrier((col_own, own_1, less_0, more_0))
    less_1 = lax.ppermute(own_1, "seq", x_up)
    more_1 = lax.ppermute(own_1, "seq", x_down)
    far_0 = lax.ppermute(less_0, "seq", x_up)
    col = swap_columns(col_own)
    attended = mix(row_out, row_stat, col)

    near = [(i, i ^ 1) for i in range(N_MP)]
    far = [(i, i ^ 2) for i in range(N_MP)]
    across = lax.ppermute(attended, "mp", far)
    after, less_1, more_1 = barrier((attended, less_1, more_1))
    far_1 = lax.ppermute(more_1, "seq", x_down)
    beside = lax.ppermute(after, "mp", near)
    last = lax.ppermute(across, "mp", near)
    place = jnp.stack([seq // 4 % 8, seq % 4, mp]).astype(jnp.int32)
    weight = arrange(place, own_0, own_1, more_0, more_1, far_0, far_1, less_0, less_1)
    total = project(None, (attended, beside), weight, 0, jnp.float32)
    total = project(total, (across,), weight, 2, jnp.float32)
    return project(total, (last,), weight, 3, jnp.bfloat16)


def solution(mesh):
    placed = (P("seq", "mp"), P("seq", "mp"), P("seq", "mp"), P("mp", "seq"))
    return jax.shard_map(
        body, mesh=mesh, in_specs=placed, out_specs=P("seq", "mp"), check_vma=False
    )
```

time: 190 us -> 169 us (0.89); the launches traced: 189 us -> 165 us
  blocking collectives: 63.3 us -> 0 us
  starting transfers between devices: 39.2 us -> 74.8 us
  waiting for transfers between devices: 45.7 us -> 61.6 us
  between operations: 13.6 us -> 0.34 us
  Pallas kernels: 19 us -> 23.1 us
  local copies, waits for them, and re-layouts: 5.88 us -> 3.68 us
    all_to_all x1 -> x0, blocking collectives: 63.3 us -> none  [swap_columns(): lax.all_to_all(value, 'seq', split_axis=0, concat_axis=0, axis_index_grou...]
    all_to_all x1 -> x2, waiting for transfers between devices: 0.01 us -> 61.6 us  [swap_columns(): lax.all_to_all(value, 'seq', split_axis=0, concat_axis=0, axis_index_grou...]
    all_to_all x1 -> x2, starting transfers between devices: 5.59 us -> 28.6 us  [swap_columns(): lax.all_to_all(value, 'seq', split_axis=0, concat_axis=0, axis_index_grou...]
    ppermute x1, waiting for transfers between devices: 18.9 us -> 0.01 us  [body(): keys_before = lax.ppermute(keys, 'seq', to_odd)]
    ppermute x1, waiting for transfers between devices: 11.6 us -> 0.01 us  [body(): values_before = lax.ppermute(values, 'seq', to_odd)]
    ppermute x5 -> x9, starting transfers between devices: 24.6 us -> 35.8 us  [the longest x1 7.25 us: body(): beside = lax.ppermute(after, 'mp', near)]
    ppermute x1, waiting for transfers between devices: 10 us -> 0.01 us  [body(): across = lax.ppermute(attended, 'mp', far)]
    pallas_call x1 -> x4, Pallas kernels: 4.68 us -> 8.72 us  [the longest x3 5.81 us: project(): pl.pallas_call(functools.partial(project_kernel, first, len(blocks)), out...]
  transfers between devices with their start and end apart: 11 -> 15, of which waited for: 5 -> 2; matrix products, arithmetic and copies ran while one was open for 1% -> 1% of each run, Pallas kernels for 8% -> 12%
where the time goes in v2:
time: 169 us; the launch traced here: 165 us
  starting transfers between devices  74.8 us (44%)
  waiting for transfers between devices  61.6 us (36%)
  Pallas kernels  23.1 us (14%)
  local copies, waits for them, and re-layouts  3.68 us (2%)
  other arithmetic  1.85 us (1%)
    all_to_all x2, waiting for transfers between devices, swap_columns(): lax.all_to_all(value, 'seq', split_axis=0, concat_axis=0, axis_index_grou...  61.6 us
    all_to_all x2, starting transfers between devices, swap_columns(): lax.all_to_all(value, 'seq', split_axis=0, concat_axis=0, axis_index_grou...  28.6 us
    pallas_call x1, Pallas kernels, row_attend(): pl.pallas_call(row_kernel, out_shape=(jax.ShapeDtypeStruct((ROWS, WIDTH),...  7.52 us
    ppermute x1, starting transfers between devices, body(): beside = lax.ppermute(after, 'mp', near)  7.25 us
    ppermute x1, starting transfers between devices, turn(): return lax.ppermute(mine, ('seq', 'mp'), pairs)  7.19 us
    pallas_call x3, Pallas kernels, project(): pl.pallas_call(functools.partial(project_kernel, first, len(blocks)), out...  5.81 us
    pallas_call x1, Pallas kernels, col_attend(): pl.pallas_call(col_kernel, out_shape=jax.ShapeDtypeStruct((ROWS, WIDTH +...  5.4 us
    ppermute x1, starting transfers between devices, body(): more_0 = lax.ppermute(own_0, 'seq', x_down)  4.27 us
  transfers between devices with their start and end apart: 15, of which 2 were waited for; matrix products, arithmetic and copies ran while one was open for 1% of the time, Pallas kernels for 12%

profile of v2, /device:TPU:1, one launch (start us, length us, event | category | flops | bytes accessed | tf_op | source)
XLA Modules:
  0.0 165.4 jit_solution(14500483312309244279)
XLA Ops:
  0.0 7.2 %collective-permute-start = (bf16[32,512]{1,0:T(8,128)(2,1)}, bf16[32,512]{1,0:T(8,128)(2,1)S(1)}, u32[]{:S(2)}, u32[]{:S(2)}) collective-permute-start(bf16[32,512]{1,0:T(8,128)(2,1)} %bitcast.31), channel_id=1, source_target_pairs={{0,0},{1,128},{2,256},{3,384},{4,4},{5,132},{6,260},{7,388},{8,8},... | collective-permute-start | bytes 98312 | tf_op jit(solution)/shard_map/ppermute | solution.py:266
  7.2 1.8 %maximum_maximum_fusion = bf16[512,2048]{1,0:T(8,128)(2,1)S(1)} fusion(bf16[512,512]{1,0:T(8,128)(2,1)} %v_ref.1, bf16[512,512]{1,0:T(8,128)(2,1)} %k_ref.1, bf16[512,512]{1,0:T(8,128)(2,1)} %q_ref.1, bf16[2048]{0:T(1024)(128)(2,1)S(1)} %pad.6.clone), kind=kLoop, calls=%fused_computation | loop fusion | flops 8388608 | bytes 3674112 | tf_op jit(solution)/shard_map/concatenate | solution.py:287
  9.0 0.0 collective-permute-done
  9.1 0.1 constant_dynamic-update-slice_fusion
  9.1 0.0 copy-start.3
  9.2 1.3 copy-done.3
  10.5 0.0 copy-start
  10.5 18.6 %all-to-all-start = ((bf16[64,8,2048]{2,1,0:T(8,128)(2,1)}), bf16[64,8,2048]{2,1,0:T(8,128)(2,1)S(1)}, u32[]{:S(2)}, u32[]{:S(2)}) async-start(bf16[64,8,2048]{2,1,0:T(8,128)(2,1)} %bitcast.29), calls=%async_computation | async-start | bytes 4194304 | tf_op jit(solution)/shard_map/all_to_all | solution.py:247
  29.1 3.0 %collective-permute-start.1 = (bf16[512,512]{1,0:T(8,128)(2,1)}, bf16[512,512]{1,0:T(8,128)(2,1)}, u32[]{:S(2)}, u32[]{:S(2)}) collective-permute-start(bf16[512,512]{1,0:T(8,128)(2,1)} %k_ref.1), channel_id=1, source_target_pairs={{0,4},{8,12},{16,20},{24,28},{32,36},{40,44},{48,52},{56,60},{64,6... | collective-permute-start | bytes 1572872 | tf_op jit(solution)/shard_map/ppermute | solution.py:293
  32.1 2.1 %collective-permute-start.2 = (bf16[512,512]{1,0:T(8,128)(2,1)}, bf16[512,512]{1,0:T(8,128)(2,1)}, u32[]{:S(2)}, u32[]{:S(2)}) collective-permute-start(bf16[512,512]{1,0:T(8,128)(2,1)} %v_ref.1), channel_id=1, source_target_pairs={{0,4},{8,12},{16,20},{24,28},{32,36},{40,44},{48,52},{56,60},{64,6... | collective-permute-start | bytes 1572872 | tf_op jit(solution)/shard_map/ppermute | solution.py:294
  34.2 47.3 %all-to-all-done = bf16[64,8,2048]{2,1,0:T(8,128)(2,1)S(1)} async-done(((bf16[64,8,2048]{2,1,0:T(8,128)(2,1)}), bf16[64,8,2048]{2,1,0:T(8,128)(2,1)S(1)}, u32[]{:S(2)}, u32[]{:S(2)}) %all-to-all-start) | async-done | bytes 2097184 | tf_op jit(solution)/shard_map/all_to_all | solution.py:247
  81.6 1.9 %collective-permute-start.3 = (bf16[4,16,32,128]{3,2,1,0:T(8,128)(2,1)S(1)}, bf16[4,16,32,128]{3,2,1,0:T(8,128)(2,1)}, u32[]{:S(2)}, u32[]{:S(2)}) collective-permute-start(bf16[4,16,32,128]{3,2,1,0:T(8,128)(2,1)S(1)} %bitcast.25), channel_id=1, source_target_pairs={{0,16},{4,20},{8,24},{12,28},{16,0},{20,4},{24,8},{28,12},{32,48},... | collective-permute-start | bytes 1572872 | tf_op jit(solution)/shard_map/ppermute | solution.py:297
  83.5 2.2 %collective-permute-start.4 = (bf16[4,16,32,128]{3,2,1,0:T(8,128)(2,1)S(1)}, bf16[4,16,32,128]{3,2,1,0:T(8,128)(2,1)}, u32[]{:S(2)}, u32[]{:S(2)}) collective-permute-start(bf16[4,16,32,128]{3,2,1,0:T(8,128)(2,1)S(1)} %bitcast.26), channel_id=1, source_target_pairs={{0,4},{4,8},{8,12},{12,0},{16,20},{20,24},{24,28},{28,16},{32,36},... | collective-permute-start | bytes 1572872 | tf_op jit(solution)/shard_map/ppermute | solution.py:298
  85.7 4.3 %collective-permute-start.5 = (bf16[4,16,32,128]{3,2,1,0:T(8,128)(2,1)S(1)}, bf16[4,16,32,128]{3,2,1,0:T(8,128)(2,1)}, u32[]{:S(2)}, u32[]{:S(2)}) collective-permute-start(bf16[4,16,32,128]{3,2,1,0:T(8,128)(2,1)S(1)} %bitcast.27), channel_id=1, source_target_pairs={{0,12},{4,0},{8,4},{12,8},{16,28},{20,16},{24,20},{28,24},{32,44},... | collective-permute-start | bytes 1572872 | tf_op jit(solution)/shard_map/ppermute | solution.py:299
  90.0 0.0 collective-permute-done.1.kp_ref
  90.0 0.0 collective-permute-done.2.vp_ref
  90.0 0.0 copy-done
  90.0 7.5 %row_attend.1 = (f32[512,512]{1,0:T(8,128)S(1)}, bf16[512,128]{1,0:T(8,128)(2,1)S(1)}) custom-call(s32[1]{0:T(128)} %bitcast.7.parity_ref, bf16[512,512]{1,0:T(8,128)(2,1)S(1)} %copy-done, bf16[512,512]{1,0:T(8,128)(2,1)} %k_ref.1, bf16[512,512]{1,0:T(8,128)(2,1)} %v_ref.1, bf16[512,512]{1,0:T(8,128)(2,1)} %collective-permute-done.1.kp_ref, ...), custom_call_target="tpu_custom_call" | custom-call | flops 1024 | bytes 1024 | tf_op jit(solution)/shard_map/row_attend/pallas_call | solution.py:93
  97.6 0.0 copy-start.1
  97.6 1.0 copy-done.1
  98.5 5.4 %col_attend.1 = bf16[512,640]{1,0:T(8,128)(2,1)} custom-call(bf16[512,2048]{1,0:T(8,128)(2,1)S(1)} %bitcast.23), custom_call_target="tpu_custom_call" | custom-call | flops 1024 | bytes 1024 | tf_op jit(solution)/shard_map/col_attend/pallas_call | solution.py:145
  103.9 0.0 collective-permute-done.3.refs_1_
  104.0 0.0 collective-permute-done.4.refs_6_
  104.0 0.0 collective-permute-done.5.refs_2_
  104.0 10.1 %all-to-all-start.1 = ((bf16[64,8,640]{2,1,0:T(8,128)(2,1)}), bf16[64,8,640]{2,1,0:T(8,128)(2,1)S(1)}, u32[]{:S(2)}, u32[]{:S(2)}) async-start(bf16[64,8,640]{2,1,0:T(8,128)(2,1)} %bitcast.13), calls=%async_computation.1 | async-start | bytes 1310720 | tf_op jit(solution)/shard_map/all_to_all | solution.py:247
  114.0 2.2 %collective-permute-start.8 = (bf16[4,16,32,128]{3,2,1,0:T(8,128)(2,1)}, bf16[4,16,32,128]{3,2,1,0:T(8,128)(2,1)S(1)}, u32[]{:S(2)}, u32[]{:S(2)}) collective-permute-start(bf16[4,16,32,128]{3,2,1,0:T(8,128)(2,1)} %collective-permute-done.3.refs_1_), channel_id=1, source_target_pairs={{0,4},{4,8},{8,12},{12,0},{16,20},{20,24},{24,28},{28,16},{32,36},... | collective-permute-start | bytes 1572872 | tf_op jit(solution)/shard_map/ppermute | solution.py:308
  116.3 4.3 %collective-permute-start.9 = (bf16[4,16,32,128]{3,2,1,0:T(8,128)(2,1)}, bf16[4,16,32,128]{3,2,1,0:T(8,128)(2,1)S(1)}, u32[]{:S(2)}, u32[]{:S(2)}) collective-permute-start(bf16[4,16,32,128]{3,2,1,0:T(8,128)(2,1)} %collective-permute-done.3.refs_1_), channel_id=1, source_target_pairs={{0,12},{4,0},{8,4},{12,8},{16,28},{20,16},{24,20},{28,24},{32,44},... | collective-permute-start | bytes 1572872 | tf_op jit(solution)/shard_map/ppermute | solution.py:309
  120.5 14.2 %all-to-all-done.1 = bf16[64,8,640]{2,1,0:T(8,128)(2,1)S(1)} async-done(((bf16[64,8,640]{2,1,0:T(8,128)(2,1)}), bf16[64,8,640]{2,1,0:T(8,128)(2,1)S(1)}, u32[]{:S(2)}, u32[]{:S(2)}) %all-to-all-start.1) | async-done | bytes 655392 | tf_op jit(solution)/shard_map/all_to_all | solution.py:247
  134.8 0.0 copy-start.2
  134.8 1.2 copy-done.2
  136.0 1.5 mix.1.refs_0_
  137.5 3.3 %collective-permute-start.6 = (bf16[512,512]{1,0:T(8,128)(2,1)S(1)}, bf16[512,512]{1,0:T(8,128)(2,1)}, u32[]{:S(2)}, u32[]{:S(2)}) collective-permute-start(bf16[512,512]{1,0:T(8,128)(2,1)S(1)} %mix.1.refs_0_), channel_id=1, source_target_pairs={{0,2},{1,3},{2,0},{3,1},{4,6},{5,7},{6,4},{7,5},{8,10},{9,11},{10,... | collective-permute-start | bytes 1572872 | tf_op jit(solution)/shard_map/ppermute | solution.py:316
  140.8 2.3 %collective-permute-start.11 = (bf16[4,16,32,128]{3,2,1,0:T(8,128)(2,1)}, bf16[4,16,32,128]{3,2,1,0:T(8,128)(2,1)}, u32[]{:S(2)}, u32[]{:S(2)}) collective-permute-start(bf16[4,16,32,128]{3,2,1,0:T(8,128)(2,1)} %collective-permute-done.4.refs_6_), channel_id=1, source_target_pairs={{0,4},{4,8},{8,12},{12,0},{16,20},{20,24},{24,28},{28,16},{32,36},... | collective-permute-start | bytes 1572872 | tf_op jit(solution)/shard_map/ppermute | solution.py:310
  143.1 0.0 collective-permute-done.8.refs_7_
  143.1 0.0 collective-permute-done.9.refs_3_
  143.1 4.2 %collective-permute-start.12 = (bf16[4,16,32,128]{3,2,1,0:T(8,128)(2,1)S(1)}, bf16[4,16,32,128]{3,2,1,0:T(8,128)(2,1)}, u32[]{:S(2)}, u32[]{:S(2)}) collective-permute-start(bf16[4,16,32,128]{3,2,1,0:T(8,128)(2,1)S(1)} %collective-permute-done.9.refs_3_), channel_id=1, source_target_pairs={{0,12},{4,0},{8,4},{12,8},{16,28},{20,16},{24,20},{28,24},{32,44},... | collective-permute-start | bytes 1572872 | tf_op jit(solution)/shard_map/ppermute | solution.py:318
  147.3 7.2 %collective-permute-start.10 = (bf16[512,512]{1,0:T(8,128)(2,1)S(1)}, bf16[512,512]{1,0:T(8,128)(2,1)S(1)}, u32[]{:S(2)}, u32[]{:S(2)}) collective-permute-start(bf16[512,512]{1,0:T(8,128)(2,1)S(1)} %mix.1.refs_0_), channel_id=1, source_target_pairs={{0,1},{1,0},{2,3},{3,2},{4,5},{5,4},{6,7},{7,6},{8,9},{9,8},{10,11... | collective-permute-start | bytes 1572872 | tf_op jit(solution)/shard_map/ppermute | solution.py:319
  154.6 0.0 collective-permute-done.6.refs_0_
  154.6 1.9 %collective-permute-start.7 = (bf16[512,512]{1,0:T(8,128)(2,1)}, bf16[512,512]{1,0:T(8,128)(2,1)}, u32[]{:S(2)}, u32[]{:S(2)}) collective-permute-start(bf16[512,512]{1,0:T(8,128)(2,1)} %collective-permute-done.6.refs_0_), channel_id=1, source_target_pairs={{0,1},{1,0},{2,3},{3,2},{4,5},{5,4},{6,7},{7,6},{8,9},{9,8},{10,11... | collective-permute-start | bytes 1572872 | tf_op jit(solution)/shard_map/ppermute | solution.py:320
  156.6 0.1 pad_add_fusion.place_ref
  156.6 0.0 collective-permute-done.11.refs_4_
  156.7 0.0 collective-permute-done.12.refs_5_
  156.7 2.9 %arrange.1.refs_2_ = bf16[4,1024,512]{2,1,0:T(8,128)(2,1)S(1)} custom-call(s32[3]{0:T(128)S(1)} %pad_add_fusion.place_ref, bf16[4,16,32,128]{3,2,1,0:T(8,128)(2,1)S(1)} %bitcast.28, bf16[4,16,32,128]{3,2,1,0:T(8,128)(2,1)} %collective-permute-done.3.refs_1_, bf16[4,16,32,128]{3,2,1,0:T(8,128)(2,1)} %collective-permute-done.5.refs_2_, ...), custom_call_target="tpu_custom_call" | custom-call | flops 1024 | bytes 1024 | tf_op jit(solution)/shard_map/arrange/pallas_call | solution.py:205
  159.6 0.0 collective-permute-done.10.refs_1_
  159.6 1.3 project.3.refs_1_
  160.9 1.8 %project.4.refs_1_ = f32[512,1024]{1,0:T(8,128)S(1)} custom-call(bf16[512,512]{1,0:T(8,128)(2,1)} %collective-permute-done.6.refs_0_, f32[512,1024]{1,0:T(8,128)S(1)} %project.3.refs_1_, bf16[4,1024,512]{2,1,0:T(8,128)(2,1)S(1)} %arrange.1.refs_2_), custom_call_target="tpu_custom_call" | custom-call | flops 1024 | bytes 1024 | tf_op jit(solution)/shard_map/project/pallas_call | solution.py:231
  162.7 0.0 collective-permute-done.7.refs_0_
  162.7 2.8 %project.5 = bf16[512,1024]{1,0:T(8,128)(2,1)} custom-call(bf16[512,512]{1,0:T(8,128)(2,1)} %collective-permute-done.7.refs_0_, f32[512,1024]{1,0:T(8,128)S(1)} %project.4.refs_1_, bf16[4,1024,512]{2,1,0:T(8,128)(2,1)S(1)} %arrange.1.refs_2_), custom_call_target="tpu_custom_call" | custom-call | flops 1024 | bytes 1024 | tf_op jit(solution)/shard_map/project/pallas_call | solution.py:231
  (5 shorter events, 0.1 us)
Async XLA Ops:
  0.0 9.0 %collective-permute-start = (bf16[32,512]{1,0:T(8,128)(2,1)}, bf16[32,512]{1,0:T(8,128)(2,1)S(1)}, u32[]{:S(2)}, u32[]{:S(2)}) collective-permute-start(bf16[32,512]{1,0:T(8,128)(2,1)} %bitcast.31), channel_id=1, source_target_pairs={{0,0},{1,128},{2,256},{3,384},{4,4},{5,132},{6,260},{7,388},{8,8},... | collective-permute-start | bytes 98312 | tf_op jit(solution)/shard_map/ppermute | solution.py:266
  9.1 1.3 copy-start.3
  10.5 79.6 %copy-start = (bf16[512,512]{1,0:T(8,128)(2,1)S(1)}, bf16[512,512]{1,0:T(8,128)(2,1)}, u32[]{:S(2)}) copy-start(bf16[512,512]{1,0:T(8,128)(2,1)} %q_ref.1) | copy-start | bytes 1572868
  10.5 71.0 %all-to-all-start = ((bf16[64,8,2048]{2,1,0:T(8,128)(2,1)}), bf16[64,8,2048]{2,1,0:T(8,128)(2,1)S(1)}, u32[]{:S(2)}, u32[]{:S(2)}) async-start(bf16[64,8,2048]{2,1,0:T(8,128)(2,1)} %bitcast.29), calls=%async_computation | async-start | bytes 4194304 | tf_op jit(solution)/shard_map/all_to_all | solution.py:247
  29.1 61.0 %collective-permute-start.1 = (bf16[512,512]{1,0:T(8,128)(2,1)}, bf16[512,512]{1,0:T(8,128)(2,1)}, u32[]{:S(2)}, u32[]{:S(2)}) collective-permute-start(bf16[512,512]{1,0:T(8,128)(2,1)} %k_ref.1), channel_id=1, source_target_pairs={{0,4},{8,12},{16,20},{24,28},{32,36},{40,44},{48,52},{56,60},{64,6... | collective-permute-start | bytes 1572872 | tf_op jit(solution)/shard_map/ppermute | solution.py:293
  32.1 57.9 %collective-permute-start.2 = (bf16[512,512]{1,0:T(8,128)(2,1)}, bf16[512,512]{1,0:T(8,128)(2,1)}, u32[]{:S(2)}, u32[]{:S(2)}) collective-permute-start(bf16[512,512]{1,0:T(8,128)(2,1)} %v_ref.1), channel_id=1, source_target_pairs={{0,4},{8,12},{16,20},{24,28},{32,36},{40,44},{48,52},{56,60},{64,6... | collective-permute-start | bytes 1572872 | tf_op jit(solution)/shard_map/ppermute | solution.py:294
  81.6 22.4 %collective-permute-start.3 = (bf16[4,16,32,128]{3,2,1,0:T(8,128)(2,1)S(1)}, bf16[4,16,32,128]{3,2,1,0:T(8,128)(2,1)}, u32[]{:S(2)}, u32[]{:S(2)}) collective-permute-start(bf16[4,16,32,128]{3,2,1,0:T(8,128)(2,1)S(1)} %bitcast.25), channel_id=1, source_target_pairs={{0,16},{4,20},{8,24},{12,28},{16,0},{20,4},{24,8},{28,12},{32,48},... | collective-permute-start | bytes 1572872 | tf_op jit(solution)/shard_map/ppermute | solution.py:297
  83.5 20.5 %collective-permute-start.4 = (bf16[4,16,32,128]{3,2,1,0:T(8,128)(2,1)S(1)}, bf16[4,16,32,128]{3,2,1,0:T(8,128)(2,1)}, u32[]{:S(2)}, u32[]{:S(2)}) collective-permute-start(bf16[4,16,32,128]{3,2,1,0:T(8,128)(2,1)S(1)} %bitcast.26), channel_id=1, source_target_pairs={{0,4},{4,8},{8,12},{12,0},{16,20},{20,24},{24,28},{28,16},{32,36},... | collective-permute-start | bytes 1572872 | tf_op jit(solution)/shard_map/ppermute | solution.py:298
  85.7 18.2 %collective-permute-start.5 = (bf16[4,16,32,128]{3,2,1,0:T(8,128)(2,1)S(1)}, bf16[4,16,32,128]{3,2,1,0:T(8,128)(2,1)}, u32[]{:S(2)}, u32[]{:S(2)}) collective-permute-start(bf16[4,16,32,128]{3,2,1,0:T(8,128)(2,1)S(1)} %bitcast.27), channel_id=1, source_target_pairs={{0,12},{4,0},{8,4},{12,8},{16,28},{20,16},{24,20},{28,24},{32,44},... | collective-permute-start | bytes 1572872 | tf_op jit(solution)/shard_map/ppermute | solution.py:299
  97.6 1.0 copy-start.1
  104.0 30.8 %all-to-all-start.1 = ((bf16[64,8,640]{2,1,0:T(8,128)(2,1)}), bf16[64,8,640]{2,1,0:T(8,128)(2,1)S(1)}, u32[]{:S(2)}, u32[]{:S(2)}) async-start(bf16[64,8,640]{2,1,0:T(8,128)(2,1)} %bitcast.13), calls=%async_computation.1 | async-start | bytes 1310720 | tf_op jit(solution)/shard_map/all_to_all | solution.py:247
  114.0 29.0 %collective-permute-start.8 = (bf16[4,16,32,128]{3,2,1,0:T(8,128)(2,1)}, bf16[4,16,32,128]{3,2,1,0:T(8,128)(2,1)S(1)}, u32[]{:S(2)}, u32[]{:S(2)}) collective-permute-start(bf16[4,16,32,128]{3,2,1,0:T(8,128)(2,1)} %collective-permute-done.3.refs_1_), channel_id=1, source_target_pairs={{0,4},{4,8},{8,12},{12,0},{16,20},{20,24},{24,28},{28,16},{32,36},... | collective-permute-start | bytes 1572872 | tf_op jit(solution)/shard_map/ppermute | solution.py:308
  116.3 26.8 %collective-permute-start.9 = (bf16[4,16,32,128]{3,2,1,0:T(8,128)(2,1)}, bf16[4,16,32,128]{3,2,1,0:T(8,128)(2,1)S(1)}, u32[]{:S(2)}, u32[]{:S(2)}) collective-permute-start(bf16[4,16,32,128]{3,2,1,0:T(8,128)(2,1)} %collective-permute-done.3.refs_1_), channel_id=1, source_target_pairs={{0,12},{4,0},{8,4},{12,8},{16,28},{20,16},{24,20},{28,24},{32,44},... | collective-permute-start | bytes 1572872 | tf_op jit(solution)/shard_map/ppermute | solution.py:309
  134.8 1.2 copy-start.2
  137.5 17.1 %collective-permute-start.6 = (bf16[512,512]{1,0:T(8,128)(2,1)S(1)}, bf16[512,512]{1,0:T(8,128)(2,1)}, u32[]{:S(2)}, u32[]{:S(2)}) collective-permute-start(bf16[512,512]{1,0:T(8,128)(2,1)S(1)} %mix.1.refs_0_), channel_id=1, source_target_pairs={{0,2},{1,3},{2,0},{3,1},{4,6},{5,7},{6,4},{7,5},{8,10},{9,11},{10,... | collective-permute-start | bytes 1572872 | tf_op jit(solution)/shard_map/ppermute | solution.py:316
  140.8 15.8 %collective-permute-start.11 = (bf16[4,16,32,128]{3,2,1,0:T(8,128)(2,1)}, bf16[4,16,32,128]{3,2,1,0:T(8,128)(2,1)}, u32[]{:S(2)}, u32[]{:S(2)}) collective-permute-start(bf16[4,16,32,128]{3,2,1,0:T(8,128)(2,1)} %collective-permute-done.4.refs_6_), channel_id=1, source_target_pairs={{0,4},{4,8},{8,12},{12,0},{16,20},{20,24},{24,28},{28,16},{32,36},... | collective-permute-start | bytes 1572872 | tf_op jit(solution)/shard_map/ppermute | solution.py:310
  143.1 13.6 %collective-permute-start.12 = (bf16[4,16,32,128]{3,2,1,0:T(8,128)(2,1)S(1)}, bf16[4,16,32,128]{3,2,1,0:T(8,128)(2,1)}, u32[]{:S(2)}, u32[]{:S(2)}) collective-permute-start(bf16[4,16,32,128]{3,2,1,0:T(8,128)(2,1)S(1)} %collective-permute-done.9.refs_3_), channel_id=1, source_target_pairs={{0,12},{4,0},{8,4},{12,8},{16,28},{20,16},{24,20},{28,24},{32,44},... | collective-permute-start | bytes 1572872 | tf_op jit(solution)/shard_map/ppermute | solution.py:318
  147.3 12.2 %collective-permute-start.10 = (bf16[512,512]{1,0:T(8,128)(2,1)S(1)}, bf16[512,512]{1,0:T(8,128)(2,1)S(1)}, u32[]{:S(2)}, u32[]{:S(2)}) collective-permute-start(bf16[512,512]{1,0:T(8,128)(2,1)S(1)} %mix.1.refs_0_), channel_id=1, source_target_pairs={{0,1},{1,0},{2,3},{3,2},{4,5},{5,4},{6,7},{7,6},{8,9},{9,8},{10,11... | collective-permute-start | bytes 1572872 | tf_op jit(solution)/shard_map/ppermute | solution.py:319
  154.6 8.1 %collective-permute-start.7 = (bf16[512,512]{1,0:T(8,128)(2,1)}, bf16[512,512]{1,0:T(8,128)(2,1)}, u32[]{:S(2)}, u32[]{:S(2)}) collective-permute-start(bf16[512,512]{1,0:T(8,128)(2,1)} %collective-permute-done.6.refs_0_), channel_id=1, source_target_pairs={{0,1},{1,0},{2,3},{3,2},{4,5},{5,4},{6,7},{7,6},{8,9},{9,8},{10,11... | collective-permute-start | bytes 1572872 | tf_op jit(solution)/shard_map/ppermute | solution.py:320

commit v3 on v2

--- a/solution.py
+++ b/solution.py
@@ -20,6 +20,7 @@
 FACTOR = DH ** (-0.5) * 1.4426950408889634
 VMEM = 40 * 1024 * 1024
 SMALL = pl.CostEstimate(flops=1024, bytes_accessed=1024, transcendentals=0)
+LARGE = pl.CostEstimate(flops=2 * 10**11, bytes_accessed=1024, transcendentals=0)
 
 NT = (((1,), (1,)), ((), ()))
 
@@ -78,9 +79,10 @@
         own = jnp.exp2(own - largest)
         before = jnp.exp2(before - largest)
         total = jnp.sum(own, axis=1, keepdims=True) + jnp.sum(before, axis=1, keepdims=True)
-        out_ref[here, :] = jnp.dot(
+        out = jnp.dot(
             own.astype(jnp.bfloat16), v_ref[:seen, :], preferred_element_type=jnp.float32
         ) + jnp.dot(before.astype(jnp.bfloat16), vp_ref[...], preferred_element_type=jnp.float32)
+        out_ref[here, :] = out.astype(jnp.bfloat16)
         stat_ref[here, :] = stat_lanes(stat_ref[here, :], head, largest, total)
 
     @pl.when(head == HEADS_HERE - 1)
@@ -93,7 +95,7 @@
     return pl.pallas_call(
         row_kernel,
         out_shape=(
-            jax.ShapeDtypeStruct((ROWS, WIDTH), jnp.float32),
+            jax.ShapeDtypeStruct((ROWS, WIDTH), jnp.bfloat16),
             jax.ShapeDtypeStruct((ROWS, 128), jnp.bfloat16),
         ),
         grid_spec=pltpu.PrefetchScalarGridSpec(
@@ -104,7 +106,7 @@
             scratch_shapes=[pltpu.VMEM((ROWS, 128), jnp.float32)],
         ),
         compiler_params=pltpu.CompilerParams(vmem_limit_bytes=VMEM),
-        cost_estimate=SMALL,
+        cost_estimate=LARGE,
         name="row_attend",
     )(parity, q, k, v, kp, vp)
 
@@ -115,29 +117,44 @@
     other = lax.broadcasted_iota(jnp.int32, (block, block), 1)
     same = (token & (COLS - 1)) == (other & (COLS - 1))
     earlier = same & (other < token)
+    heads = range(HEADS_HERE)
+
+    def lanes(part, head):
+        return slice(part * WIDTH + head * DH, part * WIDTH + (head + 1) * DH)
+
     for b in range(ROWS // block):
         here = slice(b * block, (b + 1) * block)
+        scores = [
+            [
+                jnp.where(
+                    same if c < b else earlier,
+                    nt_dot(
+                        qkv_ref[here, lanes(0, head)],
+                        qkv_ref[c * block : (c + 1) * block, lanes(1, head)],
+                    )
+                    * FACTOR,
+                    NEG,
+                )
+                for c in range(b + 1)
+            ]
+            for head in heads
+        ]
+        tops = [functools.reduce(jnp.maximum, scores[head]) for head in heads]
+        tops = [jnp.maximum(jnp.max(top, axis=1, keepdims=True), NONE) for top in tops]
+        weights = [[jnp.exp2(score - tops[head]) for score in scores[head]] for head in heads]
+        totals = [
+            jnp.sum(functools.reduce(jnp.add, weights[head]), axis=1, keepdims=True)
+            for head in heads
+        ]
         stats = jnp.zeros((block, 128), jnp.float32)
-        for head in range(HEADS_HERE):
-            q_lanes, k_lanes, v_lanes = (
-                slice(n * WIDTH + head * DH, n * WIDTH + (head + 1) * DH) for n in range(3)
-            )
-            q = qkv_ref[here, q_lanes]
-            scores = []
-            for c in range(b + 1):
-                score = nt_dot(q, qkv_ref[c * block : (c + 1) * block, k_lanes]) * FACTOR
-                scores.append(jnp.where(same if c < b else earlier, score, NEG))
-            largest = functools.reduce(jnp.maximum, scores)
-            largest = jnp.maximum(jnp.max(largest, axis=1, keepdims=True), NONE)
-            weights = [jnp.exp2(score - largest) for score in scores]
-            total = jnp.sum(functools.reduce(jnp.add, weights), axis=1, keepdims=True)
+        for head in heads:
             out = jnp.dot(
-                jnp.concatenate([w.astype(jnp.bfloat16) for w in weights], axis=1),
-                qkv_ref[: (b + 1) * block, v_lanes],
+                jnp.concatenate([w.astype(jnp.bfloat16) for w in weights[head]], axis=1),
+                qkv_ref[: (b + 1) * block, lanes(2, head)],
                 preferred_element_type=jnp.float32,
             )
             out_ref[here, head * DH : (head + 1) * DH] = out.astype(jnp.bfloat16)
-            stats = stat_lanes(stats, head, largest, total)
+            stats = stat_lanes(stats, head, tops[head], totals[head])
         out_ref[here, WIDTH:] = three_parts(stats)
 
 
@@ -148,7 +165,7 @@
         in_specs=[pl.BlockSpec(memory_space=pltpu.VMEM)],
         out_specs=pl.BlockSpec(memory_space=pltpu.VMEM),
         compiler_params=pltpu.CompilerParams(vmem_limit_bytes=VMEM),
-        cost_estimate=SMALL,
+        cost_estimate=LARGE,
         name="col_attend",
     )(qkv)
 
@@ -159,7 +176,7 @@
     highest = jnp.maximum(row_max, col_max)
     row_factor = jnp.exp2(row_max - highest)
     col_factor = jnp.exp2(col_max - highest)
-    mixed = row_factor * row_ref[...] + col_factor * col_ref[:, :WIDTH].astype(jnp.float32)
+    mixed = row_factor * row_ref[...].astype(jnp.float32) + col_factor * col_ref[:, :WIDTH].astype(jnp.float32)
     out_ref[...] = (mixed / (row_factor * row_total + col_factor * col_total)).astype(jnp.bfloat16)
 
 
@@ -181,8 +198,13 @@
     )(row_out, row_stat, col)
 
 
-def arrange_kernel(place_ref, *refs):
-    *pieces, out_ref = refs
+CHUNKS = 4
+
+
+def finish_kernel(place_ref, *refs):
+    blocks, pieces, out_ref = refs[:N_MP], refs[N_MP : N_MP + 8], refs[N_MP + 8]
+    weights, results = refs[N_MP + 9 : N_MP + 9 + CHUNKS], refs[N_MP + 9 + CHUNKS : -1]
+    done = refs[-1]
     y, x, mp = place_ref[0], place_ref[1], place_ref[2]
     spots = []
     for i, piece in enumerate(pieces):
@@ -190,53 +212,43 @@
         head = 2 * ((y + i % 2) & 1) + there // 2
         spots.append((piece, (there & 1) * 32, pl.multiple_of(head * DH, DH)))
 
-    def step(i, carry):
-        for piece, row, lane in spots:
-            start = pl.multiple_of(i * 64 + row, 32)
-            for group in range(N_MP):
-                out_ref[group ^ mp, pl.ds(start, 32), pl.ds(lane, DH)] = piece[group, i]
-        return carry
-
-    lax.fori_loop(0, 16, step, 0)
-
-
-def arrange(place, *pieces):
+    copies = []
+    width = PLANE * 32 // CHUNKS
+    for chunk in range(CHUNKS):
+        for i in range(16 // CHUNKS):
+            for piece, row, lane in spots:
+                start = pl.multiple_of(i * 64 + row, 32)
+                for group in range(N_MP):
+                    weights[chunk][group, pl.ds(start, 32), pl.ds(lane, DH)] = piece[
+                        group, chunk * (16 // CHUNKS) + i
+                    ]
+        total = None
+        for j in range(N_MP):
+            term = nt_dot(blocks[j][...], weights[chunk][mp ^ j])
+            total = term if total is None else total + term
+        results[chunk][...] = total.astype(jnp.bfloat16)
+        there = out_ref.at[:, chunk * width : (chunk + 1) * width]
+        copies.append(pltpu.make_async_copy(results[chunk], there, done.at[chunk]))
+        copies[-1].start()
+    for copy in copies:
+        copy.wait()
+
+
+def finish(place, blocks, pieces):
     vmem = pl.BlockSpec(memory_space=pltpu.VMEM)
+    width = PLANE * 32 // CHUNKS
     return pl.pallas_call(
-        arrange_kernel,
-        out_shape=jax.ShapeDtypeStruct((N_MP, PLANE * 32, WIDTH), jnp.bfloat16),
-        in_specs=[pl.BlockSpec(memory_space=pltpu.SMEM)] + [vmem] * len(pieces),
-        out_specs=vmem,
+        finish_kernel,
+        out_shape=jax.ShapeDtypeStruct((ROWS, PLANE * 32), jnp.bfloat16),
+        in_specs=[pl.BlockSpec(memory_space=pltpu.SMEM)] + [vmem] * (len(blocks) + len(pieces)),
+        out_specs=pl.BlockSpec(memory_space=pl.ANY),
+        scratch_shapes=[pltpu.VMEM((N_MP, width, WIDTH), jnp.bfloat16)] * CHUNKS
+        + [pltpu.VMEM((ROWS, width), jnp.bfloat16)] * CHUNKS
+        + [pltpu.SemaphoreType.DMA((CHUNKS,))],
         compiler_params=pltpu.CompilerParams(vmem_limit_bytes=VMEM),
         cost_estimate=SMALL,
-        name="arrange",
-    )(place, *pieces)
-
-
-def project_kernel(first, blocks, *refs):
-    *refs, weight_ref, out_ref = refs
-    step = 256
-    for i in range(out_ref.shape[1] // step):
-        here = slice(i * step, (i + 1) * step)
-        total = refs[blocks][:, here] if len(refs) > blocks else None
-        for j in range(blocks):
-            term = nt_dot(refs[j][...], weight_ref[first + j, here, :])
-            total = term if total is None else total + term
-        out_ref[:, here] = total.astype(out_ref.dtype)
-
-
-def project(before, blocks, weight, first, kind):
-    operands = [*blocks] + ([] if before is None else [before]) + [weight]
-    vmem = pl.BlockSpec(memory_space=pltpu.VMEM)
-    return pl.pallas_call(
-        functools.partial(project_kernel, first, len(blocks)),
-        out_shape=jax.ShapeDtypeStruct((ROWS, PLANE * 32), kind),
-        in_specs=[vmem] * len(operands),
-        out_specs=vmem,
-        compiler_params=pltpu.CompilerParams(vmem_limit_bytes=VMEM),
-        cost_estimate=SMALL,
-        name="project",
-    )(*operands)
+        name="finish",
+    )(place, *blocks, *pieces)
 
 
 def same_parity():
@@ -298,13 +310,14 @@
     less_0 = lax.ppermute(own_0, "seq", x_up)
     more_0 = lax.ppermute(own_0, "seq", x_down)
 
+    col_own = col_attend(arrived)
+    col_own, keys_before, values_before = barrier((col_own, keys_before, values_before))
+    keys_before, values_before, own_1, less_0, more_0 = barrier(
+        (keys_before, values_before, own_1, less_0, more_0)
+    )
     row_out, row_stat = row_attend(
         (seq % 2).astype(jnp.int32).reshape(1), queries, keys, values, keys_before, values_before
     )
-    arrived, row_out, row_stat = barrier((arrived, row_out, row_stat))
-
-    col_own = col_attend(arrived)
-    col_own, own_1, less_0, more_0 = barrier((col_own, own_1, less_0, more_0))
     less_1 = lax.ppermute(own_1, "seq", x_up)
     more_1 = lax.ppermute(own_1, "seq", x_down)
     far_0 = lax.ppermute(less_0, "seq", x_up)
@@ -316,13 +329,12 @@
     across = lax.ppermute(attended, "mp", far)
     after, less_1, more_1 = barrier((attended, less_1, more_1))
     far_1 = lax.ppermute(more_1, "seq", x_down)
+    after, across = barrier((after, across))
     beside = lax.ppermute(after, "mp", near)
     last = lax.ppermute(across, "mp", near)
     place = jnp.stack([seq // 4 % 8, seq % 4, mp]).astype(jnp.int32)
-    weight = arrange(place, own_0, own_1, more_0, more_1, far_0, far_1, less_0, less_1)
-    total = project(None, (attended, beside), weight, 0, jnp.float32)
-    total = project(total, (across,), weight, 2, jnp.float32)
-    return project(total, (last,), weight, 3, jnp.bfloat16)
+    pieces = (own_0, own_1, more_0, more_1, far_0, far_1, less_0, less_1)
+    return finish(place, (after, beside, across, last), pieces)
 
 
 def solution(mesh):

time: 169 us -> 156 us (0.923); the launches traced: 165 us -> 156 us
  waiting for transfers between devices: 61.6 us -> 56.9 us
  Pallas kernels: 23.1 us -> 19.3 us
    all_to_all x2, waiting for transfers between devices: 61.6 us -> 53.5 us  [swap_columns(): lax.all_to_all(value, 'seq', split_axis=0, concat_axis=0, axis_index_grou...]
    pallas_call x4 -> x1, Pallas kernels: 8.72 us -> 5.73 us  [finish(): pl.pallas_call(finish_kernel, out_shape=jax.ShapeDtypeStruct((ROWS, PLANE...]
    ppermute x1, starting transfers between devices: 4.27 us -> 1.91 us  [body(): more_0 = lax.ppermute(own_0, 'seq', x_down)]
    pallas_call x1, Pallas kernels: 5.4 us -> 3.1 us  [col_attend(): pl.pallas_call(col_kernel, out_shape=jax.ShapeDtypeStruct((ROWS, WIDTH +...]
    unnamed x8 -> x4, local copies, waits for them, and re-layouts: 3.53 us -> 1.35 us
    ppermute x1, waiting for transfers between devices: 0.01 us -> 1.75 us  [body(): last = lax.ppermute(across, 'mp', near)]
  transfers between devices with their start and end apart: 15 -> 15, of which waited for: 2 -> 4; matrix products, arithmetic and copies ran while one was open for 1% -> 2% of each run, Pallas kernels for 12% -> 9%
where the time goes in v3:
time: 156 us
  starting transfers between devices  75 us (48%)
  waiting for transfers between devices  56.9 us (36%)
  Pallas kernels  19.3 us (12%)
  local copies, waits for them, and re-layouts  2.31 us (1%)
  other arithmetic  1.85 us (1%)
    all_to_all x2, waiting for transfers between devices, swap_columns(): lax.all_to_all(value, 'seq', split_axis=0, concat_axis=0, axis_index_grou...  53.5 us
    all_to_all x2, starting transfers between devices, swap_columns(): lax.all_to_all(value, 'seq', split_axis=0, concat_axis=0, axis_index_grou...  29.9 us
    pallas_call x1, Pallas kernels, row_attend(): pl.pallas_call(row_kernel, out_shape=(jax.ShapeDtypeStruct((ROWS, WIDTH),...  7.52 us
    ppermute x1, starting transfers between devices, body(): beside = lax.ppermute(after, 'mp', near)  7.22 us
    ppermute x1, starting transfers between devices, turn(): return lax.ppermute(mine, ('seq', 'mp'), pairs)  7.19 us
    pallas_call x1, Pallas kernels, finish(): pl.pallas_call(finish_kernel, out_shape=jax.ShapeDtypeStruct((ROWS, PLANE...  5.73 us
    ppermute x1, starting transfers between devices, body(): more_1 = lax.ppermute(own_1, 'seq', x_down)  5.31 us
    ppermute x1, starting transfers between devices, body(): far_0 = lax.ppermute(less_0, 'seq', x_up)  3.44 us
  transfers between devices with their start and end apart: 15, of which 4 were waited for; matrix products, arithmetic and copies ran while one was open for 2% of the time, Pallas kernels for 9%

profile of v3, /device:TPU:1, one launch (start us, length us, event | category | flops | bytes accessed | tf_op | source)
XLA Modules:
  0.0 155.7 jit_solution(16691303626213810962)
XLA Ops:
  0.0 7.2 %collective-permute-start = (bf16[32,512]{1,0:T(8,128)(2,1)}, bf16[32,512]{1,0:T(8,128)(2,1)S(1)}, u32[]{:S(2)}, u32[]{:S(2)}) collective-permute-start(bf16[32,512]{1,0:T(8,128)(2,1)} %bitcast.26), channel_id=1, source_target_pairs={{0,0},{1,128},{2,256},{3,384},{4,4},{5,132},{6,260},{7,388},{8,8},... | collective-permute-start | bytes 98312 | tf_op jit(solution)/shard_map/ppermute | solution.py:278
  7.2 1.8 %maximum_maximum_fusion = bf16[512,2048]{1,0:T(8,128)(2,1)S(1)} fusion(bf16[512,512]{1,0:T(8,128)(2,1)} %v_ref.1, bf16[512,512]{1,0:T(8,128)(2,1)} %k_ref.1, bf16[512,512]{1,0:T(8,128)(2,1)} %q_ref.1, bf16[2048]{0:T(1024)(128)(2,1)S(1)} %pad.3.clone), kind=kLoop, calls=%fused_computation | loop fusion | flops 8388608 | bytes 3674112 | tf_op jit(solution)/shard_map/concatenate | solution.py:299
  9.0 0.0 collective-permute-done
  9.1 0.1 constant_dynamic-update-slice_fusion
  9.1 0.0 copy-start.1
  9.1 1.3 copy-done.1
  10.5 18.4 %all-to-all-start = ((bf16[64,8,2048]{2,1,0:T(8,128)(2,1)}), bf16[64,8,2048]{2,1,0:T(8,128)(2,1)S(1)}, u32[]{:S(2)}, u32[]{:S(2)}) async-start(bf16[64,8,2048]{2,1,0:T(8,128)(2,1)} %bitcast.24), calls=%async_computation | async-start | bytes 4194304 | tf_op jit(solution)/shard_map/all_to_all | solution.py:259
  28.9 3.0 %collective-permute-start.1 = (bf16[512,512]{1,0:T(8,128)(2,1)}, bf16[512,512]{1,0:T(8,128)(2,1)}, u32[]{:S(2)}, u32[]{:S(2)}) collective-permute-start(bf16[512,512]{1,0:T(8,128)(2,1)} %k_ref.1), channel_id=1, source_target_pairs={{0,4},{8,12},{16,20},{24,28},{32,36},{40,44},{48,52},{56,60},{64,6... | collective-permute-start | bytes 1572872 | tf_op jit(solution)/shard_map/ppermute | solution.py:305
  31.9 2.1 %collective-permute-start.2 = (bf16[512,512]{1,0:T(8,128)(2,1)}, bf16[512,512]{1,0:T(8,128)(2,1)}, u32[]{:S(2)}, u32[]{:S(2)}) collective-permute-start(bf16[512,512]{1,0:T(8,128)(2,1)} %v_ref.1), channel_id=1, source_target_pairs={{0,4},{8,12},{16,20},{24,28},{32,36},{40,44},{48,52},{56,60},{64,6... | collective-permute-start | bytes 1572872 | tf_op jit(solution)/shard_map/ppermute | solution.py:306
  34.0 47.3 %all-to-all-done = bf16[64,8,2048]{2,1,0:T(8,128)(2,1)S(1)} async-done(((bf16[64,8,2048]{2,1,0:T(8,128)(2,1)}), bf16[64,8,2048]{2,1,0:T(8,128)(2,1)S(1)}, u32[]{:S(2)}, u32[]{:S(2)}) %all-to-all-start) | async-done | bytes 2097184 | tf_op jit(solution)/shard_map/all_to_all | solution.py:259
  81.4 0.8 slice.4
  82.2 1.9 %collective-permute-start.5 = (bf16[4,16,32,128]{3,2,1,0:T(8,128)(2,1)}, bf16[4,16,32,128]{3,2,1,0:T(8,128)(2,1)}, u32[]{:S(2)}, u32[]{:S(2)}) collective-permute-start(bf16[4,16,32,128]{3,2,1,0:T(8,128)(2,1)} %bitcast.13.refs_4_), channel_id=1, source_target_pairs={{0,12},{4,0},{8,4},{12,8},{16,28},{20,16},{24,20},{28,24},{32,44},... | collective-permute-start | bytes 1572872 | tf_op jit(solution)/shard_map/ppermute | solution.py:311
  84.2 3.4 %collective-permute-start.4 = (bf16[4,16,32,128]{3,2,1,0:T(8,128)(2,1)}, bf16[4,16,32,128]{3,2,1,0:T(8,128)(2,1)}, u32[]{:S(2)}, u32[]{:S(2)}) collective-permute-start(bf16[4,16,32,128]{3,2,1,0:T(8,128)(2,1)} %bitcast.13.refs_4_), channel_id=1, source_target_pairs={{0,4},{4,8},{8,12},{12,0},{16,20},{20,24},{24,28},{28,16},{32,36},... | collective-permute-start | bytes 1572872 | tf_op jit(solution)/shard_map/ppermute | solution.py:310
  87.5 1.9 %collective-permute-start.3 = (bf16[4,16,32,128]{3,2,1,0:T(8,128)(2,1)}, bf16[4,16,32,128]{3,2,1,0:T(8,128)(2,1)}, u32[]{:S(2)}, u32[]{:S(2)}) collective-permute-start(bf16[4,16,32,128]{3,2,1,0:T(8,128)(2,1)} %bitcast.13.refs_4_), channel_id=1, source_target_pairs={{0,16},{4,20},{8,24},{12,28},{16,0},{20,4},{24,8},{28,12},{32,48},... | collective-permute-start | bytes 1572872 | tf_op jit(solution)/shard_map/ppermute | solution.py:309
  89.5 0.0 copy-start
  89.5 3.1 %col_attend.1 = bf16[512,640]{1,0:T(8,128)(2,1)} custom-call(bf16[512,2048]{1,0:T(8,128)(2,1)S(1)} %bitcast.23), custom_call_target="tpu_custom_call" | custom-call | flops 199999995904 | bytes 1024 | tf_op jit(solution)/shard_map/col_attend/pallas_call | solution.py:162
  92.6 0.0 collective-permute-done.1.kp_ref
  92.6 0.0 collective-permute-done.2.vp_ref
  92.6 11.5 %all-to-all-start.1 = ((bf16[64,8,640]{2,1,0:T(8,128)(2,1)}), bf16[64,8,640]{2,1,0:T(8,128)(2,1)}, u32[]{:S(2)}, u32[]{:S(2)}) async-start(bf16[64,8,640]{2,1,0:T(8,128)(2,1)} %bitcast.16), calls=%async_computation.1 | async-start | bytes 1310720 | tf_op jit(solution)/shard_map/all_to_all | solution.py:259
  104.1 0.0 collective-permute-done.5.refs_6_
  104.1 0.0 collective-permute-done.4.refs_10_
  104.1 0.0 collective-permute-done.3.refs_5_
  104.1 5.3 %collective-permute-start.7 = (bf16[4,16,32,128]{3,2,1,0:T(8,128)(2,1)}, bf16[4,16,32,128]{3,2,1,0:T(8,128)(2,1)}, u32[]{:S(2)}, u32[]{:S(2)}) collective-permute-start(bf16[4,16,32,128]{3,2,1,0:T(8,128)(2,1)} %collective-permute-done.3.refs_5_), channel_id=1, source_target_pairs={{0,12},{4,0},{8,4},{12,8},{16,28},{20,16},{24,20},{28,24},{32,44},... | collective-permute-start | bytes 1572872 | tf_op jit(solution)/shard_map/ppermute | solution.py:322
  109.4 1.9 %collective-permute-start.6 = (bf16[4,16,32,128]{3,2,1,0:T(8,128)(2,1)}, bf16[4,16,32,128]{3,2,1,0:T(8,128)(2,1)}, u32[]{:S(2)}, u32[]{:S(2)}) collective-permute-start(bf16[4,16,32,128]{3,2,1,0:T(8,128)(2,1)} %collective-permute-done.3.refs_5_), channel_id=1, source_target_pairs={{0,4},{4,8},{8,12},{12,0},{16,20},{20,24},{24,28},{28,16},{32,36},... | collective-permute-start | bytes 1572872 | tf_op jit(solution)/shard_map/ppermute | solution.py:321
  111.4 0.0 copy-done
  111.4 7.5 %row_attend.1 = (bf16[512,512]{1,0:T(8,128)(2,1)S(1)}, bf16[512,128]{1,0:T(8,128)(2,1)S(1)}) custom-call(s32[1]{0:T(128)} %bitcast.3.parity_ref, bf16[512,512]{1,0:T(8,128)(2,1)S(1)} %copy-done, bf16[512,512]{1,0:T(8,128)(2,1)} %k_ref.1, bf16[512,512]{1,0:T(8,128)(2,1)} %v_ref.1, bf16[512,512]{1,0:T(8,128)(2,1)} %collective-permute-done.1.kp_ref, ...), custom_call_target="tpu_custom_call" | custom-call | flops 199999995904 | bytes 1024 | tf_op jit(solution)/shard_map/row_attend/pallas_call | solution.py:95
  118.9 6.2 %all-to-all-done.1 = bf16[64,8,640]{2,1,0:T(8,128)(2,1)} async-done(((bf16[64,8,640]{2,1,0:T(8,128)(2,1)}), bf16[64,8,640]{2,1,0:T(8,128)(2,1)}, u32[]{:S(2)}, u32[]{:S(2)}) %all-to-all-start.1) | async-done | bytes 655392 | tf_op jit(solution)/shard_map/all_to_all | solution.py:259
  125.1 3.0 %mix.1.refs_0_ = bf16[512,512]{1,0:T(8,128)(2,1)S(1)} custom-call(bf16[512,512]{1,0:T(8,128)(2,1)S(1)} %get-tuple-element.28.row_ref, bf16[512,128]{1,0:T(8,128)(2,1)S(1)} %get-tuple-element.29.row_stat_ref, bf16[512,640]{1,0:T(8,128)(2,1)} %bitcast.17.col_ref), custom_call_target="tpu_custom_call" | custom-call | flops 1024 | bytes 1024 | tf_op jit(solution)/shard_map/mix/pallas_call | solution.py:189
  128.0 2.7 %collective-permute-start.8 = (bf16[512,512]{1,0:T(8,128)(2,1)S(1)}, bf16[512,512]{1,0:T(8,128)(2,1)S(1)}, u32[]{:S(2)}, u32[]{:S(2)}) collective-permute-start(bf16[512,512]{1,0:T(8,128)(2,1)S(1)} %mix.1.refs_0_), channel_id=1, source_target_pairs={{0,2},{1,3},{2,0},{3,1},{4,6},{5,7},{6,4},{7,5},{8,10},{9,11},{10,... | collective-permute-start | bytes 1572872 | tf_op jit(solution)/shard_map/ppermute | solution.py:329
  130.8 3.4 %collective-permute-start.11 = (bf16[4,16,32,128]{3,2,1,0:T(8,128)(2,1)}, bf16[4,16,32,128]{3,2,1,0:T(8,128)(2,1)S(1)}, u32[]{:S(2)}, u32[]{:S(2)}) collective-permute-start(bf16[4,16,32,128]{3,2,1,0:T(8,128)(2,1)} %collective-permute-done.4.refs_10_), channel_id=1, source_target_pairs={{0,4},{4,8},{8,12},{12,0},{16,20},{20,24},{24,28},{28,16},{32,36},... | collective-permute-start | bytes 1572872 | tf_op jit(solution)/shard_map/ppermute | solution.py:323
  134.2 0.0 collective-permute-done.7.refs_7_
  134.2 0.0 collective-permute-done.6.refs_11_
  134.2 3.0 %collective-permute-start.12 = (bf16[4,16,32,128]{3,2,1,0:T(8,128)(2,1)}, bf16[4,16,32,128]{3,2,1,0:T(8,128)(2,1)S(1)}, u32[]{:S(2)}, u32[]{:S(2)}) collective-permute-start(bf16[4,16,32,128]{3,2,1,0:T(8,128)(2,1)} %collective-permute-done.7.refs_7_), channel_id=1, source_target_pairs={{0,12},{4,0},{8,4},{12,8},{16,28},{20,16},{24,20},{28,24},{32,44},... | collective-permute-start | bytes 1572872 | tf_op jit(solution)/shard_map/ppermute | solution.py:331
  137.3 1.7 %collective-permute-done.8.refs_2_ = bf16[512,512]{1,0:T(8,128)(2,1)S(1)} collective-permute-done((bf16[512,512]{1,0:T(8,128)(2,1)S(1)}, bf16[512,512]{1,0:T(8,128)(2,1)S(1)}, u32[]{:S(2)}, u32[]{:S(2)}) %collective-permute-start.8) | collective-permute-done | bytes 524320 | tf_op jit(solution)/shard_map/ppermute | solution.py:329
  138.9 7.2 %collective-permute-start.9 = (bf16[512,512]{1,0:T(8,128)(2,1)S(1)}, bf16[512,512]{1,0:T(8,128)(2,1)S(1)}, u32[]{:S(2)}, u32[]{:S(2)}) collective-permute-start(bf16[512,512]{1,0:T(8,128)(2,1)S(1)} %mix.1.refs_0_), channel_id=1, source_target_pairs={{0,1},{1,0},{2,3},{3,2},{4,5},{5,4},{6,7},{7,6},{8,9},{9,8},{10,11... | collective-permute-start | bytes 1572872 | tf_op jit(solution)/shard_map/ppermute | solution.py:333
  146.2 1.9 %collective-permute-start.10 = (bf16[512,512]{1,0:T(8,128)(2,1)S(1)}, bf16[512,512]{1,0:T(8,128)(2,1)S(1)}, u32[]{:S(2)}, u32[]{:S(2)}) collective-permute-start(bf16[512,512]{1,0:T(8,128)(2,1)S(1)} %collective-permute-done.8.refs_2_), channel_id=1, source_target_pairs={{0,1},{1,0},{2,3},{3,2},{4,5},{5,4},{6,7},{7,6},{8,9},{9,8},{10,11... | collective-permute-start | bytes 1572872 | tf_op jit(solution)/shard_map/ppermute | solution.py:334
  148.1 0.1 pad_add_fusion.place_ref
  148.2 0.0 collective-permute-done.11.refs_8_
  148.2 0.0 collective-permute-done.12.refs_9_
  148.2 0.0 collective-permute-done.9.refs_1_
  148.2 1.7 %collective-permute-done.10.refs_3_ = bf16[512,512]{1,0:T(8,128)(2,1)S(1)} collective-permute-done((bf16[512,512]{1,0:T(8,128)(2,1)S(1)}, bf16[512,512]{1,0:T(8,128)(2,1)S(1)}, u32[]{:S(2)}, u32[]{:S(2)}) %collective-permute-start.10) | collective-permute-done | bytes 524320 | tf_op jit(solution)/shard_map/ppermute | solution.py:334
  150.0 5.7 %finish.1 = bf16[512,1024]{1,0:T(8,128)(2,1)} custom-call(s32[3]{0:T(128)S(1)} %pad_add_fusion.place_ref, bf16[512,512]{1,0:T(8,128)(2,1)S(1)} %mix.1.refs_0_, bf16[512,512]{1,0:T(8,128)(2,1)S(1)} %collective-permute-done.9.refs_1_, bf16[512,512]{1,0:T(8,128)(2,1)S(1)} %collective-permute-done.8.refs_2_, ...), custom_call_target="tpu_custom_call" | custom-call | flops 1024 | bytes 1024 | tf_op jit(solution)/shard_map/finish/pallas_call | solution.py:240
  (4 shorter events, 0.1 us)
Async XLA Ops:
  0.0 9.0 %collective-permute-start = (bf16[32,512]{1,0:T(8,128)(2,1)}, bf16[32,512]{1,0:T(8,128)(2,1)S(1)}, u32[]{:S(2)}, u32[]{:S(2)}) collective-permute-start(bf16[32,512]{1,0:T(8,128)(2,1)} %bitcast.26), channel_id=1, source_target_pairs={{0,0},{1,128},{2,256},{3,384},{4,4},{5,132},{6,260},{7,388},{8,8},... | collective-permute-start | bytes 98312 | tf_op jit(solution)/shard_map/ppermute | solution.py:278
  9.1 1.3 copy-start.1
  10.5 70.9 %all-to-all-start = ((bf16[64,8,2048]{2,1,0:T(8,128)(2,1)}), bf16[64,8,2048]{2,1,0:T(8,128)(2,1)S(1)}, u32[]{:S(2)}, u32[]{:S(2)}) async-start(bf16[64,8,2048]{2,1,0:T(8,128)(2,1)} %bitcast.24), calls=%async_computation | async-start | bytes 4194304 | tf_op jit(solution)/shard_map/all_to_all | solution.py:259
  28.9 63.6 %collective-permute-start.1 = (bf16[512,512]{1,0:T(8,128)(2,1)}, bf16[512,512]{1,0:T(8,128)(2,1)}, u32[]{:S(2)}, u32[]{:S(2)}) collective-permute-start(bf16[512,512]{1,0:T(8,128)(2,1)} %k_ref.1), channel_id=1, source_target_pairs={{0,4},{8,12},{16,20},{24,28},{32,36},{40,44},{48,52},{56,60},{64,6... | collective-permute-start | bytes 1572872 | tf_op jit(solution)/shard_map/ppermute | solution.py:305
  31.9 60.6 %collective-permute-start.2 = (bf16[512,512]{1,0:T(8,128)(2,1)}, bf16[512,512]{1,0:T(8,128)(2,1)}, u32[]{:S(2)}, u32[]{:S(2)}) collective-permute-start(bf16[512,512]{1,0:T(8,128)(2,1)} %v_ref.1), channel_id=1, source_target_pairs={{0,4},{8,12},{16,20},{24,28},{32,36},{40,44},{48,52},{56,60},{64,6... | collective-permute-start | bytes 1572872 | tf_op jit(solution)/shard_map/ppermute | solution.py:306
  82.2 21.9 %collective-permute-start.5 = (bf16[4,16,32,128]{3,2,1,0:T(8,128)(2,1)}, bf16[4,16,32,128]{3,2,1,0:T(8,128)(2,1)}, u32[]{:S(2)}, u32[]{:S(2)}) collective-permute-start(bf16[4,16,32,128]{3,2,1,0:T(8,128)(2,1)} %bitcast.13.refs_4_), channel_id=1, source_target_pairs={{0,12},{4,0},{8,4},{12,8},{16,28},{20,16},{24,20},{28,24},{32,44},... | collective-permute-start | bytes 1572872 | tf_op jit(solution)/shard_map/ppermute | solution.py:311
  84.2 19.9 %collective-permute-start.4 = (bf16[4,16,32,128]{3,2,1,0:T(8,128)(2,1)}, bf16[4,16,32,128]{3,2,1,0:T(8,128)(2,1)}, u32[]{:S(2)}, u32[]{:S(2)}) collective-permute-start(bf16[4,16,32,128]{3,2,1,0:T(8,128)(2,1)} %bitcast.13.refs_4_), channel_id=1, source_target_pairs={{0,4},{4,8},{8,12},{12,0},{16,20},{20,24},{24,28},{28,16},{32,36},... | collective-permute-start | bytes 1572872 | tf_op jit(solution)/shard_map/ppermute | solution.py:310
  87.5 16.6 %collective-permute-start.3 = (bf16[4,16,32,128]{3,2,1,0:T(8,128)(2,1)}, bf16[4,16,32,128]{3,2,1,0:T(8,128)(2,1)}, u32[]{:S(2)}, u32[]{:S(2)}) collective-permute-start(bf16[4,16,32,128]{3,2,1,0:T(8,128)(2,1)} %bitcast.13.refs_4_), channel_id=1, source_target_pairs={{0,16},{4,20},{8,24},{12,28},{16,0},{20,4},{24,8},{28,12},{32,48},... | collective-permute-start | bytes 1572872 | tf_op jit(solution)/shard_map/ppermute | solution.py:309
  89.5 21.9 %copy-start = (bf16[512,512]{1,0:T(8,128)(2,1)S(1)}, bf16[512,512]{1,0:T(8,128)(2,1)}, u32[]{:S(2)}) copy-start(bf16[512,512]{1,0:T(8,128)(2,1)} %q_ref.1) | copy-start | bytes 1572868
  92.6 32.5 %all-to-all-start.1 = ((bf16[64,8,640]{2,1,0:T(8,128)(2,1)}), bf16[64,8,640]{2,1,0:T(8,128)(2,1)}, u32[]{:S(2)}, u32[]{:S(2)}) async-start(bf16[64,8,640]{2,1,0:T(8,128)(2,1)} %bitcast.16), calls=%async_computation.1 | async-start | bytes 1310720 | tf_op jit(solution)/shard_map/all_to_all | solution.py:259
  104.1 30.1 %collective-permute-start.7 = (bf16[4,16,32,128]{3,2,1,0:T(8,128)(2,1)}, bf16[4,16,32,128]{3,2,1,0:T(8,128)(2,1)}, u32[]{:S(2)}, u32[]{:S(2)}) collective-permute-start(bf16[4,16,32,128]{3,2,1,0:T(8,128)(2,1)} %collective-permute-done.3.refs_5_), channel_id=1, source_target_pairs={{0,12},{4,0},{8,4},{12,8},{16,28},{20,16},{24,20},{28,24},{32,44},... | collective-permute-start | bytes 1572872 | tf_op jit(solution)/shard_map/ppermute | solution.py:322
  109.4 24.8 %collective-permute-start.6 = (bf16[4,16,32,128]{3,2,1,0:T(8,128)(2,1)}, bf16[4,16,32,128]{3,2,1,0:T(8,128)(2,1)}, u32[]{:S(2)}, u32[]{:S(2)}) collective-permute-start(bf16[4,16,32,128]{3,2,1,0:T(8,128)(2,1)} %collective-permute-done.3.refs_5_), channel_id=1, source_target_pairs={{0,4},{4,8},{8,12},{12,0},{16,20},{20,24},{24,28},{28,16},{32,36},... | collective-permute-start | bytes 1572872 | tf_op jit(solution)/shard_map/ppermute | solution.py:321
  128.0 10.9 %collective-permute-start.8 = (bf16[512,512]{1,0:T(8,128)(2,1)S(1)}, bf16[512,512]{1,0:T(8,128)(2,1)S(1)}, u32[]{:S(2)}, u32[]{:S(2)}) collective-permute-start(bf16[512,512]{1,0:T(8,128)(2,1)S(1)} %mix.1.refs_0_), channel_id=1, source_target_pairs={{0,2},{1,3},{2,0},{3,1},{4,6},{5,7},{6,4},{7,5},{8,10},{9,11},{10,... | collective-permute-start | bytes 1572872 | tf_op jit(solution)/shard_map/ppermute | solution.py:329
  130.8 17.5 %collective-permute-start.11 = (bf16[4,16,32,128]{3,2,1,0:T(8,128)(2,1)}, bf16[4,16,32,128]{3,2,1,0:T(8,128)(2,1)S(1)}, u32[]{:S(2)}, u32[]{:S(2)}) collective-permute-start(bf16[4,16,32,128]{3,2,1,0:T(8,128)(2,1)} %collective-permute-done.4.refs_10_), channel_id=1, source_target_pairs={{0,4},{4,8},{8,12},{12,0},{16,20},{20,24},{24,28},{28,16},{32,36},... | collective-permute-start | bytes 1572872 | tf_op jit(solution)/shard_map/ppermute | solution.py:323
  134.2 14.0 %collective-permute-start.12 = (bf16[4,16,32,128]{3,2,1,0:T(8,128)(2,1)}, bf16[4,16,32,128]{3,2,1,0:T(8,128)(2,1)S(1)}, u32[]{:S(2)}, u32[]{:S(2)}) collective-permute-start(bf16[4,16,32,128]{3,2,1,0:T(8,128)(2,1)} %collective-permute-done.7.refs_7_), channel_id=1, source_target_pairs={{0,12},{4,0},{8,4},{12,8},{16,28},{20,16},{24,20},{28,24},{32,44},... | collective-permute-start | bytes 1572872 | tf_op jit(solution)/shard_map/ppermute | solution.py:331
  138.9 9.3 %collective-permute-start.9 = (bf16[512,512]{1,0:T(8,128)(2,1)S(1)}, bf16[512,512]{1,0:T(8,128)(2,1)S(1)}, u32[]{:S(2)}, u32[]{:S(2)}) collective-permute-start(bf16[512,512]{1,0:T(8,128)(2,1)S(1)} %mix.1.refs_0_), channel_id=1, source_target_pairs={{0,1},{1,0},{2,3},{3,2},{4,5},{5,4},{6,7},{7,6},{8,9},{9,8},{10,11... | collective-permute-start | bytes 1572872 | tf_op jit(solution)/shard_map/ppermute | solution.py:333
  146.2 3.8 %collective-permute-start.10 = (bf16[512,512]{1,0:T(8,128)(2,1)S(1)}, bf16[512,512]{1,0:T(8,128)(2,1)S(1)}, u32[]{:S(2)}, u32[]{:S(2)}) collective-permute-start(bf16[512,512]{1,0:T(8,128)(2,1)S(1)} %collective-permute-done.8.refs_2_), channel_id=1, source_target_pairs={{0,1},{1,0},{2,3},{3,2},{4,5},{5,4},{6,7},{7,6},{8,9},{9,8},{10,11... | collective-permute-start | bytes 1572872 | tf_op jit(solution)/shard_map/ppermute | solution.py:334

commit v4 on v3

--- a/solution.py
+++ b/solution.py
@@ -54,57 +54,69 @@
     return largest, total
 
 
-def row_kernel(parity_ref, q_ref, k_ref, v_ref, kp_ref, vp_ref, out_ref, packed_ref, stat_ref):
-    head = pl.program_id(0)
+def head_lanes(head, part=0):
+    return slice(part * WIDTH + head * DH, part * WIDTH + (head + 1) * DH)
+
+
+def soften(scores):
+    top = jnp.max(functools.reduce(jnp.maximum, scores), axis=1, keepdims=True)
+    top = jnp.maximum(top, NONE)
+    weights = [jnp.exp2(score - top) for score in scores]
+    total = jnp.sum(functools.reduce(jnp.add, weights), axis=1, keepdims=True)
+    return top, weights, total
+
+
+def row_kernel(parity_ref, q_ref, k_ref, v_ref, kp_ref, vp_ref, out_ref, packed_ref):
     odd = parity_ref[0] == 1
     block = 128
-
-    @pl.when(head == 0)
-    def _():
-        stat_ref[...] = jnp.zeros_like(stat_ref)
-
+    token = lax.broadcasted_iota(jnp.int32, (block, block), 0)
+    other = lax.broadcasted_iota(jnp.int32, (block, block), 1)
+    causal = other <= token
+    heads = range(HEADS_HERE)
     for b in range(ROWS // block):
         here = slice(b * block, (b + 1) * block)
-        seen = (b + 1) * block
-        q = q_ref[here, :]
-        own = nt_dot(q, k_ref[:seen, :]) * FACTOR
-        place = lax.broadcasted_iota(jnp.int32, (block, seen), 0) + b * block
-        other = lax.broadcasted_iota(jnp.int32, (block, seen), 1)
-        own = jnp.where(other <= place, own, NEG)
-        before = nt_dot(q, kp_ref[...]) * FACTOR
-        before = jnp.where(odd, before, NEG)
-        largest = jnp.maximum(
-            jnp.max(own, axis=1, keepdims=True), jnp.max(before, axis=1, keepdims=True)
-        )
-        own = jnp.exp2(own - largest)
-        before = jnp.exp2(before - largest)
-        total = jnp.sum(own, axis=1, keepdims=True) + jnp.sum(before, axis=1, keepdims=True)
-        out = jnp.dot(
-            own.astype(jnp.bfloat16), v_ref[:seen, :], preferred_element_type=jnp.float32
-        ) + jnp.dot(before.astype(jnp.bfloat16), vp_ref[...], preferred_element_type=jnp.float32)
-        out_ref[here, :] = out.astype(jnp.bfloat16)
-        stat_ref[here, :] = stat_lanes(stat_ref[here, :], head, largest, total)
-
-    @pl.when(head == HEADS_HERE - 1)
-    def _():
-        packed_ref[...] = three_parts(stat_ref[...])
+        scores = []
+        for head in heads:
+            lanes = head_lanes(head)
+            q = q_ref[here, lanes]
+            row = []
+            for c in range(b + 1):
+                score = nt_dot(q, k_ref[c * block : (c + 1) * block, lanes]) * FACTOR
+                row.append(score if c < b else jnp.where(causal, score, NEG))
+            for c in range(ROWS // block):
+                score = nt_dot(q, kp_ref[c * block : (c + 1) * block, lanes]) * FACTOR
+                row.append(jnp.where(odd, score, NEG))
+            scores.append(row)
+        soft = [soften(row) for row in scores]
+        stats = jnp.zeros((block, 128), jnp.float32)
+        for head in heads:
+            lanes = head_lanes(head)
+            top, weights, total = soft[head]
+            weights = [w.astype(jnp.bfloat16) for w in weights]
+            out = jnp.dot(
+                jnp.concatenate(weights[: b + 1], axis=1),
+                v_ref[: (b + 1) * block, lanes],
+                preferred_element_type=jnp.float32,
+            ) + jnp.dot(
+                jnp.concatenate(weights[b + 1 :], axis=1),
+                vp_ref[:, lanes],
+                preferred_element_type=jnp.float32,
+            )
+            out_ref[here, lanes] = out.astype(jnp.bfloat16)
+            stats = stat_lanes(stats, head, top, total)
+        packed_ref[here, :] = three_parts(stats)
 
 
 def row_attend(parity, q, k, v, kp, vp):
-    per_head = pl.BlockSpec((ROWS, DH), lambda h, s: (0, h))
+    vmem = pl.BlockSpec(memory_space=pltpu.VMEM)
     return pl.pallas_call(
         row_kernel,
         out_shape=(
             jax.ShapeDtypeStruct((ROWS, WIDTH), jnp.bfloat16),
             jax.ShapeDtypeStruct((ROWS, 128), jnp.bfloat16),
         ),
-        grid_spec=pltpu.PrefetchScalarGridSpec(
-            num_scalar_prefetch=1,
-            grid=(HEADS_HERE,),
-            in_specs=[per_head] * 5,
-            out_specs=(per_head, pl.BlockSpec((ROWS, 128), lambda h, s: (0, 0))),
-            scratch_shapes=[pltpu.VMEM((ROWS, 128), jnp.float32)],
-        ),
+        in_specs=[pl.BlockSpec(memory_space=pltpu.SMEM)] + [vmem] * 5,
+        out_specs=(vmem, vmem),
         compiler_params=pltpu.CompilerParams(vmem_limit_bytes=VMEM),
         cost_estimate=LARGE,
         name="row_attend",
@@ -171,27 +183,27 @@
 
 
 def mix_kernel(row_ref, row_stat_ref, col_ref, out_ref):
-    row_max, row_total = spread_stats(row_stat_ref[...])
-    col_max, col_total = spread_stats(col_ref[:, WIDTH : WIDTH + 128])
-    highest = jnp.maximum(row_max, col_max)
-    row_factor = jnp.exp2(row_max - highest)
-    col_factor = jnp.exp2(col_max - highest)
-    mixed = row_factor * row_ref[...].astype(jnp.float32) + col_factor * col_ref[:, :WIDTH].astype(jnp.float32)
-    out_ref[...] = (mixed / (row_factor * row_total + col_factor * col_total)).astype(jnp.bfloat16)
+    block = 128
+    for b in range(ROWS // block):
+        here = slice(b * block, (b + 1) * block)
+        row_max, row_total = spread_stats(row_stat_ref[here, :])
+        col_max, col_total = spread_stats(col_ref[here, WIDTH : WIDTH + 128])
+        highest = jnp.maximum(row_max, col_max)
+        row_factor = jnp.exp2(row_max - highest)
+        col_factor = jnp.exp2(col_max - highest)
+        row, col = (ref[here, :WIDTH].astype(jnp.float32) for ref in (row_ref, col_ref))
+        mixed = row_factor * row + col_factor * col
+        total = row_factor * row_total + col_factor * col_total
+        out_ref[here, :] = (mixed / total).astype(jnp.bfloat16)
 
 
 def mix(row_out, row_stat, col):
-    block = 128
-
-    def rows(width):
-        return pl.BlockSpec((block, width), lambda i: (i, 0))
-
+    vmem = pl.BlockSpec(memory_space=pltpu.VMEM)
     return pl.pallas_call(
         mix_kernel,
         out_shape=jax.ShapeDtypeStruct((ROWS, WIDTH), jnp.bfloat16),
-        grid=(ROWS // block,),
-        in_specs=[rows(WIDTH), rows(128), rows(WIDTH + 128)],
-        out_specs=rows(WIDTH),
+        in_specs=[vmem] * 3,
+        out_specs=vmem,
         compiler_params=pltpu.CompilerParams(vmem_limit_bytes=VMEM),
         cost_estimate=SMALL,
         name="mix",
@@ -307,27 +319,27 @@
 
     own_0 = weight_piece(arrived[:, 3 * WIDTH :])
     own_1 = lax.ppermute(own_0, "seq", y_pair)
+
+    col_own = col_attend(arrived)
+    col_own, keys_before, values_before, own_0 = barrier(
+        (col_own, keys_before, values_before, own_0)
+    )
+    keys_before, values_before, own_1 = barrier((keys_before, values_before, own_1))
     less_0 = lax.ppermute(own_0, "seq", x_up)
     more_0 = lax.ppermute(own_0, "seq", x_down)
-
-    col_own = col_attend(arrived)
-    col_own, keys_before, values_before = barrier((col_own, keys_before, values_before))
-    keys_before, values_before, own_1, less_0, more_0 = barrier(
-        (keys_before, values_before, own_1, less_0, more_0)
-    )
     row_out, row_stat = row_attend(
         (seq % 2).astype(jnp.int32).reshape(1), queries, keys, values, keys_before, values_before
     )
     less_1 = lax.ppermute(own_1, "seq", x_up)
     more_1 = lax.ppermute(own_1, "seq", x_down)
-    far_0 = lax.ppermute(less_0, "seq", x_up)
     col = swap_columns(col_own)
     attended = mix(row_out, row_stat, col)
 
     near = [(i, i ^ 1) for i in range(N_MP)]
     far = [(i, i ^ 2) for i in range(N_MP)]
     across = lax.ppermute(attended, "mp", far)
-    after, less_1, more_1 = barrier((attended, less_1, more_1))
+    after, less_0, more_0, less_1, more_1 = barrier((attended, less_0, more_0, less_1, more_1))
+    far_0 = lax.ppermute(less_0, "seq", x_up)
     far_1 = lax.ppermute(more_1, "seq", x_down)
     after, across = barrier((after, across))
     beside = lax.ppermute(after, "mp", near)

time: 156 us -> 156 us (level)
  waiting for transfers between devices: 56.9 us -> 60.1 us
  Pallas kernels: 19.3 us -> 16.4 us
    all_to_all x2, waiting for transfers between devices: 53.5 us -> 55.5 us  [swap_columns(): lax.all_to_all(value, 'seq', split_axis=0, concat_axis=0, axis_index_grou...]
    pallas_call x1, Pallas kernels: 7.52 us -> 5.51 us  [row_attend(): pl.pallas_call(row_kernel, out_shape=(jax.ShapeDtypeStruct((ROWS, WIDTH),...]
  transfers between devices with their start and end apart: 15 -> 15, of which waited for: 4 -> 4; matrix products, arithmetic and copies ran while one was open for 2% -> 2% of each run, Pallas kernels for 9% -> 7%
where the time goes in v4:
time: 156 us; the launch traced here: 155 us
  starting transfers between devices  73.9 us (47%)
  waiting for transfers between devices  60.1 us (39%)
  Pallas kernels  16.4 us (11%)
  local copies, waits for them, and re-layouts  2.31 us (1%)
  other arithmetic  1.85 us (1%)
    all_to_all x2, waiting for transfers between devices, swap_columns(): lax.all_to_all(value, 'seq', split_axis=0, concat_axis=0, axis_index_grou...  55.5 us
    all_to_all x2, starting transfers between devices, swap_columns(): lax.all_to_all(value, 'seq', split_axis=0, concat_axis=0, axis_index_grou...  29.9 us
    ppermute x1, starting transfers between devices, body(): beside = lax.ppermute(after, 'mp', near)  7.22 us
    ppermute x1, starting transfers between devices, turn(): return lax.ppermute(mine, ('seq', 'mp'), pairs)  7.19 us
    pallas_call x1, Pallas kernels, finish(): pl.pallas_call(finish_kernel, out_shape=jax.ShapeDtypeStruct((ROWS, PLANE...  5.73 us
    pallas_call x1, Pallas kernels, row_attend(): pl.pallas_call(row_kernel, out_shape=(jax.ShapeDtypeStruct((ROWS, WIDTH),...  5.51 us
    ppermute x1, starting transfers between devices, body(): more_1 = lax.ppermute(own_1, 'seq', x_down)  5.31 us
    ppermute x1, starting transfers between devices, body(): far_0 = lax.ppermute(less_0, 'seq', x_up)  3.44 us
  transfers between devices with their start and end apart: 15, of which 4 were waited for; matrix products, arithmetic and copies ran while one was open for 2% of the time, Pallas kernels for 7%

profile of v4, /device:TPU:1, one launch (start us, length us, event | category | flops | bytes accessed | tf_op | source)
XLA Modules:
  0.0 154.8 jit_solution(11531162384260880903)
XLA Ops:
  0.0 7.2 %collective-permute-start = (bf16[32,512]{1,0:T(8,128)(2,1)}, bf16[32,512]{1,0:T(8,128)(2,1)S(1)}, u32[]{:S(2)}, u32[]{:S(2)}) collective-permute-start(bf16[32,512]{1,0:T(8,128)(2,1)} %bitcast.26), channel_id=1, source_target_pairs={{0,0},{1,128},{2,256},{3,384},{4,4},{5,132},{6,260},{7,388},{8,8},... | collective-permute-start | bytes 98312 | tf_op jit(solution)/shard_map/ppermute | solution.py:290
  7.2 1.8 %maximum_maximum_fusion = bf16[512,2048]{1,0:T(8,128)(2,1)S(1)} fusion(bf16[512,512]{1,0:T(8,128)(2,1)} %v_ref.1, bf16[512,512]{1,0:T(8,128)(2,1)} %k_ref.1, bf16[512,512]{1,0:T(8,128)(2,1)} %q_ref.1, bf16[2048]{0:T(1024)(128)(2,1)S(1)} %pad.3.clone), kind=kLoop, calls=%fused_computation | loop fusion | flops 8388608 | bytes 3674112 | tf_op jit(solution)/shard_map/concatenate | solution.py:311
  9.0 0.0 collective-permute-done
  9.1 0.1 constant_dynamic-update-slice_fusion
  9.1 0.0 copy-start.1
  9.1 1.3 copy-done.1
  10.5 18.4 %all-to-all-start = ((bf16[64,8,2048]{2,1,0:T(8,128)(2,1)}), bf16[64,8,2048]{2,1,0:T(8,128)(2,1)S(1)}, u32[]{:S(2)}, u32[]{:S(2)}) async-start(bf16[64,8,2048]{2,1,0:T(8,128)(2,1)} %bitcast.24), calls=%async_computation | async-start | bytes 4194304 | tf_op jit(solution)/shard_map/all_to_all | solution.py:271
  28.9 3.0 %collective-permute-start.1 = (bf16[512,512]{1,0:T(8,128)(2,1)}, bf16[512,512]{1,0:T(8,128)(2,1)}, u32[]{:S(2)}, u32[]{:S(2)}) collective-permute-start(bf16[512,512]{1,0:T(8,128)(2,1)} %k_ref.1), channel_id=1, source_target_pairs={{0,4},{8,12},{16,20},{24,28},{32,36},{40,44},{48,52},{56,60},{64,6... | collective-permute-start | bytes 1572872 | tf_op jit(solution)/shard_map/ppermute | solution.py:317
  31.9 2.1 %collective-permute-start.2 = (bf16[512,512]{1,0:T(8,128)(2,1)}, bf16[512,512]{1,0:T(8,128)(2,1)}, u32[]{:S(2)}, u32[]{:S(2)}) collective-permute-start(bf16[512,512]{1,0:T(8,128)(2,1)} %v_ref.1), channel_id=1, source_target_pairs={{0,4},{8,12},{16,20},{24,28},{32,36},{40,44},{48,52},{56,60},{64,6... | collective-permute-start | bytes 1572872 | tf_op jit(solution)/shard_map/ppermute | solution.py:318
  34.0 47.3 %all-to-all-done = bf16[64,8,2048]{2,1,0:T(8,128)(2,1)S(1)} async-done(((bf16[64,8,2048]{2,1,0:T(8,128)(2,1)}), bf16[64,8,2048]{2,1,0:T(8,128)(2,1)S(1)}, u32[]{:S(2)}, u32[]{:S(2)}) %all-to-all-start) | async-done | bytes 2097184 | tf_op jit(solution)/shard_map/all_to_all | solution.py:271
  81.4 0.8 slice.4
  82.2 1.9 %collective-permute-start.3 = (bf16[4,16,32,128]{3,2,1,0:T(8,128)(2,1)}, bf16[4,16,32,128]{3,2,1,0:T(8,128)(2,1)}, u32[]{:S(2)}, u32[]{:S(2)}) collective-permute-start(bf16[4,16,32,128]{3,2,1,0:T(8,128)(2,1)} %bitcast.13.refs_4_), channel_id=1, source_target_pairs={{0,16},{4,20},{8,24},{12,28},{16,0},{20,4},{24,8},{28,12},{32,48},... | collective-permute-start | bytes 1572872 | tf_op jit(solution)/shard_map/ppermute | solution.py:321
  84.2 0.0 copy-start
  84.2 3.1 %col_attend.1 = bf16[512,640]{1,0:T(8,128)(2,1)} custom-call(bf16[512,2048]{1,0:T(8,128)(2,1)S(1)} %bitcast.23), custom_call_target="tpu_custom_call" | custom-call | flops 199999995904 | bytes 1024 | tf_op jit(solution)/shard_map/col_attend/pallas_call | solution.py:174
  87.3 0.0 collective-permute-done.1.kp_ref
  87.3 0.0 collective-permute-done.2.vp_ref
  87.3 1.9 %collective-permute-start.5 = (bf16[4,16,32,128]{3,2,1,0:T(8,128)(2,1)}, bf16[4,16,32,128]{3,2,1,0:T(8,128)(2,1)}, u32[]{:S(2)}, u32[]{:S(2)}) collective-permute-start(bf16[4,16,32,128]{3,2,1,0:T(8,128)(2,1)} %bitcast.13.refs_4_), channel_id=1, source_target_pairs={{0,12},{4,0},{8,4},{12,8},{16,28},{20,16},{24,20},{28,24},{32,44},... | collective-permute-start | bytes 1572872 | tf_op jit(solution)/shard_map/ppermute | solution.py:329
  89.2 3.4 %collective-permute-start.4 = (bf16[4,16,32,128]{3,2,1,0:T(8,128)(2,1)}, bf16[4,16,32,128]{3,2,1,0:T(8,128)(2,1)}, u32[]{:S(2)}, u32[]{:S(2)}) collective-permute-start(bf16[4,16,32,128]{3,2,1,0:T(8,128)(2,1)} %bitcast.13.refs_4_), channel_id=1, source_target_pairs={{0,4},{4,8},{8,12},{12,0},{16,20},{20,24},{24,28},{28,16},{32,36},... | collective-permute-start | bytes 1572872 | tf_op jit(solution)/shard_map/ppermute | solution.py:328
  92.6 11.5 %all-to-all-start.1 = ((bf16[64,8,640]{2,1,0:T(8,128)(2,1)}), bf16[64,8,640]{2,1,0:T(8,128)(2,1)}, u32[]{:S(2)}, u32[]{:S(2)}) async-start(bf16[64,8,640]{2,1,0:T(8,128)(2,1)} %bitcast.16), calls=%async_computation.1 | async-start | bytes 1310720 | tf_op jit(solution)/shard_map/all_to_all | solution.py:271
  104.1 0.0 collective-permute-done.3.refs_5_
  104.1 5.3 %collective-permute-start.7 = (bf16[4,16,32,128]{3,2,1,0:T(8,128)(2,1)}, bf16[4,16,32,128]{3,2,1,0:T(8,128)(2,1)}, u32[]{:S(2)}, u32[]{:S(2)}) collective-permute-start(bf16[4,16,32,128]{3,2,1,0:T(8,128)(2,1)} %collective-permute-done.3.refs_5_), channel_id=1, source_target_pairs={{0,12},{4,0},{8,4},{12,8},{16,28},{20,16},{24,20},{28,24},{32,44},... | collective-permute-start | bytes 1572872 | tf_op jit(solution)/shard_map/ppermute | solution.py:334
  109.4 1.9 %collective-permute-start.6 = (bf16[4,16,32,128]{3,2,1,0:T(8,128)(2,1)}, bf16[4,16,32,128]{3,2,1,0:T(8,128)(2,1)}, u32[]{:S(2)}, u32[]{:S(2)}) collective-permute-start(bf16[4,16,32,128]{3,2,1,0:T(8,128)(2,1)} %collective-permute-done.3.refs_5_), channel_id=1, source_target_pairs={{0,4},{4,8},{8,12},{12,0},{16,20},{20,24},{24,28},{28,16},{32,36},... | collective-permute-start | bytes 1572872 | tf_op jit(solution)/shard_map/ppermute | solution.py:333
  111.3 0.0 copy-done
  111.3 5.5 %row_attend.1 = (bf16[512,512]{1,0:T(8,128)(2,1)S(1)}, bf16[512,128]{1,0:T(8,128)(2,1)S(1)}) custom-call(s32[1]{0:T(128)} %bitcast.3.parity_ref, bf16[512,512]{1,0:T(8,128)(2,1)S(1)} %copy-done, bf16[512,512]{1,0:T(8,128)(2,1)} %k_ref.1, bf16[512,512]{1,0:T(8,128)(2,1)} %v_ref.1, bf16[512,512]{1,0:T(8,128)(2,1)} %collective-permute-done.1.kp_ref, ...), custom_call_target="tpu_custom_call" | custom-call | flops 199999995904 | bytes 1024 | tf_op jit(solution)/shard_map/row_attend/pallas_call | solution.py:112
  116.9 8.2 %all-to-all-done.1 = bf16[64,8,640]{2,1,0:T(8,128)(2,1)} async-done(((bf16[64,8,640]{2,1,0:T(8,128)(2,1)}), bf16[64,8,640]{2,1,0:T(8,128)(2,1)}, u32[]{:S(2)}, u32[]{:S(2)}) %all-to-all-start.1) | async-done | bytes 655392 | tf_op jit(solution)/shard_map/all_to_all | solution.py:271
  125.1 2.0 %mix.1.refs_0_ = bf16[512,512]{1,0:T(8,128)(2,1)S(1)} custom-call(bf16[512,512]{1,0:T(8,128)(2,1)S(1)} %get-tuple-element.29.row_ref, bf16[512,128]{1,0:T(8,128)(2,1)S(1)} %get-tuple-element.30.row_stat_ref, bf16[512,640]{1,0:T(8,128)(2,1)} %bitcast.17.col_ref), custom_call_target="tpu_custom_call" | custom-call | flops 1024 | bytes 1024 | tf_op jit(solution)/shard_map/mix/pallas_call | solution.py:202
  127.1 2.7 %collective-permute-start.8 = (bf16[512,512]{1,0:T(8,128)(2,1)S(1)}, bf16[512,512]{1,0:T(8,128)(2,1)S(1)}, u32[]{:S(2)}, u32[]{:S(2)}) collective-permute-start(bf16[512,512]{1,0:T(8,128)(2,1)S(1)} %mix.1.refs_0_), channel_id=1, source_target_pairs={{0,2},{1,3},{2,0},{3,1},{4,6},{5,7},{6,4},{7,5},{8,10},{9,11},{10,... | collective-permute-start | bytes 1572872 | tf_op jit(solution)/shard_map/ppermute | solution.py:340
  129.8 0.0 collective-permute-done.5.refs_6_
  129.8 0.0 collective-permute-done.4.refs_10_
  129.9 0.0 collective-permute-done.7.refs_7_
  129.9 0.0 collective-permute-done.6.refs_11_
  129.9 1.9 %collective-permute-start.12 = (bf16[4,16,32,128]{3,2,1,0:T(8,128)(2,1)}, bf16[4,16,32,128]{3,2,1,0:T(8,128)(2,1)S(1)}, u32[]{:S(2)}, u32[]{:S(2)}) collective-permute-start(bf16[4,16,32,128]{3,2,1,0:T(8,128)(2,1)} %collective-permute-done.7.refs_7_), channel_id=1, source_target_pairs={{0,12},{4,0},{8,4},{12,8},{16,28},{20,16},{24,20},{28,24},{32,44},... | collective-permute-start | bytes 1572872 | tf_op jit(solution)/shard_map/ppermute | solution.py:343
  131.8 3.4 %collective-permute-start.11 = (bf16[4,16,32,128]{3,2,1,0:T(8,128)(2,1)}, bf16[4,16,32,128]{3,2,1,0:T(8,128)(2,1)S(1)}, u32[]{:S(2)}, u32[]{:S(2)}) collective-permute-start(bf16[4,16,32,128]{3,2,1,0:T(8,128)(2,1)} %collective-permute-done.4.refs_10_), channel_id=1, source_target_pairs={{0,4},{4,8},{8,12},{12,0},{16,20},{20,24},{24,28},{28,16},{32,36},... | collective-permute-start | bytes 1572872 | tf_op jit(solution)/shard_map/ppermute | solution.py:342
  135.2 2.8 %collective-permute-done.8.refs_2_ = bf16[512,512]{1,0:T(8,128)(2,1)S(1)} collective-permute-done((bf16[512,512]{1,0:T(8,128)(2,1)S(1)}, bf16[512,512]{1,0:T(8,128)(2,1)S(1)}, u32[]{:S(2)}, u32[]{:S(2)}) %collective-permute-start.8) | collective-permute-done | bytes 524320 | tf_op jit(solution)/shard_map/ppermute | solution.py:340
  138.0 7.2 %collective-permute-start.9 = (bf16[512,512]{1,0:T(8,128)(2,1)S(1)}, bf16[512,512]{1,0:T(8,128)(2,1)S(1)}, u32[]{:S(2)}, u32[]{:S(2)}) collective-permute-start(bf16[512,512]{1,0:T(8,128)(2,1)S(1)} %mix.1.refs_0_), channel_id=1, source_target_pairs={{0,1},{1,0},{2,3},{3,2},{4,5},{5,4},{6,7},{7,6},{8,9},{9,8},{10,11... | collective-permute-start | bytes 1572872 | tf_op jit(solution)/shard_map/ppermute | solution.py:345
  145.2 1.9 %collective-permute-start.10 = (bf16[512,512]{1,0:T(8,128)(2,1)S(1)}, bf16[512,512]{1,0:T(8,128)(2,1)S(1)}, u32[]{:S(2)}, u32[]{:S(2)}) collective-permute-start(bf16[512,512]{1,0:T(8,128)(2,1)S(1)} %collective-permute-done.8.refs_2_), channel_id=1, source_target_pairs={{0,1},{1,0},{2,3},{3,2},{4,5},{5,4},{6,7},{7,6},{8,9},{9,8},{10,11... | collective-permute-start | bytes 1572872 | tf_op jit(solution)/shard_map/ppermute | solution.py:346
  147.2 0.1 pad_add_fusion.place_ref
  147.3 0.0 collective-permute-done.12.refs_9_
  147.3 0.0 collective-permute-done.11.refs_8_
  147.3 0.0 collective-permute-done.9.refs_1_
  147.3 1.7 %collective-permute-done.10.refs_3_ = bf16[512,512]{1,0:T(8,128)(2,1)S(1)} collective-permute-done((bf16[512,512]{1,0:T(8,128)(2,1)S(1)}, bf16[512,512]{1,0:T(8,128)(2,1)S(1)}, u32[]{:S(2)}, u32[]{:S(2)}) %collective-permute-start.10) | collective-permute-done | bytes 524320 | tf_op jit(solution)/shard_map/ppermute | solution.py:346
  149.0 5.7 %finish.1 = bf16[512,1024]{1,0:T(8,128)(2,1)} custom-call(s32[3]{0:T(128)S(1)} %pad_add_fusion.place_ref, bf16[512,512]{1,0:T(8,128)(2,1)S(1)} %mix.1.refs_0_, bf16[512,512]{1,0:T(8,128)(2,1)S(1)} %collective-permute-done.9.refs_1_, bf16[512,512]{1,0:T(8,128)(2,1)S(1)} %collective-permute-done.8.refs_2_, ...), custom_call_target="tpu_custom_call" | custom-call | flops 1024 | bytes 1024 | tf_op jit(solution)/shard_map/finish/pallas_call | solution.py:252
  (4 shorter events, 0.1 us)
Async XLA Ops:
  0.0 9.0 %collective-permute-start = (bf16[32,512]{1,0:T(8,128)(2,1)}, bf16[32,512]{1,0:T(8,128)(2,1)S(1)}, u32[]{:S(2)}, u32[]{:S(2)}) collective-permute-start(bf16[32,512]{1,0:T(8,128)(2,1)} %bitcast.26), channel_id=1, source_target_pairs={{0,0},{1,128},{2,256},{3,384},{4,4},{5,132},{6,260},{7,388},{8,8},... | collective-permute-start | bytes 98312 | tf_op jit(solution)/shard_map/ppermute | solution.py:290
  9.1 1.3 copy-start.1
  10.5 70.9 %all-to-all-start = ((bf16[64,8,2048]{2,1,0:T(8,128)(2,1)}), bf16[64,8,2048]{2,1,0:T(8,128)(2,1)S(1)}, u32[]{:S(2)}, u32[]{:S(2)}) async-start(bf16[64,8,2048]{2,1,0:T(8,128)(2,1)} %bitcast.24), calls=%async_computation | async-start | bytes 4194304 | tf_op jit(solution)/shard_map/all_to_all | solution.py:271
  28.9 58.3 %collective-permute-start.1 = (bf16[512,512]{1,0:T(8,128)(2,1)}, bf16[512,512]{1,0:T(8,128)(2,1)}, u32[]{:S(2)}, u32[]{:S(2)}) collective-permute-start(bf16[512,512]{1,0:T(8,128)(2,1)} %k_ref.1), channel_id=1, source_target_pairs={{0,4},{8,12},{16,20},{24,28},{32,36},{40,44},{48,52},{56,60},{64,6... | collective-permute-start | bytes 1572872 | tf_op jit(solution)/shard_map/ppermute | solution.py:317
  31.9 55.3 %collective-permute-start.2 = (bf16[512,512]{1,0:T(8,128)(2,1)}, bf16[512,512]{1,0:T(8,128)(2,1)}, u32[]{:S(2)}, u32[]{:S(2)}) collective-permute-start(bf16[512,512]{1,0:T(8,128)(2,1)} %v_ref.1), channel_id=1, source_target_pairs={{0,4},{8,12},{16,20},{24,28},{32,36},{40,44},{48,52},{56,60},{64,6... | collective-permute-start | bytes 1572872 | tf_op jit(solution)/shard_map/ppermute | solution.py:318
  82.2 21.9 %collective-permute-start.3 = (bf16[4,16,32,128]{3,2,1,0:T(8,128)(2,1)}, bf16[4,16,32,128]{3,2,1,0:T(8,128)(2,1)}, u32[]{:S(2)}, u32[]{:S(2)}) collective-permute-start(bf16[4,16,32,128]{3,2,1,0:T(8,128)(2,1)} %bitcast.13.refs_4_), channel_id=1, source_target_pairs={{0,16},{4,20},{8,24},{12,28},{16,0},{20,4},{24,8},{28,12},{32,48},... | collective-permute-start | bytes 1572872 | tf_op jit(solution)/shard_map/ppermute | solution.py:321
  84.2 27.2 %copy-start = (bf16[512,512]{1,0:T(8,128)(2,1)S(1)}, bf16[512,512]{1,0:T(8,128)(2,1)}, u32[]{:S(2)}) copy-start(bf16[512,512]{1,0:T(8,128)(2,1)} %q_ref.1) | copy-start | bytes 1572868
  87.3 42.6 %collective-permute-start.5 = (bf16[4,16,32,128]{3,2,1,0:T(8,128)(2,1)}, bf16[4,16,32,128]{3,2,1,0:T(8,128)(2,1)}, u32[]{:S(2)}, u32[]{:S(2)}) collective-permute-start(bf16[4,16,32,128]{3,2,1,0:T(8,128)(2,1)} %bitcast.13.refs_4_), channel_id=1, source_target_pairs={{0,12},{4,0},{8,4},{12,8},{16,28},{20,16},{24,20},{28,24},{32,44},... | collective-permute-start | bytes 1572872 | tf_op jit(solution)/shard_map/ppermute | solution.py:329
  89.2 40.7 %collective-permute-start.4 = (bf16[4,16,32,128]{3,2,1,0:T(8,128)(2,1)}, bf16[4,16,32,128]{3,2,1,0:T(8,128)(2,1)}, u32[]{:S(2)}, u32[]{:S(2)}) collective-permute-start(bf16[4,16,32,128]{3,2,1,0:T(8,128)(2,1)} %bitcast.13.refs_4_), channel_id=1, source_target_pairs={{0,4},{4,8},{8,12},{12,0},{16,20},{20,24},{24,28},{28,16},{32,36},... | collective-permute-start | bytes 1572872 | tf_op jit(solution)/shard_map/ppermute | solution.py:328
  92.6 32.5 %all-to-all-start.1 = ((bf16[64,8,640]{2,1,0:T(8,128)(2,1)}), bf16[64,8,640]{2,1,0:T(8,128)(2,1)}, u32[]{:S(2)}, u32[]{:S(2)}) async-start(bf16[64,8,640]{2,1,0:T(8,128)(2,1)} %bitcast.16), calls=%async_computation.1 | async-start | bytes 1310720 | tf_op jit(solution)/shard_map/all_to_all | solution.py:271
  104.1 25.8 %collective-permute-start.7 = (bf16[4,16,32,128]{3,2,1,0:T(8,128)(2,1)}, bf16[4,16,32,128]{3,2,1,0:T(8,128)(2,1)}, u32[]{:S(2)}, u32[]{:S(2)}) collective-permute-start(bf16[4,16,32,128]{3,2,1,0:T(8,128)(2,1)} %collective-permute-done.3.refs_5_), channel_id=1, source_target_pairs={{0,12},{4,0},{8,4},{12,8},{16,28},{20,16},{24,20},{28,24},{32,44},... | collective-permute-start | bytes 1572872 | tf_op jit(solution)/shard_map/ppermute | solution.py:334
  109.4 20.5 %collective-permute-start.6 = (bf16[4,16,32,128]{3,2,1,0:T(8,128)(2,1)}, bf16[4,16,32,128]{3,2,1,0:T(8,128)(2,1)}, u32[]{:S(2)}, u32[]{:S(2)}) collective-permute-start(bf16[4,16,32,128]{3,2,1,0:T(8,128)(2,1)} %collective-permute-done.3.refs_5_), channel_id=1, source_target_pairs={{0,4},{4,8},{8,12},{12,0},{16,20},{20,24},{24,28},{28,16},{32,36},... | collective-permute-start | bytes 1572872 | tf_op jit(solution)/shard_map/ppermute | solution.py:333
  127.1 10.9 %collective-permute-start.8 = (bf16[512,512]{1,0:T(8,128)(2,1)S(1)}, bf16[512,512]{1,0:T(8,128)(2,1)S(1)}, u32[]{:S(2)}, u32[]{:S(2)}) collective-permute-start(bf16[512,512]{1,0:T(8,128)(2,1)S(1)} %mix.1.refs_0_), channel_id=1, source_target_pairs={{0,2},{1,3},{2,0},{3,1},{4,6},{5,7},{6,4},{7,5},{8,10},{9,11},{10,... | collective-permute-start | bytes 1572872 | tf_op jit(solution)/shard_map/ppermute | solution.py:340
  129.9 17.4 %collective-permute-start.12 = (bf16[4,16,32,128]{3,2,1,0:T(8,128)(2,1)}, bf16[4,16,32,128]{3,2,1,0:T(8,128)(2,1)S(1)}, u32[]{:S(2)}, u32[]{:S(2)}) collective-permute-start(bf16[4,16,32,128]{3,2,1,0:T(8,128)(2,1)} %collective-permute-done.7.refs_7_), channel_id=1, source_target_pairs={{0,12},{4,0},{8,4},{12,8},{16,28},{20,16},{24,20},{28,24},{32,44},... | collective-permute-start | bytes 1572872 | tf_op jit(solution)/shard_map/ppermute | solution.py:343
  131.8 15.5 %collective-permute-start.11 = (bf16[4,16,32,128]{3,2,1,0:T(8,128)(2,1)}, bf16[4,16,32,128]{3,2,1,0:T(8,128)(2,1)S(1)}, u32[]{:S(2)}, u32[]{:S(2)}) collective-permute-start(bf16[4,16,32,128]{3,2,1,0:T(8,128)(2,1)} %collective-permute-done.4.refs_10_), channel_id=1, source_target_pairs={{0,4},{4,8},{8,12},{12,0},{16,20},{20,24},{24,28},{28,16},{32,36},... | collective-permute-start | bytes 1572872 | tf_op jit(solution)/shard_map/ppermute | solution.py:342
  138.0 9.3 %collective-permute-start.9 = (bf16[512,512]{1,0:T(8,128)(2,1)S(1)}, bf16[512,512]{1,0:T(8,128)(2,1)S(1)}, u32[]{:S(2)}, u32[]{:S(2)}) collective-permute-start(bf16[512,512]{1,0:T(8,128)(2,1)S(1)} %mix.1.refs_0_), channel_id=1, source_target_pairs={{0,1},{1,0},{2,3},{3,2},{4,5},{5,4},{6,7},{7,6},{8,9},{9,8},{10,11... | collective-permute-start | bytes 1572872 | tf_op jit(solution)/shard_map/ppermute | solution.py:345
  145.2 3.8 %collective-permute-start.10 = (bf16[512,512]{1,0:T(8,128)(2,1)S(1)}, bf16[512,512]{1,0:T(8,128)(2,1)S(1)}, u32[]{:S(2)}, u32[]{:S(2)}) collective-permute-start(bf16[512,512]{1,0:T(8,128)(2,1)S(1)} %collective-permute-done.8.refs_2_), channel_id=1, source_target_pairs={{0,1},{1,0},{2,3},{3,2},{4,5},{5,4},{6,7},{7,6},{8,9},{9,8},{10,11... | collective-permute-start | bytes 1572872 | tf_op jit(solution)/shard_map/ppermute | solution.py:346

commit v5 on v4

--- a/solution.py
+++ b/solution.py
@@ -211,56 +211,79 @@
 
 
 CHUNKS = 4
+EARLY = ((0, 0), (0, 1), (1, 0), (1, 1), (3, 0), (3, 1))
+LATE = ((2, 0), (2, 1))
+
+
+def put_pieces(place_ref, pieces, origins, weight_ref, places):
+    y, x, mp = place_ref[0], place_ref[1], place_ref[2]
+    for (step, other), piece in zip(origins, pieces):
+        there = (x + step) & 3
+        lane = pl.multiple_of((2 * ((y + other) & 1) + there // 2) * DH, DH)
+        for i in places:
+            start = pl.multiple_of(i * 64 + (there & 1) * 32, 32)
+            for group in range(N_MP):
+                weight_ref[group ^ mp, pl.ds(start, 32), pl.ds(lane, DH)] = piece[group, i]
+
+
+def arrange_kernel(place_ref, *refs):
+    put_pieces(place_ref, refs[:-1], EARLY, refs[-1], range(16))
+
+
+def arrange(place, pieces):
+    vmem = pl.BlockSpec(memory_space=pltpu.VMEM)
+    return pl.pallas_call(
+        arrange_kernel,
+        out_shape=jax.ShapeDtypeStruct((N_MP, PLANE * 32, WIDTH), jnp.bfloat16),
+        in_specs=[pl.BlockSpec(memory_space=pltpu.SMEM)] + [vmem] * len(pieces),
+        out_specs=vmem,
+        compiler_params=pltpu.CompilerParams(vmem_limit_bytes=VMEM),
+        cost_estimate=SMALL,
+        name="arrange",
+    )(place, *pieces)
 
 
 def finish_kernel(place_ref, *refs):
-    blocks, pieces, out_ref = refs[:N_MP], refs[N_MP : N_MP + 8], refs[N_MP + 8]
-    weights, results = refs[N_MP + 9 : N_MP + 9 + CHUNKS], refs[N_MP + 9 + CHUNKS : -1]
-    done = refs[-1]
-    y, x, mp = place_ref[0], place_ref[1], place_ref[2]
-    spots = []
-    for i, piece in enumerate(pieces):
-        there = (x + i // 2) & 3
-        head = 2 * ((y + i % 2) & 1) + there // 2
-        spots.append((piece, (there & 1) * 32, pl.multiple_of(head * DH, DH)))
-
+    blocks, pieces = refs[:N_MP], refs[N_MP : N_MP + 2]
+    out_ref, weight_ref, *results, done = refs[N_MP + 3 :]
     copies = []
     width = PLANE * 32 // CHUNKS
     for chunk in range(CHUNKS):
-        for i in range(16 // CHUNKS):
-            for piece, row, lane in spots:
-                start = pl.multiple_of(i * 64 + row, 32)
-                for group in range(N_MP):
-                    weights[chunk][group, pl.ds(start, 32), pl.ds(lane, DH)] = piece[
-                        group, chunk * (16 // CHUNKS) + i
-                    ]
+        here = slice(chunk * width, (chunk + 1) * width)
+        part = 16 // CHUNKS
+        put_pieces(place_ref, pieces, LATE, weight_ref, range(chunk * part, (chunk + 1) * part))
         total = None
         for j in range(N_MP):
-            term = nt_dot(blocks[j][...], weights[chunk][mp ^ j])
+            term = nt_dot(blocks[j][...], weight_ref[j, here, :])
             total = term if total is None else total + term
         results[chunk][...] = total.astype(jnp.bfloat16)
-        there = out_ref.at[:, chunk * width : (chunk + 1) * width]
-        copies.append(pltpu.make_async_copy(results[chunk], there, done.at[chunk]))
+        copies.append(
+            pltpu.make_async_copy(results[chunk], out_ref.at[:, here], done.at[chunk])
+        )
         copies[-1].start()
     for copy in copies:
         copy.wait()
 
 
-def finish(place, blocks, pieces):
+def finish(place, blocks, pieces, weight):
     vmem = pl.BlockSpec(memory_space=pltpu.VMEM)
     width = PLANE * 32 // CHUNKS
+    inputs = (*blocks, *pieces, weight)
     return pl.pallas_call(
         finish_kernel,
-        out_shape=jax.ShapeDtypeStruct((ROWS, PLANE * 32), jnp.bfloat16),
-        in_specs=[pl.BlockSpec(memory_space=pltpu.SMEM)] + [vmem] * (len(blocks) + len(pieces)),
-        out_specs=pl.BlockSpec(memory_space=pl.ANY),
-        scratch_shapes=[pltpu.VMEM((N_MP, width, WIDTH), jnp.bfloat16)] * CHUNKS
-        + [pltpu.VMEM((ROWS, width), jnp.bfloat16)] * CHUNKS
+        out_shape=(
+            jax.ShapeDtypeStruct((ROWS, PLANE * 32), jnp.bfloat16),
+            jax.ShapeDtypeStruct(weight.shape, weight.dtype),
+        ),
+        in_specs=[pl.BlockSpec(memory_space=pltpu.SMEM)] + [vmem] * len(inputs),
+        out_specs=(pl.BlockSpec(memory_space=pl.ANY), vmem),
+        input_output_aliases={len(inputs): 1},
+        scratch_shapes=[pltpu.VMEM((ROWS, width), jnp.bfloat16)] * CHUNKS
         + [pltpu.SemaphoreType.DMA((CHUNKS,))],
         compiler_params=pltpu.CompilerParams(vmem_limit_bytes=VMEM),
         cost_estimate=SMALL,
         name="finish",
-    )(place, *blocks, *pieces)
+    )(place, *inputs)[0]
 
 
 def same_parity():
@@ -341,12 +364,12 @@
     after, less_0, more_0, less_1, more_1 = barrier((attended, less_0, more_0, less_1, more_1))
     far_0 = lax.ppermute(less_0, "seq", x_up)
     far_1 = lax.ppermute(more_1, "seq", x_down)
-    after, across = barrier((after, across))
+    place = jnp.stack([seq // 4 % 8, seq % 4, mp]).astype(jnp.int32)
+    weight = arrange(place, (own_0, own_1, more_0, more_1, less_0, less_1))
+    after, weight = barrier((after, weight))
     beside = lax.ppermute(after, "mp", near)
     last = lax.ppermute(across, "mp", near)
-    place = jnp.stack([seq // 4 % 8, seq % 4, mp]).astype(jnp.int32)
-    pieces = (own_0, own_1, more_0, more_1, far_0, far_1, less_0, less_1)
-    return finish(place, (after, beside, across, last), pieces)
+    return finish(place, (after, beside, across, last), (far_0, far_1), weight)
 
 
 def solution(mesh):

time: 156 us -> 154 us (0.987)
  waiting for transfers between devices: 60.1 us -> 57.4 us
    ppermute x1, waiting for transfers between devices: 2.76 us -> 0.01 us  [body(): across = lax.ppermute(attended, 'mp', far)]
    pallas_call x1 -> x2, Pallas kernels: 5.73 us -> 6.5 us  [the longest x1 3.85 us: finish(): pl.pallas_call(finish_kernel, out_shape=(jax.ShapeDtypeStruct((ROWS, PLAN...]
  transfers between devices with their start and end apart: 15 -> 15, of which waited for: 4 -> 3; matrix products, arithmetic and copies ran while one was open for 2% -> 2% of each run, Pallas kernels for 7% -> 9%
where the time goes in v5:
time: 154 us; the launch traced here: 153 us
  starting transfers between devices  73.8 us (48%)
  waiting for transfers between devices  57.4 us (37%)
  Pallas kernels  17.2 us (11%)
  local copies, waits for them, and re-layouts  2.29 us (1%)
  other arithmetic  1.85 us (1%)
    all_to_all x2, waiting for transfers between devices, swap_columns(): lax.all_to_all(value, 'seq', split_axis=0, concat_axis=0, axis_index_grou...  55.5 us
    all_to_all x2, starting transfers between devices, swap_columns(): lax.all_to_all(value, 'seq', split_axis=0, concat_axis=0, axis_index_grou...  29.9 us
    ppermute x1, starting transfers between devices, turn(): return lax.ppermute(mine, ('seq', 'mp'), pairs)  7.19 us
    ppermute x1, starting transfers between devices, body(): beside = lax.ppermute(after, 'mp', near)  7.17 us
    pallas_call x1, Pallas kernels, row_attend(): pl.pallas_call(row_kernel, out_shape=(jax.ShapeDtypeStruct((ROWS, WIDTH),...  5.52 us
    ppermute x1, starting transfers between devices, body(): more_1 = lax.ppermute(own_1, 'seq', x_down)  5.3 us
    pallas_call x1, Pallas kernels, finish(): pl.pallas_call(finish_kernel, out_shape=(jax.ShapeDtypeStruct((ROWS, PLAN...  3.85 us
    ppermute x1, starting transfers between devices, body(): far_0 = lax.ppermute(less_0, 'seq', x_up)  3.44 us
  transfers between devices with their start and end apart: 15, of which 3 were waited for; matrix products, arithmetic and copies ran while one was open for 2% of the time, Pallas kernels for 9%

profile of v5, /device:TPU:1, one launch (start us, length us, event | category | flops | bytes accessed | tf_op | source)
XLA Modules:
  0.0 152.8 jit_solution(6408387400084929792)
XLA Ops:
  0.0 7.2 %collective-permute-start = (bf16[32,512]{1,0:T(8,128)(2,1)}, bf16[32,512]{1,0:T(8,128)(2,1)S(1)}, u32[]{:S(2)}, u32[]{:S(2)}) collective-permute-start(bf16[32,512]{1,0:T(8,128)(2,1)} %bitcast.26), channel_id=1, source_target_pairs={{0,0},{1,128},{2,256},{3,384},{4,4},{5,132},{6,260},{7,388},{8,8},... | collective-permute-start | bytes 98312 | tf_op jit(solution)/shard_map/ppermute | solution.py:313
  7.2 1.8 %maximum_maximum_fusion = bf16[512,2048]{1,0:T(8,128)(2,1)S(1)} fusion(bf16[512,512]{1,0:T(8,128)(2,1)} %v_ref.1, bf16[512,512]{1,0:T(8,128)(2,1)} %k_ref.1, bf16[512,512]{1,0:T(8,128)(2,1)} %q_ref.1, bf16[2048]{0:T(1024)(128)(2,1)S(1)} %pad.3.clone), kind=kLoop, calls=%fused_computation | loop fusion | flops 8388608 | bytes 3674112 | tf_op jit(solution)/shard_map/concatenate | solution.py:334
  9.0 0.0 collective-permute-done
  9.1 0.1 constant_dynamic-update-slice_fusion
  9.1 0.0 copy-start.1
  9.1 1.3 copy-done.1
  10.5 18.4 %all-to-all-start = ((bf16[64,8,2048]{2,1,0:T(8,128)(2,1)}), bf16[64,8,2048]{2,1,0:T(8,128)(2,1)S(1)}, u32[]{:S(2)}, u32[]{:S(2)}) async-start(bf16[64,8,2048]{2,1,0:T(8,128)(2,1)} %bitcast.24), calls=%async_computation | async-start | bytes 4194304 | tf_op jit(solution)/shard_map/all_to_all | solution.py:294
  28.9 3.0 %collective-permute-start.1 = (bf16[512,512]{1,0:T(8,128)(2,1)}, bf16[512,512]{1,0:T(8,128)(2,1)}, u32[]{:S(2)}, u32[]{:S(2)}) collective-permute-start(bf16[512,512]{1,0:T(8,128)(2,1)} %k_ref.1), channel_id=1, source_target_pairs={{0,4},{8,12},{16,20},{24,28},{32,36},{40,44},{48,52},{56,60},{64,6... | collective-permute-start | bytes 1572872 | tf_op jit(solution)/shard_map/ppermute | solution.py:340
  31.9 2.1 %collective-permute-start.2 = (bf16[512,512]{1,0:T(8,128)(2,1)}, bf16[512,512]{1,0:T(8,128)(2,1)}, u32[]{:S(2)}, u32[]{:S(2)}) collective-permute-start(bf16[512,512]{1,0:T(8,128)(2,1)} %v_ref.1), channel_id=1, source_target_pairs={{0,4},{8,12},{16,20},{24,28},{32,36},{40,44},{48,52},{56,60},{64,6... | collective-permute-start | bytes 1572872 | tf_op jit(solution)/shard_map/ppermute | solution.py:341
  34.0 47.3 %all-to-all-done = bf16[64,8,2048]{2,1,0:T(8,128)(2,1)S(1)} async-done(((bf16[64,8,2048]{2,1,0:T(8,128)(2,1)}), bf16[64,8,2048]{2,1,0:T(8,128)(2,1)S(1)}, u32[]{:S(2)}, u32[]{:S(2)}) %all-to-all-start) | async-done | bytes 2097184 | tf_op jit(solution)/shard_map/all_to_all | solution.py:294
  81.4 0.8 slice.4
  82.2 1.9 %collective-permute-start.3 = (bf16[4,16,32,128]{3,2,1,0:T(8,128)(2,1)}, bf16[4,16,32,128]{3,2,1,0:T(8,128)(2,1)}, u32[]{:S(2)}, u32[]{:S(2)}) collective-permute-start(bf16[4,16,32,128]{3,2,1,0:T(8,128)(2,1)} %bitcast.13.refs_0_), channel_id=1, source_target_pairs={{0,16},{4,20},{8,24},{12,28},{16,0},{20,4},{24,8},{28,12},{32,48},... | collective-permute-start | bytes 1572872 | tf_op jit(solution)/shard_map/ppermute | solution.py:344
  84.1 0.0 copy-start
  84.1 3.1 %col_attend.1 = bf16[512,640]{1,0:T(8,128)(2,1)} custom-call(bf16[512,2048]{1,0:T(8,128)(2,1)S(1)} %bitcast.23), custom_call_target="tpu_custom_call" | custom-call | flops 199999995904 | bytes 1024 | tf_op jit(solution)/shard_map/col_attend/pallas_call | solution.py:174
  87.2 0.0 collective-permute-done.1.kp_ref
  87.2 0.0 collective-permute-done.2.vp_ref
  87.2 1.9 %collective-permute-start.5 = (bf16[4,16,32,128]{3,2,1,0:T(8,128)(2,1)}, bf16[4,16,32,128]{3,2,1,0:T(8,128)(2,1)}, u32[]{:S(2)}, u32[]{:S(2)}) collective-permute-start(bf16[4,16,32,128]{3,2,1,0:T(8,128)(2,1)} %bitcast.13.refs_0_), channel_id=1, source_target_pairs={{0,12},{4,0},{8,4},{12,8},{16,28},{20,16},{24,20},{28,24},{32,44},... | collective-permute-start | bytes 1572872 | tf_op jit(solution)/shard_map/ppermute | solution.py:352
  89.2 3.4 %collective-permute-start.4 = (bf16[4,16,32,128]{3,2,1,0:T(8,128)(2,1)}, bf16[4,16,32,128]{3,2,1,0:T(8,128)(2,1)}, u32[]{:S(2)}, u32[]{:S(2)}) collective-permute-start(bf16[4,16,32,128]{3,2,1,0:T(8,128)(2,1)} %bitcast.13.refs_0_), channel_id=1, source_target_pairs={{0,4},{4,8},{8,12},{12,0},{16,20},{20,24},{24,28},{28,16},{32,36},... | collective-permute-start | bytes 1572872 | tf_op jit(solution)/shard_map/ppermute | solution.py:351
  92.5 11.5 %all-to-all-start.1 = ((bf16[64,8,640]{2,1,0:T(8,128)(2,1)}), bf16[64,8,640]{2,1,0:T(8,128)(2,1)}, u32[]{:S(2)}, u32[]{:S(2)}) async-start(bf16[64,8,640]{2,1,0:T(8,128)(2,1)} %bitcast.16), calls=%async_computation.1 | async-start | bytes 1310720 | tf_op jit(solution)/shard_map/all_to_all | solution.py:294
  104.1 0.0 collective-permute-done.3.refs_1_
  104.1 5.3 %collective-permute-start.7 = (bf16[4,16,32,128]{3,2,1,0:T(8,128)(2,1)}, bf16[4,16,32,128]{3,2,1,0:T(8,128)(2,1)}, u32[]{:S(2)}, u32[]{:S(2)}) collective-permute-start(bf16[4,16,32,128]{3,2,1,0:T(8,128)(2,1)} %collective-permute-done.3.refs_1_), channel_id=1, source_target_pairs={{0,12},{4,0},{8,4},{12,8},{16,28},{20,16},{24,20},{28,24},{32,44},... | collective-permute-start | bytes 1572872 | tf_op jit(solution)/shard_map/ppermute | solution.py:357
  109.4 1.9 %collective-permute-start.6 = (bf16[4,16,32,128]{3,2,1,0:T(8,128)(2,1)}, bf16[4,16,32,128]{3,2,1,0:T(8,128)(2,1)}, u32[]{:S(2)}, u32[]{:S(2)}) collective-permute-start(bf16[4,16,32,128]{3,2,1,0:T(8,128)(2,1)} %collective-permute-done.3.refs_1_), channel_id=1, source_target_pairs={{0,4},{4,8},{8,12},{12,0},{16,20},{20,24},{24,28},{28,16},{32,36},... | collective-permute-start | bytes 1572872 | tf_op jit(solution)/shard_map/ppermute | solution.py:356
  111.3 0.0 copy-done
  111.3 5.5 %row_attend.1 = (bf16[512,512]{1,0:T(8,128)(2,1)S(1)}, bf16[512,128]{1,0:T(8,128)(2,1)S(1)}) custom-call(s32[1]{0:T(128)} %bitcast.3.parity_ref, bf16[512,512]{1,0:T(8,128)(2,1)S(1)} %copy-done, bf16[512,512]{1,0:T(8,128)(2,1)} %k_ref.1, bf16[512,512]{1,0:T(8,128)(2,1)} %v_ref.1, bf16[512,512]{1,0:T(8,128)(2,1)} %collective-permute-done.1.kp_ref, ...), custom_call_target="tpu_custom_call" | custom-call | flops 199999995904 | bytes 1024 | tf_op jit(solution)/shard_map/row_attend/pallas_call | solution.py:112
  116.8 8.2 %all-to-all-done.1 = bf16[64,8,640]{2,1,0:T(8,128)(2,1)} async-done(((bf16[64,8,640]{2,1,0:T(8,128)(2,1)}), bf16[64,8,640]{2,1,0:T(8,128)(2,1)}, u32[]{:S(2)}, u32[]{:S(2)}) %all-to-all-start.1) | async-done | bytes 655392 | tf_op jit(solution)/shard_map/all_to_all | solution.py:294
  125.0 2.0 %mix.1.refs_0_ = bf16[512,512]{1,0:T(8,128)(2,1)S(1)} custom-call(bf16[512,512]{1,0:T(8,128)(2,1)S(1)} %get-tuple-element.30.row_ref, bf16[512,128]{1,0:T(8,128)(2,1)S(1)} %get-tuple-element.31.row_stat_ref, bf16[512,640]{1,0:T(8,128)(2,1)} %bitcast.17.col_ref), custom_call_target="tpu_custom_call" | custom-call | flops 1024 | bytes 1024 | tf_op jit(solution)/shard_map/mix/pallas_call | solution.py:202
  127.1 2.7 %collective-permute-start.9 = (bf16[512,512]{1,0:T(8,128)(2,1)S(1)}, bf16[512,512]{1,0:T(8,128)(2,1)S(1)}, u32[]{:S(2)}, u32[]{:S(2)}) collective-permute-start(bf16[512,512]{1,0:T(8,128)(2,1)S(1)} %mix.1.refs_0_), channel_id=1, source_target_pairs={{0,2},{1,3},{2,0},{3,1},{4,6},{5,7},{6,4},{7,5},{8,10},{9,11},{10,... | collective-permute-start | bytes 1572872 | tf_op jit(solution)/shard_map/ppermute | solution.py:363
  129.9 0.1 pad_add_fusion.place_ref
  129.9 0.0 collective-permute-done.5.refs_2_
  129.9 0.0 collective-permute-done.4.refs_4_
  129.9 0.0 collective-permute-done.7.refs_3_
  129.9 0.0 collective-permute-done.6.refs_5_
  130.0 1.9 %collective-permute-start.12 = (bf16[4,16,32,128]{3,2,1,0:T(8,128)(2,1)}, bf16[4,16,32,128]{3,2,1,0:T(8,128)(2,1)S(1)}, u32[]{:S(2)}, u32[]{:S(2)}) collective-permute-start(bf16[4,16,32,128]{3,2,1,0:T(8,128)(2,1)} %collective-permute-done.7.refs_3_), channel_id=1, source_target_pairs={{0,12},{4,0},{8,4},{12,8},{16,28},{20,16},{24,20},{28,24},{32,44},... | collective-permute-start | bytes 1572872 | tf_op jit(solution)/shard_map/ppermute | solution.py:366
  131.9 3.4 %collective-permute-start.11 = (bf16[4,16,32,128]{3,2,1,0:T(8,128)(2,1)}, bf16[4,16,32,128]{3,2,1,0:T(8,128)(2,1)S(1)}, u32[]{:S(2)}, u32[]{:S(2)}) collective-permute-start(bf16[4,16,32,128]{3,2,1,0:T(8,128)(2,1)} %collective-permute-done.4.refs_4_), channel_id=1, source_target_pairs={{0,4},{4,8},{8,12},{12,0},{16,20},{20,24},{24,28},{28,16},{32,36},... | collective-permute-start | bytes 1572872 | tf_op jit(solution)/shard_map/ppermute | solution.py:365
  135.3 2.6 %arrange.1.refs_6_ = bf16[4,1024,512]{2,1,0:T(8,128)(2,1)S(1)} custom-call(s32[3]{0:T(128)S(1)} %pad_add_fusion.place_ref, bf16[4,16,32,128]{3,2,1,0:T(8,128)(2,1)} %bitcast.13.refs_0_, bf16[4,16,32,128]{3,2,1,0:T(8,128)(2,1)} %collective-permute-done.3.refs_1_, bf16[4,16,32,128]{3,2,1,0:T(8,128)(2,1)} %collective-permute-done.5.refs_2_, ...), custom_call_target="tpu_custom_call" | custom-call | flops 1024 | bytes 1024 | tf_op jit(solution)/shard_map/arrange/pallas_call | solution.py:235
  138.0 7.2 %collective-permute-start.8 = (bf16[512,512]{1,0:T(8,128)(2,1)S(1)}, bf16[512,512]{1,0:T(8,128)(2,1)S(1)}, u32[]{:S(2)}, u32[]{:S(2)}) collective-permute-start(bf16[512,512]{1,0:T(8,128)(2,1)S(1)} %mix.1.refs_0_), channel_id=1, source_target_pairs={{0,1},{1,0},{2,3},{3,2},{4,5},{5,4},{6,7},{7,6},{8,9},{9,8},{10,11... | collective-permute-start | bytes 1572872 | tf_op jit(solution)/shard_map/ppermute | solution.py:370
  145.2 0.0 collective-permute-done.9.refs_2_
  145.2 1.9 %collective-permute-start.10 = (bf16[512,512]{1,0:T(8,128)(2,1)S(1)}, bf16[512,512]{1,0:T(8,128)(2,1)S(1)}, u32[]{:S(2)}, u32[]{:S(2)}) collective-permute-start(bf16[512,512]{1,0:T(8,128)(2,1)S(1)} %collective-permute-done.9.refs_2_), channel_id=1, source_target_pairs={{0,1},{1,0},{2,3},{3,2},{4,5},{5,4},{6,7},{7,6},{8,9},{9,8},{10,11... | collective-permute-start | bytes 1572872 | tf_op jit(solution)/shard_map/ppermute | solution.py:371
  147.1 0.0 collective-permute-done.12.refs_5_
  147.1 0.0 collective-permute-done.11.refs_4_
  147.1 0.0 collective-permute-done.8.refs_1_
  147.1 1.8 %collective-permute-done.10.refs_3_ = bf16[512,512]{1,0:T(8,128)(2,1)S(1)} collective-permute-done((bf16[512,512]{1,0:T(8,128)(2,1)S(1)}, bf16[512,512]{1,0:T(8,128)(2,1)S(1)}, u32[]{:S(2)}, u32[]{:S(2)}) %collective-permute-start.10) | collective-permute-done | bytes 524320 | tf_op jit(solution)/shard_map/ppermute | solution.py:371
  149.0 3.9 %finish.1 = (bf16[512,1024]{1,0:T(8,128)(2,1)}, bf16[4,1024,512]{2,1,0:T(8,128)(2,1)S(1)}) custom-call(s32[3]{0:T(128)S(1)} %pad_add_fusion.place_ref, bf16[512,512]{1,0:T(8,128)(2,1)S(1)} %mix.1.refs_0_, bf16[512,512]{1,0:T(8,128)(2,1)S(1)} %collective-permute-done.8.refs_1_, ...), custom_call_target="tpu_custom_call", output_to_operand_aliasing={{1}: (7, {})} | custom-call | flops 1024 | bytes 1024 | tf_op jit(solution)/shard_map/finish/pallas_call | solution.py:272
  (4 shorter events, 0.1 us)
Async XLA Ops:
  0.0 9.0 %collective-permute-start = (bf16[32,512]{1,0:T(8,128)(2,1)}, bf16[32,512]{1,0:T(8,128)(2,1)S(1)}, u32[]{:S(2)}, u32[]{:S(2)}) collective-permute-start(bf16[32,512]{1,0:T(8,128)(2,1)} %bitcast.26), channel_id=1, source_target_pairs={{0,0},{1,128},{2,256},{3,384},{4,4},{5,132},{6,260},{7,388},{8,8},... | collective-permute-start | bytes 98312 | tf_op jit(solution)/shard_map/ppermute | solution.py:313
  9.1 1.3 copy-start.1
  10.5 70.9 %all-to-all-start = ((bf16[64,8,2048]{2,1,0:T(8,128)(2,1)}), bf16[64,8,2048]{2,1,0:T(8,128)(2,1)S(1)}, u32[]{:S(2)}, u32[]{:S(2)}) async-start(bf16[64,8,2048]{2,1,0:T(8,128)(2,1)} %bitcast.24), calls=%async_computation | async-start | bytes 4194304 | tf_op jit(solution)/shard_map/all_to_all | solution.py:294
  28.9 58.3 %collective-permute-start.1 = (bf16[512,512]{1,0:T(8,128)(2,1)}, bf16[512,512]{1,0:T(8,128)(2,1)}, u32[]{:S(2)}, u32[]{:S(2)}) collective-permute-start(bf16[512,512]{1,0:T(8,128)(2,1)} %k_ref.1), channel_id=1, source_target_pairs={{0,4},{8,12},{16,20},{24,28},{32,36},{40,44},{48,52},{56,60},{64,6... | collective-permute-start | bytes 1572872 | tf_op jit(solution)/shard_map/ppermute | solution.py:340
  31.9 55.3 %collective-permute-start.2 = (bf16[512,512]{1,0:T(8,128)(2,1)}, bf16[512,512]{1,0:T(8,128)(2,1)}, u32[]{:S(2)}, u32[]{:S(2)}) collective-permute-start(bf16[512,512]{1,0:T(8,128)(2,1)} %v_ref.1), channel_id=1, source_target_pairs={{0,4},{8,12},{16,20},{24,28},{32,36},{40,44},{48,52},{56,60},{64,6... | collective-permute-start | bytes 1572872 | tf_op jit(solution)/shard_map/ppermute | solution.py:341
  82.2 21.9 %collective-permute-start.3 = (bf16[4,16,32,128]{3,2,1,0:T(8,128)(2,1)}, bf16[4,16,32,128]{3,2,1,0:T(8,128)(2,1)}, u32[]{:S(2)}, u32[]{:S(2)}) collective-permute-start(bf16[4,16,32,128]{3,2,1,0:T(8,128)(2,1)} %bitcast.13.refs_0_), channel_id=1, source_target_pairs={{0,16},{4,20},{8,24},{12,28},{16,0},{20,4},{24,8},{28,12},{32,48},... | collective-permute-start | bytes 1572872 | tf_op jit(solution)/shard_map/ppermute | solution.py:344
  84.1 27.2 %copy-start = (bf16[512,512]{1,0:T(8,128)(2,1)S(1)}, bf16[512,512]{1,0:T(8,128)(2,1)}, u32[]{:S(2)}) copy-start(bf16[512,512]{1,0:T(8,128)(2,1)} %q_ref.1) | copy-start | bytes 1572868
  87.2 42.7 %collective-permute-start.5 = (bf16[4,16,32,128]{3,2,1,0:T(8,128)(2,1)}, bf16[4,16,32,128]{3,2,1,0:T(8,128)(2,1)}, u32[]{:S(2)}, u32[]{:S(2)}) collective-permute-start(bf16[4,16,32,128]{3,2,1,0:T(8,128)(2,1)} %bitcast.13.refs_0_), channel_id=1, source_target_pairs={{0,12},{4,0},{8,4},{12,8},{16,28},{20,16},{24,20},{28,24},{32,44},... | collective-permute-start | bytes 1572872 | tf_op jit(solution)/shard_map/ppermute | solution.py:352
  89.2 40.8 %collective-permute-start.4 = (bf16[4,16,32,128]{3,2,1,0:T(8,128)(2,1)}, bf16[4,16,32,128]{3,2,1,0:T(8,128)(2,1)}, u32[]{:S(2)}, u32[]{:S(2)}) collective-permute-start(bf16[4,16,32,128]{3,2,1,0:T(8,128)(2,1)} %bitcast.13.refs_0_), channel_id=1, source_target_pairs={{0,4},{4,8},{8,12},{12,0},{16,20},{20,24},{24,28},{28,16},{32,36},... | collective-permute-start | bytes 1572872 | tf_op jit(solution)/shard_map/ppermute | solution.py:351
  92.5 32.5 %all-to-all-start.1 = ((bf16[64,8,640]{2,1,0:T(8,128)(2,1)}), bf16[64,8,640]{2,1,0:T(8,128)(2,1)}, u32[]{:S(2)}, u32[]{:S(2)}) async-start(bf16[64,8,640]{2,1,0:T(8,128)(2,1)} %bitcast.16), calls=%async_computation.1 | async-start | bytes 1310720 | tf_op jit(solution)/shard_map/all_to_all | solution.py:294
  104.1 25.9 %collective-permute-start.7 = (bf16[4,16,32,128]{3,2,1,0:T(8,128)(2,1)}, bf16[4,16,32,128]{3,2,1,0:T(8,128)(2,1)}, u32[]{:S(2)}, u32[]{:S(2)}) collective-permute-start(bf16[4,16,32,128]{3,2,1,0:T(8,128)(2,1)} %collective-permute-done.3.refs_1_), channel_id=1, source_target_pairs={{0,12},{4,0},{8,4},{12,8},{16,28},{20,16},{24,20},{28,24},{32,44},... | collective-permute-start | bytes 1572872 | tf_op jit(solution)/shard_map/ppermute | solution.py:357
  109.4 20.6 %collective-permute-start.6 = (bf16[4,16,32,128]{3,2,1,0:T(8,128)(2,1)}, bf16[4,16,32,128]{3,2,1,0:T(8,128)(2,1)}, u32[]{:S(2)}, u32[]{:S(2)}) collective-permute-start(bf16[4,16,32,128]{3,2,1,0:T(8,128)(2,1)} %collective-permute-done.3.refs_1_), channel_id=1, source_target_pairs={{0,4},{4,8},{8,12},{12,0},{16,20},{20,24},{24,28},{28,16},{32,36},... | collective-permute-start | bytes 1572872 | tf_op jit(solution)/shard_map/ppermute | solution.py:356
  127.1 18.1 %collective-permute-start.9 = (bf16[512,512]{1,0:T(8,128)(2,1)S(1)}, bf16[512,512]{1,0:T(8,128)(2,1)S(1)}, u32[]{:S(2)}, u32[]{:S(2)}) collective-permute-start(bf16[512,512]{1,0:T(8,128)(2,1)S(1)} %mix.1.refs_0_), channel_id=1, source_target_pairs={{0,2},{1,3},{2,0},{3,1},{4,6},{5,7},{6,4},{7,5},{8,10},{9,11},{10,... | collective-permute-start | bytes 1572872 | tf_op jit(solution)/shard_map/ppermute | solution.py:363
  130.0 17.1 %collective-permute-start.12 = (bf16[4,16,32,128]{3,2,1,0:T(8,128)(2,1)}, bf16[4,16,32,128]{3,2,1,0:T(8,128)(2,1)S(1)}, u32[]{:S(2)}, u32[]{:S(2)}) collective-permute-start(bf16[4,16,32,128]{3,2,1,0:T(8,128)(2,1)} %collective-permute-done.7.refs_3_), channel_id=1, source_target_pairs={{0,12},{4,0},{8,4},{12,8},{16,28},{20,16},{24,20},{28,24},{32,44},... | collective-permute-start | bytes 1572872 | tf_op jit(solution)/shard_map/ppermute | solution.py:366
  131.9 15.2 %collective-permute-start.11 = (bf16[4,16,32,128]{3,2,1,0:T(8,128)(2,1)}, bf16[4,16,32,128]{3,2,1,0:T(8,128)(2,1)S(1)}, u32[]{:S(2)}, u32[]{:S(2)}) collective-permute-start(bf16[4,16,32,128]{3,2,1,0:T(8,128)(2,1)} %collective-permute-done.4.refs_4_), channel_id=1, source_target_pairs={{0,4},{4,8},{8,12},{12,0},{16,20},{20,24},{24,28},{28,16},{32,36},... | collective-permute-start | bytes 1572872 | tf_op jit(solution)/shard_map/ppermute | solution.py:365
  138.0 9.1 %collective-permute-start.8 = (bf16[512,512]{1,0:T(8,128)(2,1)S(1)}, bf16[512,512]{1,0:T(8,128)(2,1)S(1)}, u32[]{:S(2)}, u32[]{:S(2)}) collective-permute-start(bf16[512,512]{1,0:T(8,128)(2,1)S(1)} %mix.1.refs_0_), channel_id=1, source_target_pairs={{0,1},{1,0},{2,3},{3,2},{4,5},{5,4},{6,7},{7,6},{8,9},{9,8},{10,11... | collective-permute-start | bytes 1572872 | tf_op jit(solution)/shard_map/ppermute | solution.py:370
  145.2 3.8 %collective-permute-start.10 = (bf16[512,512]{1,0:T(8,128)(2,1)S(1)}, bf16[512,512]{1,0:T(8,128)(2,1)S(1)}, u32[]{:S(2)}, u32[]{:S(2)}) collective-permute-start(bf16[512,512]{1,0:T(8,128)(2,1)S(1)} %collective-permute-done.9.refs_2_), channel_id=1, source_target_pairs={{0,1},{1,0},{2,3},{3,2},{4,5},{5,4},{6,7},{7,6},{8,9},{9,8},{10,11... | collective-permute-start | bytes 1572872 | tf_op jit(solution)/shard_map/ppermute | solution.py:371

commit v6 on v5

--- a/solution.py
+++ b/solution.py
@@ -347,8 +347,10 @@
     col_own, keys_before, values_before, own_0 = barrier(
         (col_own, keys_before, values_before, own_0)
     )
-    keys_before, values_before, own_1 = barrier((keys_before, values_before, own_1))
     less_0 = lax.ppermute(own_0, "seq", x_up)
+    keys_before, values_before, own_0, own_1, less_0 = barrier(
+        (keys_before, values_before, own_0, own_1, less_0)
+    )
     more_0 = lax.ppermute(own_0, "seq", x_down)
     row_out, row_stat = row_attend(
         (seq % 2).astype(jnp.int32).reshape(1), queries, keys, values, keys_before, values_before
@@ -361,7 +363,7 @@
     near = [(i, i ^ 1) for i in range(N_MP)]
     far = [(i, i ^ 2) for i in range(N_MP)]
     across = lax.ppermute(attended, "mp", far)
-    after, less_0, more_0, less_1, more_1 = barrier((attended, less_0, more_0, less_1, more_1))
+    after, less_1, more_1 = barrier((attended, less_1, more_1))
     far_0 = lax.ppermute(less_0, "seq", x_up)
     far_1 = lax.ppermute(more_1, "seq", x_down)
     place = jnp.stack([seq // 4 % 8, seq % 4, mp]).astype(jnp.int32)

time: 154 us -> 152 us (0.987)
  waiting for transfers between devices: 57.4 us -> 53.9 us
  starting transfers between devices: 73.8 us -> 76 us
    all_to_all x2, waiting for transfers between devices: 55.5 us -> 52 us  [swap_columns(): lax.all_to_all(value, 'seq', split_axis=0, concat_axis=0, axis_index_grou...]
    ppermute x1, starting transfers between devices: 1.91 us -> 4.57 us  [body(): more_0 = lax.ppermute(own_0, 'seq', x_down)]
    ppermute x1, starting transfers between devices: 1.92 us -> 3.55 us  [body(): far_1 = lax.ppermute(more_1, 'seq', x_down)]
where the time goes in v6:
time: 152 us; the launch traced here: 151 us
  starting transfers between devices  76 us (50%)
  waiting for transfers between devices  53.9 us (35%)
  Pallas kernels  17.1 us (11%)
  local copies, waits for them, and re-layouts  2.29 us (2%)
  other arithmetic  1.85 us (1%)
    all_to_all x2, waiting for transfers between devices, swap_columns(): lax.all_to_all(value, 'seq', split_axis=0, concat_axis=0, axis_index_grou...  52 us
    all_to_all x2, starting transfers between devices, swap_columns(): lax.all_to_all(value, 'seq', split_axis=0, concat_axis=0, axis_index_grou...  30.6 us
    ppermute x1, starting transfers between devices, body(): beside = lax.ppermute(after, 'mp', near)  7.2 us
    ppermute x1, starting transfers between devices, turn(): return lax.ppermute(mine, ('seq', 'mp'), pairs)  7.19 us
    pallas_call x1, Pallas kernels, row_attend(): pl.pallas_call(row_kernel, out_shape=(jax.ShapeDtypeStruct((ROWS, WIDTH),...  5.51 us
    ppermute x1, starting transfers between devices, body(): more_0 = lax.ppermute(own_0, 'seq', x_down)  4.57 us
    ppermute x1, starting transfers between devices, body(): more_1 = lax.ppermute(own_1, 'seq', x_down)  4.43 us
    pallas_call x1, Pallas kernels, finish(): pl.pallas_call(finish_kernel, out_shape=(jax.ShapeDtypeStruct((ROWS, PLAN...  3.85 us
  transfers between devices with their start and end apart: 15, of which 3 were waited for; matrix products, arithmetic and copies ran while one was open for 2% of the time, Pallas kernels for 9%

profile of v6, /device:TPU:1, one launch (start us, length us, event | category | flops | bytes accessed | tf_op | source)
XLA Modules:
  0.0 151.5 jit_solution(6548514540784274994)
XLA Ops:
  0.0 7.2 %collective-permute-start = (bf16[32,512]{1,0:T(8,128)(2,1)}, bf16[32,512]{1,0:T(8,128)(2,1)S(1)}, u32[]{:S(2)}, u32[]{:S(2)}) collective-permute-start(bf16[32,512]{1,0:T(8,128)(2,1)} %bitcast.26), channel_id=1, source_target_pairs={{0,0},{1,128},{2,256},{3,384},{4,4},{5,132},{6,260},{7,388},{8,8},... | collective-permute-start | bytes 98312 | tf_op jit(solution)/shard_map/ppermute | solution.py:313
  7.2 1.8 %maximum_maximum_fusion = bf16[512,2048]{1,0:T(8,128)(2,1)S(1)} fusion(bf16[512,512]{1,0:T(8,128)(2,1)} %v_ref.1, bf16[512,512]{1,0:T(8,128)(2,1)} %k_ref.1, bf16[512,512]{1,0:T(8,128)(2,1)} %q_ref.1, bf16[2048]{0:T(1024)(128)(2,1)S(1)} %pad.3.clone), kind=kLoop, calls=%fused_computation | loop fusion | flops 8388608 | bytes 3674112 | tf_op jit(solution)/shard_map/concatenate | solution.py:334
  9.0 0.0 collective-permute-done
  9.1 0.1 constant_dynamic-update-slice_fusion
  9.1 0.0 copy-start.3
  9.1 1.3 copy-done.3
  10.5 18.4 %all-to-all-start = ((bf16[64,8,2048]{2,1,0:T(8,128)(2,1)}), bf16[64,8,2048]{2,1,0:T(8,128)(2,1)S(1)}, u32[]{:S(2)}, u32[]{:S(2)}) async-start(bf16[64,8,2048]{2,1,0:T(8,128)(2,1)} %bitcast.24), calls=%async_computation | async-start | bytes 4194304 | tf_op jit(solution)/shard_map/all_to_all | solution.py:294
  28.9 3.0 %collective-permute-start.1 = (bf16[512,512]{1,0:T(8,128)(2,1)}, bf16[512,512]{1,0:T(8,128)(2,1)}, u32[]{:S(2)}, u32[]{:S(2)}) collective-permute-start(bf16[512,512]{1,0:T(8,128)(2,1)} %k_ref.1), channel_id=1, source_target_pairs={{0,4},{8,12},{16,20},{24,28},{32,36},{40,44},{48,52},{56,60},{64,6... | collective-permute-start | bytes 1572872 | tf_op jit(solution)/shard_map/ppermute | solution.py:340
  31.9 2.1 %collective-permute-start.2 = (bf16[512,512]{1,0:T(8,128)(2,1)}, bf16[512,512]{1,0:T(8,128)(2,1)}, u32[]{:S(2)}, u32[]{:S(2)}) collective-permute-start(bf16[512,512]{1,0:T(8,128)(2,1)} %v_ref.1), channel_id=1, source_target_pairs={{0,4},{8,12},{16,20},{24,28},{32,36},{40,44},{48,52},{56,60},{64,6... | collective-permute-start | bytes 1572872 | tf_op jit(solution)/shard_map/ppermute | solution.py:341
  34.1 47.3 %all-to-all-done = bf16[64,8,2048]{2,1,0:T(8,128)(2,1)S(1)} async-done(((bf16[64,8,2048]{2,1,0:T(8,128)(2,1)}), bf16[64,8,2048]{2,1,0:T(8,128)(2,1)S(1)}, u32[]{:S(2)}, u32[]{:S(2)}) %all-to-all-start) | async-done | bytes 2097184 | tf_op jit(solution)/shard_map/all_to_all | solution.py:294
  81.4 3.1 %col_attend.1 = bf16[512,640]{1,0:T(8,128)(2,1)} custom-call(bf16[512,2048]{1,0:T(8,128)(2,1)S(1)} %bitcast.22), custom_call_target="tpu_custom_call" | custom-call | flops 199999995904 | bytes 1024 | tf_op jit(solution)/shard_map/col_attend/pallas_call | solution.py:174
  84.5 0.0 copy-start
  84.5 0.8 slice.4
  85.3 0.0 collective-permute-done.1.kp_ref
  85.3 0.0 collective-permute-done.2.vp_ref
  85.3 2.2 %collective-permute-start.4 = (bf16[4,16,32,128]{3,2,1,0:T(8,128)(2,1)}, bf16[4,16,32,128]{3,2,1,0:T(8,128)(2,1)S(1)}, u32[]{:S(2)}, u32[]{:S(2)}) collective-permute-start(bf16[4,16,32,128]{3,2,1,0:T(8,128)(2,1)} %bitcast.13.refs_0_), channel_id=1, source_target_pairs={{0,4},{4,8},{8,12},{12,0},{16,20},{20,24},{24,28},{28,16},{32,36},... | collective-permute-start | bytes 1572872 | tf_op jit(solution)/shard_map/ppermute | solution.py:350
  87.5 1.9 %collective-permute-start.3 = (bf16[4,16,32,128]{3,2,1,0:T(8,128)(2,1)}, bf16[4,16,32,128]{3,2,1,0:T(8,128)(2,1)}, u32[]{:S(2)}, u32[]{:S(2)}) collective-permute-start(bf16[4,16,32,128]{3,2,1,0:T(8,128)(2,1)} %bitcast.13.refs_0_), channel_id=1, source_target_pairs={{0,16},{4,20},{8,24},{12,28},{16,0},{20,4},{24,8},{28,12},{32,48},... | collective-permute-start | bytes 1572872 | tf_op jit(solution)/shard_map/ppermute | solution.py:344
  89.5 12.1 %all-to-all-start.1 = ((bf16[64,8,640]{2,1,0:T(8,128)(2,1)}), bf16[64,8,640]{2,1,0:T(8,128)(2,1)}, u32[]{:S(2)}, u32[]{:S(2)}) async-start(bf16[64,8,640]{2,1,0:T(8,128)(2,1)} %bitcast.16), calls=%async_computation.1 | async-start | bytes 1310720 | tf_op jit(solution)/shard_map/all_to_all | solution.py:294
  101.6 0.0 collective-permute-done.4.refs_4_
  101.6 0.0 copy-start.1
  101.6 0.0 collective-permute-done.3.refs_1_
  101.6 4.4 %collective-permute-start.6 = (bf16[4,16,32,128]{3,2,1,0:T(8,128)(2,1)}, bf16[4,16,32,128]{3,2,1,0:T(8,128)(2,1)}, u32[]{:S(2)}, u32[]{:S(2)}) collective-permute-start(bf16[4,16,32,128]{3,2,1,0:T(8,128)(2,1)} %collective-permute-done.3.refs_1_), channel_id=1, source_target_pairs={{0,12},{4,0},{8,4},{12,8},{16,28},{20,16},{24,20},{28,24},{32,44},... | collective-permute-start | bytes 1572872 | tf_op jit(solution)/shard_map/ppermute | solution.py:359
  106.1 1.9 %collective-permute-start.5 = (bf16[4,16,32,128]{3,2,1,0:T(8,128)(2,1)}, bf16[4,16,32,128]{3,2,1,0:T(8,128)(2,1)}, u32[]{:S(2)}, u32[]{:S(2)}) collective-permute-start(bf16[4,16,32,128]{3,2,1,0:T(8,128)(2,1)} %collective-permute-done.3.refs_1_), channel_id=1, source_target_pairs={{0,4},{4,8},{8,12},{12,0},{16,20},{20,24},{24,28},{28,16},{32,36},... | collective-permute-start | bytes 1572872 | tf_op jit(solution)/shard_map/ppermute | solution.py:358
  108.0 4.6 %collective-permute-start.7 = (bf16[4,16,32,128]{3,2,1,0:T(8,128)(2,1)}, bf16[4,16,32,128]{3,2,1,0:T(8,128)(2,1)}, u32[]{:S(2)}, u32[]{:S(2)}) collective-permute-start(bf16[4,16,32,128]{3,2,1,0:T(8,128)(2,1)} %bitcast.13.refs_0_), channel_id=1, source_target_pairs={{0,12},{4,0},{8,4},{12,8},{16,28},{20,16},{24,20},{28,24},{32,44},... | collective-permute-start | bytes 1572872 | tf_op jit(solution)/shard_map/ppermute | solution.py:354
  112.6 0.0 copy-done
  112.6 5.5 %row_attend.1 = (bf16[512,512]{1,0:T(8,128)(2,1)S(1)}, bf16[512,128]{1,0:T(8,128)(2,1)S(1)}) custom-call(s32[1]{0:T(128)} %bitcast.3.parity_ref, bf16[512,512]{1,0:T(8,128)(2,1)S(1)} %copy-done, bf16[512,512]{1,0:T(8,128)(2,1)} %k_ref.1, bf16[512,512]{1,0:T(8,128)(2,1)} %v_ref.1, bf16[512,512]{1,0:T(8,128)(2,1)} %collective-permute-done.1.kp_ref, ...), custom_call_target="tpu_custom_call" | custom-call | flops 199999995904 | bytes 1024 | tf_op jit(solution)/shard_map/row_attend/pallas_call | solution.py:112
  118.1 0.0 copy-done.1
  118.1 4.7 %all-to-all-done.1 = bf16[64,8,640]{2,1,0:T(8,128)(2,1)} async-done(((bf16[64,8,640]{2,1,0:T(8,128)(2,1)}), bf16[64,8,640]{2,1,0:T(8,128)(2,1)}, u32[]{:S(2)}, u32[]{:S(2)}) %all-to-all-start.1) | async-done | bytes 655392 | tf_op jit(solution)/shard_map/all_to_all | solution.py:294
  122.8 0.0 copy-start.2
  122.8 2.1 %mix.1.refs_0_ = bf16[512,512]{1,0:T(8,128)(2,1)S(1)} custom-call(bf16[512,512]{1,0:T(8,128)(2,1)S(1)} %get-tuple-element.31.row_ref, bf16[512,128]{1,0:T(8,128)(2,1)S(1)} %get-tuple-element.32.row_stat_ref, bf16[512,640]{1,0:T(8,128)(2,1)} %bitcast.17.col_ref), custom_call_target="tpu_custom_call" | custom-call | flops 1024 | bytes 1024 | tf_op jit(solution)/shard_map/mix/pallas_call | solution.py:202
  124.9 2.5 %collective-permute-start.9 = (bf16[512,512]{1,0:T(8,128)(2,1)S(1)}, bf16[512,512]{1,0:T(8,128)(2,1)S(1)}, u32[]{:S(2)}, u32[]{:S(2)}) collective-permute-start(bf16[512,512]{1,0:T(8,128)(2,1)S(1)} %mix.1.refs_0_), channel_id=1, source_target_pairs={{0,2},{1,3},{2,0},{3,1},{4,6},{5,7},{6,4},{7,5},{8,10},{9,11},{10,... | collective-permute-start | bytes 1572872 | tf_op jit(solution)/shard_map/ppermute | solution.py:365
  127.5 0.1 pad_add_fusion.place_ref
  127.5 2.9 %collective-permute-start.11 = (bf16[4,16,32,128]{3,2,1,0:T(8,128)(2,1)}, bf16[4,16,32,128]{3,2,1,0:T(8,128)(2,1)S(1)}, u32[]{:S(2)}, u32[]{:S(2)}) collective-permute-start(bf16[4,16,32,128]{3,2,1,0:T(8,128)(2,1)} %copy-done.1), channel_id=1, source_target_pairs={{0,4},{4,8},{8,12},{12,0},{16,20},{20,24},{24,28},{28,16},{32,36},... | collective-permute-start | bytes 1572872 | tf_op jit(solution)/shard_map/ppermute | solution.py:367
  130.5 0.0 collective-permute-done.6.refs_3_
  130.5 0.0 collective-permute-done.5.refs_5_
  130.5 3.6 %collective-permute-start.12 = (bf16[4,16,32,128]{3,2,1,0:T(8,128)(2,1)}, bf16[4,16,32,128]{3,2,1,0:T(8,128)(2,1)S(1)}, u32[]{:S(2)}, u32[]{:S(2)}) collective-permute-start(bf16[4,16,32,128]{3,2,1,0:T(8,128)(2,1)} %collective-permute-done.6.refs_3_), channel_id=1, source_target_pairs={{0,12},{4,0},{8,4},{12,8},{16,28},{20,16},{24,20},{28,24},{32,44},... | collective-permute-start | bytes 1572872 | tf_op jit(solution)/shard_map/ppermute | solution.py:368
  134.1 0.0 collective-permute-done.7.refs_2_
  134.1 0.0 copy-done.2
  134.1 2.5 %arrange.1.refs_6_ = bf16[4,1024,512]{2,1,0:T(8,128)(2,1)S(1)} custom-call(s32[3]{0:T(128)S(1)} %pad_add_fusion.place_ref, bf16[4,16,32,128]{3,2,1,0:T(8,128)(2,1)} %bitcast.13.refs_0_, bf16[4,16,32,128]{3,2,1,0:T(8,128)(2,1)} %collective-permute-done.3.refs_1_, bf16[4,16,32,128]{3,2,1,0:T(8,128)(2,1)} %collective-permute-done.7.refs_2_, ...), custom_call_target="tpu_custom_call" | custom-call | flops 1024 | bytes 1024 | tf_op jit(solution)/shard_map/arrange/pallas_call | solution.py:235
  136.6 7.2 %collective-permute-start.8 = (bf16[512,512]{1,0:T(8,128)(2,1)S(1)}, bf16[512,512]{1,0:T(8,128)(2,1)S(1)}, u32[]{:S(2)}, u32[]{:S(2)}) collective-permute-start(bf16[512,512]{1,0:T(8,128)(2,1)S(1)} %mix.1.refs_0_), channel_id=1, source_target_pairs={{0,1},{1,0},{2,3},{3,2},{4,5},{5,4},{6,7},{7,6},{8,9},{9,8},{10,11... | collective-permute-start | bytes 1572872 | tf_op jit(solution)/shard_map/ppermute | solution.py:372
  143.8 0.0 collective-permute-done.9.refs_2_
  143.8 1.9 %collective-permute-start.10 = (bf16[512,512]{1,0:T(8,128)(2,1)S(1)}, bf16[512,512]{1,0:T(8,128)(2,1)S(1)}, u32[]{:S(2)}, u32[]{:S(2)}) collective-permute-start(bf16[512,512]{1,0:T(8,128)(2,1)S(1)} %collective-permute-done.9.refs_2_), channel_id=1, source_target_pairs={{0,1},{1,0},{2,3},{3,2},{4,5},{5,4},{6,7},{7,6},{8,9},{9,8},{10,11... | collective-permute-start | bytes 1572872 | tf_op jit(solution)/shard_map/ppermute | solution.py:373
  145.7 0.0 collective-permute-done.11.refs_4_
  145.8 0.0 collective-permute-done.12.refs_5_
  145.8 0.0 collective-permute-done.8.refs_1_
  145.8 1.8 %collective-permute-done.10.refs_3_ = bf16[512,512]{1,0:T(8,128)(2,1)S(1)} collective-permute-done((bf16[512,512]{1,0:T(8,128)(2,1)S(1)}, bf16[512,512]{1,0:T(8,128)(2,1)S(1)}, u32[]{:S(2)}, u32[]{:S(2)}) %collective-permute-start.10) | collective-permute-done | bytes 524320 | tf_op jit(solution)/shard_map/ppermute | solution.py:373
  147.6 3.9 %finish.1 = (bf16[512,1024]{1,0:T(8,128)(2,1)}, bf16[4,1024,512]{2,1,0:T(8,128)(2,1)S(1)}) custom-call(s32[3]{0:T(128)S(1)} %pad_add_fusion.place_ref, bf16[512,512]{1,0:T(8,128)(2,1)S(1)} %mix.1.refs_0_, bf16[512,512]{1,0:T(8,128)(2,1)S(1)} %collective-permute-done.8.refs_1_, ...), custom_call_target="tpu_custom_call", output_to_operand_aliasing={{1}: (7, {})} | custom-call | flops 1024 | bytes 1024 | tf_op jit(solution)/shard_map/finish/pallas_call | solution.py:272
  (4 shorter events, 0.1 us)
Async XLA Ops:
  0.0 9.0 %collective-permute-start = (bf16[32,512]{1,0:T(8,128)(2,1)}, bf16[32,512]{1,0:T(8,128)(2,1)S(1)}, u32[]{:S(2)}, u32[]{:S(2)}) collective-permute-start(bf16[32,512]{1,0:T(8,128)(2,1)} %bitcast.26), channel_id=1, source_target_pairs={{0,0},{1,128},{2,256},{3,384},{4,4},{5,132},{6,260},{7,388},{8,8},... | collective-permute-start | bytes 98312 | tf_op jit(solution)/shard_map/ppermute | solution.py:313
  9.1 1.3 copy-start.3
  10.5 70.9 %all-to-all-start = ((bf16[64,8,2048]{2,1,0:T(8,128)(2,1)}), bf16[64,8,2048]{2,1,0:T(8,128)(2,1)S(1)}, u32[]{:S(2)}, u32[]{:S(2)}) async-start(bf16[64,8,2048]{2,1,0:T(8,128)(2,1)} %bitcast.24), calls=%async_computation | async-start | bytes 4194304 | tf_op jit(solution)/shard_map/all_to_all | solution.py:294
  28.9 56.4 %collective-permute-start.1 = (bf16[512,512]{1,0:T(8,128)(2,1)}, bf16[512,512]{1,0:T(8,128)(2,1)}, u32[]{:S(2)}, u32[]{:S(2)}) collective-permute-start(bf16[512,512]{1,0:T(8,128)(2,1)} %k_ref.1), channel_id=1, source_target_pairs={{0,4},{8,12},{16,20},{24,28},{32,36},{40,44},{48,52},{56,60},{64,6... | collective-permute-start | bytes 1572872 | tf_op jit(solution)/shard_map/ppermute | solution.py:340
  31.9 53.4 %collective-permute-start.2 = (bf16[512,512]{1,0:T(8,128)(2,1)}, bf16[512,512]{1,0:T(8,128)(2,1)}, u32[]{:S(2)}, u32[]{:S(2)}) collective-permute-start(bf16[512,512]{1,0:T(8,128)(2,1)} %v_ref.1), channel_id=1, source_target_pairs={{0,4},{8,12},{16,20},{24,28},{32,36},{40,44},{48,52},{56,60},{64,6... | collective-permute-start | bytes 1572872 | tf_op jit(solution)/shard_map/ppermute | solution.py:341
  84.5 28.1 %copy-start = (bf16[512,512]{1,0:T(8,128)(2,1)S(1)}, bf16[512,512]{1,0:T(8,128)(2,1)}, u32[]{:S(2)}) copy-start(bf16[512,512]{1,0:T(8,128)(2,1)} %q_ref.1) | copy-start | bytes 1572868
  85.3 16.3 %collective-permute-start.4 = (bf16[4,16,32,128]{3,2,1,0:T(8,128)(2,1)}, bf16[4,16,32,128]{3,2,1,0:T(8,128)(2,1)S(1)}, u32[]{:S(2)}, u32[]{:S(2)}) collective-permute-start(bf16[4,16,32,128]{3,2,1,0:T(8,128)(2,1)} %bitcast.13.refs_0_), channel_id=1, source_target_pairs={{0,4},{4,8},{8,12},{12,0},{16,20},{20,24},{24,28},{28,16},{32,36},... | collective-permute-start | bytes 1572872 | tf_op jit(solution)/shard_map/ppermute | solution.py:350
  87.5 14.1 %collective-permute-start.3 = (bf16[4,16,32,128]{3,2,1,0:T(8,128)(2,1)}, bf16[4,16,32,128]{3,2,1,0:T(8,128)(2,1)}, u32[]{:S(2)}, u32[]{:S(2)}) collective-permute-start(bf16[4,16,32,128]{3,2,1,0:T(8,128)(2,1)} %bitcast.13.refs_0_), channel_id=1, source_target_pairs={{0,16},{4,20},{8,24},{12,28},{16,0},{20,4},{24,8},{28,12},{32,48},... | collective-permute-start | bytes 1572872 | tf_op jit(solution)/shard_map/ppermute | solution.py:344
  89.5 33.3 %all-to-all-start.1 = ((bf16[64,8,640]{2,1,0:T(8,128)(2,1)}), bf16[64,8,640]{2,1,0:T(8,128)(2,1)}, u32[]{:S(2)}, u32[]{:S(2)}) async-start(bf16[64,8,640]{2,1,0:T(8,128)(2,1)} %bitcast.16), calls=%async_computation.1 | async-start | bytes 1310720 | tf_op jit(solution)/shard_map/all_to_all | solution.py:294
  101.6 16.5 %copy-start.1 = (bf16[4,16,32,128]{3,2,1,0:T(8,128)(2,1)}, bf16[4,16,32,128]{3,2,1,0:T(8,128)(2,1)S(1)}, u32[]{:S(2)}) copy-start(bf16[4,16,32,128]{3,2,1,0:T(8,128)(2,1)S(1)} %collective-permute-done.4.refs_4_) | copy-start | bytes 1572868
  101.6 28.9 %collective-permute-start.6 = (bf16[4,16,32,128]{3,2,1,0:T(8,128)(2,1)}, bf16[4,16,32,128]{3,2,1,0:T(8,128)(2,1)}, u32[]{:S(2)}, u32[]{:S(2)}) collective-permute-start(bf16[4,16,32,128]{3,2,1,0:T(8,128)(2,1)} %collective-permute-done.3.refs_1_), channel_id=1, source_target_pairs={{0,12},{4,0},{8,4},{12,8},{16,28},{20,16},{24,20},{28,24},{32,44},... | collective-permute-start | bytes 1572872 | tf_op jit(solution)/shard_map/ppermute | solution.py:359
  106.1 24.4 %collective-permute-start.5 = (bf16[4,16,32,128]{3,2,1,0:T(8,128)(2,1)}, bf16[4,16,32,128]{3,2,1,0:T(8,128)(2,1)}, u32[]{:S(2)}, u32[]{:S(2)}) collective-permute-start(bf16[4,16,32,128]{3,2,1,0:T(8,128)(2,1)} %collective-permute-done.3.refs_1_), channel_id=1, source_target_pairs={{0,4},{4,8},{8,12},{12,0},{16,20},{20,24},{24,28},{28,16},{32,36},... | collective-permute-start | bytes 1572872 | tf_op jit(solution)/shard_map/ppermute | solution.py:358
  108.0 26.1 %collective-permute-start.7 = (bf16[4,16,32,128]{3,2,1,0:T(8,128)(2,1)}, bf16[4,16,32,128]{3,2,1,0:T(8,128)(2,1)}, u32[]{:S(2)}, u32[]{:S(2)}) collective-permute-start(bf16[4,16,32,128]{3,2,1,0:T(8,128)(2,1)} %bitcast.13.refs_0_), channel_id=1, source_target_pairs={{0,12},{4,0},{8,4},{12,8},{16,28},{20,16},{24,20},{28,24},{32,44},... | collective-permute-start | bytes 1572872 | tf_op jit(solution)/shard_map/ppermute | solution.py:354
  122.8 11.3 %copy-start.2 = (bf16[4,16,32,128]{3,2,1,0:T(8,128)(2,1)S(1)}, bf16[4,16,32,128]{3,2,1,0:T(8,128)(2,1)}, u32[]{:S(2)}) copy-start(bf16[4,16,32,128]{3,2,1,0:T(8,128)(2,1)} %copy-done.1) | copy-start | bytes 1572868
  124.9 18.9 %collective-permute-start.9 = (bf16[512,512]{1,0:T(8,128)(2,1)S(1)}, bf16[512,512]{1,0:T(8,128)(2,1)S(1)}, u32[]{:S(2)}, u32[]{:S(2)}) collective-permute-start(bf16[512,512]{1,0:T(8,128)(2,1)S(1)} %mix.1.refs_0_), channel_id=1, source_target_pairs={{0,2},{1,3},{2,0},{3,1},{4,6},{5,7},{6,4},{7,5},{8,10},{9,11},{10,... | collective-permute-start | bytes 1572872 | tf_op jit(solution)/shard_map/ppermute | solution.py:365
  127.5 18.2 %collective-permute-start.11 = (bf16[4,16,32,128]{3,2,1,0:T(8,128)(2,1)}, bf16[4,16,32,128]{3,2,1,0:T(8,128)(2,1)S(1)}, u32[]{:S(2)}, u32[]{:S(2)}) collective-permute-start(bf16[4,16,32,128]{3,2,1,0:T(8,128)(2,1)} %copy-done.1), channel_id=1, source_target_pairs={{0,4},{4,8},{8,12},{12,0},{16,20},{20,24},{24,28},{28,16},{32,36},... | collective-permute-start | bytes 1572872 | tf_op jit(solution)/shard_map/ppermute | solution.py:367
  130.5 15.3 %collective-permute-start.12 = (bf16[4,16,32,128]{3,2,1,0:T(8,128)(2,1)}, bf16[4,16,32,128]{3,2,1,0:T(8,128)(2,1)S(1)}, u32[]{:S(2)}, u32[]{:S(2)}) collective-permute-start(bf16[4,16,32,128]{3,2,1,0:T(8,128)(2,1)} %collective-permute-done.6.refs_3_), channel_id=1, source_target_pairs={{0,12},{4,0},{8,4},{12,8},{16,28},{20,16},{24,20},{28,24},{32,44},... | collective-permute-start | bytes 1572872 | tf_op jit(solution)/shard_map/ppermute | solution.py:368
  136.6 9.2 %collective-permute-start.8 = (bf16[512,512]{1,0:T(8,128)(2,1)S(1)}, bf16[512,512]{1,0:T(8,128)(2,1)S(1)}, u32[]{:S(2)}, u32[]{:S(2)}) collective-permute-start(bf16[512,512]{1,0:T(8,128)(2,1)S(1)} %mix.1.refs_0_), channel_id=1, source_target_pairs={{0,1},{1,0},{2,3},{3,2},{4,5},{5,4},{6,7},{7,6},{8,9},{9,8},{10,11... | collective-permute-start | bytes 1572872 | tf_op jit(solution)/shard_map/ppermute | solution.py:372
  143.8 3.8 %collective-permute-start.10 = (bf16[512,512]{1,0:T(8,128)(2,1)S(1)}, bf16[512,512]{1,0:T(8,128)(2,1)S(1)}, u32[]{:S(2)}, u32[]{:S(2)}) collective-permute-start(bf16[512,512]{1,0:T(8,128)(2,1)S(1)} %collective-permute-done.9.refs_2_), channel_id=1, source_target_pairs={{0,1},{1,0},{2,3},{3,2},{4,5},{5,4},{6,7},{7,6},{8,9},{9,8},{10,11... | collective-permute-start | bytes 1572872 | tf_op jit(solution)/shard_map/ppermute | solution.py:373

commit v7 on v6

--- a/solution.py
+++ b/solution.py
@@ -66,8 +66,7 @@
     return top, weights, total
 
 
-def row_kernel(parity_ref, q_ref, k_ref, v_ref, kp_ref, vp_ref, out_ref, packed_ref):
-    odd = parity_ref[0] == 1
+def own_kernel(q_ref, k_ref, v_ref, out_ref, stat_ref):
     block = 128
     token = lax.broadcasted_iota(jnp.int32, (block, block), 0)
     other = lax.broadcasted_iota(jnp.int32, (block, block), 1)
@@ -78,39 +77,84 @@
         scores = []
         for head in heads:
             lanes = head_lanes(head)
-            q = q_ref[here, lanes]
             row = []
             for c in range(b + 1):
-                score = nt_dot(q, k_ref[c * block : (c + 1) * block, lanes]) * FACTOR
+                there = slice(c * block, (c + 1) * block)
+                score = nt_dot(q_ref[here, lanes], k_ref[there, lanes]) * FACTOR
                 row.append(score if c < b else jnp.where(causal, score, NEG))
-            for c in range(ROWS // block):
-                score = nt_dot(q, kp_ref[c * block : (c + 1) * block, lanes]) * FACTOR
-                row.append(jnp.where(odd, score, NEG))
             scores.append(row)
         soft = [soften(row) for row in scores]
         stats = jnp.zeros((block, 128), jnp.float32)
         for head in heads:
             lanes = head_lanes(head)
             top, weights, total = soft[head]
-            weights = [w.astype(jnp.bfloat16) for w in weights]
             out = jnp.dot(
-                jnp.concatenate(weights[: b + 1], axis=1),
+                jnp.concatenate([w.astype(jnp.bfloat16) for w in weights], axis=1),
                 v_ref[: (b + 1) * block, lanes],
-                preferred_element_type=jnp.float32,
-            ) + jnp.dot(
-                jnp.concatenate(weights[b + 1 :], axis=1),
-                vp_ref[:, lanes],
                 preferred_element_type=jnp.float32,
             )
             out_ref[here, lanes] = out.astype(jnp.bfloat16)
             stats = stat_lanes(stats, head, top, total)
+        stat_ref[here, :] = stats
+
+
+def before_kernel(parity_ref, q_ref, kp_ref, vp_ref, own_ref, stat_ref, out_ref, packed_ref):
+    odd = parity_ref[0] == 1
+    block = 128
+    heads = range(HEADS_HERE)
+    for b in range(ROWS // block):
+        here = slice(b * block, (b + 1) * block)
+        scores = []
+        for head in heads:
+            lanes = head_lanes(head)
+            row = []
+            for c in range(ROWS // block):
+                there = slice(c * block, (c + 1) * block)
+                score = nt_dot(q_ref[here, lanes], kp_ref[there, lanes]) * FACTOR
+                row.append(jnp.where(odd, score, NEG))
+            scores.append(row)
+        soft = [soften(row) for row in scores]
+        own_stats = stat_ref[here, :]
+        stats = jnp.zeros((block, 128), jnp.float32)
+        for head in heads:
+            lanes = head_lanes(head)
+            top, weights, total = soft[head]
+            own_top = own_stats[:, head : head + 1]
+            own_total = own_stats[:, 4 + head : 5 + head]
+            highest = jnp.maximum(top, own_top)
+            factor, own_factor = jnp.exp2(top - highest), jnp.exp2(own_top - highest)
+            out = jnp.dot(
+                jnp.concatenate([w.astype(jnp.bfloat16) for w in weights], axis=1),
+                vp_ref[:, lanes],
+                preferred_element_type=jnp.float32,
+            )
+            out = factor * out + own_factor * own_ref[here, lanes].astype(jnp.float32)
+            out_ref[here, lanes] = out.astype(jnp.bfloat16)
+            total = factor * total + own_factor * own_total
+            stats = stat_lanes(stats, head, highest, total)
         packed_ref[here, :] = three_parts(stats)
 
 
-def row_attend(parity, q, k, v, kp, vp):
+def row_own(q, k, v):
     vmem = pl.BlockSpec(memory_space=pltpu.VMEM)
     return pl.pallas_call(
-        row_kernel,
+        own_kernel,
+        out_shape=(
+            jax.ShapeDtypeStruct((ROWS, WIDTH), jnp.bfloat16),
+            jax.ShapeDtypeStruct((ROWS, 128), jnp.float32),
+        ),
+        in_specs=[vmem] * 3,
+        out_specs=(vmem, vmem),
+        compiler_params=pltpu.CompilerParams(vmem_limit_bytes=VMEM),
+        cost_estimate=LARGE,
+        name="row_own",
+    )(q, k, v)
+
+
+def row_before(parity, q, kp, vp, own, stats):
+    vmem = pl.BlockSpec(memory_space=pltpu.VMEM)
+    return pl.pallas_call(
+        before_kernel,
         out_shape=(
             jax.ShapeDtypeStruct((ROWS, WIDTH), jnp.bfloat16),
             jax.ShapeDtypeStruct((ROWS, 128), jnp.bfloat16),
@@ -119,8 +163,8 @@
         out_specs=(vmem, vmem),
         compiler_params=pltpu.CompilerParams(vmem_limit_bytes=VMEM),
         cost_estimate=LARGE,
-        name="row_attend",
-    )(parity, q, k, v, kp, vp)
+        name="row_before",
+    )(parity, q, kp, vp, own, stats)
 
 
 def col_kernel(qkv_ref, out_ref):
@@ -340,6 +384,8 @@
     keys_before = lax.ppermute(keys, "seq", to_odd)
     values_before = lax.ppermute(values, "seq", to_odd)
 
+    half_out, half_stat = row_own(queries, keys, values)
+    arrived, half_out, half_stat = barrier((arrived, half_out, half_stat))
     own_0 = weight_piece(arrived[:, 3 * WIDTH :])
     own_1 = lax.ppermute(own_0, "seq", y_pair)
 
@@ -352,8 +398,9 @@
         (keys_before, values_before, own_0, own_1, less_0)
     )
     more_0 = lax.ppermute(own_0, "seq", x_down)
-    row_out, row_stat = row_attend(
-        (seq % 2).astype(jnp.int32).reshape(1), queries, keys, values, keys_before, values_before
+    parity = (seq % 2).astype(jnp.int32).reshape(1)
+    row_out, row_stat = row_before(
+        parity, queries, keys_before, values_before, half_out, half_stat
     )
     less_1 = lax.ppermute(own_1, "seq", x_up)
     more_1 = lax.ppermute(own_1, "seq", x_down)

time: 152 us -> 163 us (1.072)
  Pallas kernels: 17.1 us -> 22.7 us
  starting transfers between devices: 76 us -> 79.7 us
    pallas_call x1 -> x2, Pallas kernels: 5.51 us -> 9.57 us  [the longest x1 7.56 us: row_before(): pl.pallas_call(before_kernel, out_shape=(jax.ShapeDtypeStruct((ROWS, WIDT...]
    ppermute x1, starting transfers between devices: 4.43 us -> 6.74 us  [body(): more_1 = lax.ppermute(own_1, 'seq', x_down)]
  transfers between devices with their start and end apart: 15 -> 15, of which waited for: 3 -> 5; matrix products, arithmetic and copies ran while one was open for 2% -> 2% of each run, Pallas kernels for 9% -> 12%
where the time goes in v7:
time: 163 us; the launch traced here: 162 us
  starting transfers between devices  79.7 us (49%)
  waiting for transfers between devices  53.9 us (33%)
  Pallas kernels  22.7 us (14%)
  local copies, waits for them, and re-layouts  3.32 us (2%)
  other arithmetic  1.84 us (1%)
    all_to_all x2, waiting for transfers between devices, swap_columns(): lax.all_to_all(value, 'seq', split_axis=0, concat_axis=0, axis_index_grou...  51 us
    all_to_all x2, starting transfers between devices, swap_columns(): lax.all_to_all(value, 'seq', split_axis=0, concat_axis=0, axis_index_grou...  32 us
    pallas_call x1, Pallas kernels, row_before(): pl.pallas_call(before_kernel, out_shape=(jax.ShapeDtypeStruct((ROWS, WIDT...  7.56 us
    ppermute x1, starting transfers between devices, turn(): return lax.ppermute(mine, ('seq', 'mp'), pairs)  7.19 us
    ppermute x1, starting transfers between devices, body(): more_1 = lax.ppermute(own_1, 'seq', x_down)  6.74 us
    ppermute x1, starting transfers between devices, body(): beside = lax.ppermute(after, 'mp', near)  6.21 us
    ppermute x1, starting transfers between devices, body(): more_0 = lax.ppermute(own_0, 'seq', x_down)  4.75 us
    pallas_call x1, Pallas kernels, col_attend(): pl.pallas_call(col_kernel, out_shape=jax.ShapeDtypeStruct((ROWS, WIDTH +...  4.69 us
  transfers between devices with their start and end apart: 15, of which 5 were waited for; matrix products, arithmetic and copies ran while one was open for 2% of the time, Pallas kernels for 12%

profile of v7, /device:TPU:1, one launch (start us, length us, event | category | flops | bytes accessed | tf_op | source)
XLA Modules:
  0.0 162.0 jit_solution(1163369618886513964)
XLA Ops:
  0.0 7.2 %collective-permute-start = (bf16[32,512]{1,0:T(8,128)(2,1)}, bf16[32,512]{1,0:T(8,128)(2,1)S(1)}, u32[]{:S(2)}, u32[]{:S(2)}) collective-permute-start(bf16[32,512]{1,0:T(8,128)(2,1)} %bitcast.24), channel_id=1, source_target_pairs={{0,0},{1,128},{2,256},{3,384},{4,4},{5,132},{6,260},{7,388},{8,8},... | collective-permute-start | bytes 98312 | tf_op jit(solution)/shard_map/ppermute | solution.py:357
  7.2 3.9 %collective-permute-start.1 = (bf16[512,512]{1,0:T(8,128)(2,1)}, bf16[512,512]{1,0:T(8,128)(2,1)}, u32[]{:S(2)}, u32[]{:S(2)}) collective-permute-start(bf16[512,512]{1,0:T(8,128)(2,1)} %k_ref.1), channel_id=1, source_target_pairs={{0,4},{8,12},{16,20},{24,28},{32,36},{40,44},{48,52},{56,60},{64,6... | collective-permute-start | bytes 1572872 | tf_op jit(solution)/shard_map/ppermute | solution.py:384
  11.1 2.1 %collective-permute-start.2 = (bf16[512,512]{1,0:T(8,128)(2,1)}, bf16[512,512]{1,0:T(8,128)(2,1)}, u32[]{:S(2)}, u32[]{:S(2)}) collective-permute-start(bf16[512,512]{1,0:T(8,128)(2,1)} %v_ref.1), channel_id=1, source_target_pairs={{0,4},{8,12},{16,20},{24,28},{32,36},{40,44},{48,52},{56,60},{64,6... | collective-permute-start | bytes 1572872 | tf_op jit(solution)/shard_map/ppermute | solution.py:385
  13.2 1.8 %maximum_maximum_fusion = bf16[512,2048]{1,0:T(8,128)(2,1)S(1)} fusion(bf16[512,512]{1,0:T(8,128)(2,1)} %v_ref.1, bf16[512,512]{1,0:T(8,128)(2,1)} %k_ref.1, bf16[512,512]{1,0:T(8,128)(2,1)} %q_ref.3, bf16[2048]{0:T(1024)(128)(2,1)S(1)} %pad.3.clone), kind=kLoop, calls=%fused_computation | loop fusion | flops 8388608 | bytes 3674112 | tf_op jit(solution)/shard_map/concatenate | solution.py:378
  15.0 0.0 collective-permute-done
  15.1 0.1 constant_dynamic-update-slice_fusion
  15.1 0.0 copy-start.5
  15.2 1.3 copy-done.5
  16.5 0.0 copy-start
  16.5 0.0 copy-start.1
  16.5 0.0 copy-start.2
  16.5 14.4 %all-to-all-start = ((bf16[64,8,2048]{2,1,0:T(8,128)(2,1)}), bf16[64,8,2048]{2,1,0:T(8,128)(2,1)}, u32[]{:S(2)}, u32[]{:S(2)}) async-start(bf16[64,8,2048]{2,1,0:T(8,128)(2,1)} %bitcast.22), calls=%async_computation | async-start | bytes 4194304 | tf_op jit(solution)/shard_map/all_to_all | solution.py:338
  30.9 0.0 copy-done
  30.9 0.0 copy-done.1
  30.9 0.0 copy-done.2
  30.9 2.0 %row_own.1 = (bf16[512,512]{1,0:T(8,128)(2,1)S(1)}, f32[512,128]{1,0:T(8,128)S(1)}) custom-call(bf16[512,512]{1,0:T(8,128)(2,1)S(1)} %copy-done.2, bf16[512,512]{1,0:T(8,128)(2,1)S(1)} %copy-done, bf16[512,512]{1,0:T(8,128)(2,1)S(1)} %copy-done.1), custom_call_target="tpu_custom_call" | custom-call | flops 199999995904 | bytes 1024 | tf_op jit(solution)/shard_map/row_own/pallas_call | solution.py:140
  32.9 50.5 %all-to-all-done = bf16[64,8,2048]{2,1,0:T(8,128)(2,1)} async-done(((bf16[64,8,2048]{2,1,0:T(8,128)(2,1)}), bf16[64,8,2048]{2,1,0:T(8,128)(2,1)}, u32[]{:S(2)}, u32[]{:S(2)}) %all-to-all-start) | async-done | bytes 2097184 | tf_op jit(solution)/shard_map/all_to_all | solution.py:338
  83.4 4.7 %col_attend.1 = bf16[512,640]{1,0:T(8,128)(2,1)} custom-call(bf16[512,2048]{1,0:T(8,128)(2,1)} %bitcast.10.qkv_ref), custom_call_target="tpu_custom_call" | custom-call | flops 199999995904 | bytes 1024 | tf_op jit(solution)/shard_map/col_attend/pallas_call | solution.py:218
  88.1 1.9 %slice.3 = bf16[512,512]{1,0:T(8,128)(2,1)} slice(bf16[512,2048]{1,0:T(8,128)(2,1)} %bitcast.10.qkv_ref), slice={[0:512], [1536:2048]} | slice | bytes 1048576 | tf_op jit(solution)/shard_map/slice | solution.py:389
  90.0 0.0 collective-permute-done.1.kp_ref
  90.0 0.0 collective-permute-done.2.vp_ref
  90.0 1.9 %collective-permute-start.4 = (bf16[4,16,32,128]{3,2,1,0:T(8,128)(2,1)}, bf16[4,16,32,128]{3,2,1,0:T(8,128)(2,1)S(1)}, u32[]{:S(2)}, u32[]{:S(2)}) collective-permute-start(bf16[4,16,32,128]{3,2,1,0:T(8,128)(2,1)} %bitcast.13.refs_0_), channel_id=1, source_target_pairs={{0,4},{4,8},{8,12},{12,0},{16,20},{20,24},{24,28},{28,16},{32,36},... | collective-permute-start | bytes 1572872 | tf_op jit(solution)/shard_map/ppermute | solution.py:396
  91.9 1.9 %collective-permute-start.3 = (bf16[4,16,32,128]{3,2,1,0:T(8,128)(2,1)}, bf16[4,16,32,128]{3,2,1,0:T(8,128)(2,1)}, u32[]{:S(2)}, u32[]{:S(2)}) collective-permute-start(bf16[4,16,32,128]{3,2,1,0:T(8,128)(2,1)} %bitcast.13.refs_0_), channel_id=1, source_target_pairs={{0,16},{4,20},{8,24},{12,28},{16,0},{20,4},{24,8},{28,12},{32,48},... | collective-permute-start | bytes 1572872 | tf_op jit(solution)/shard_map/ppermute | solution.py:390
  93.8 17.5 %all-to-all-start.1 = ((bf16[64,8,640]{2,1,0:T(8,128)(2,1)}), bf16[64,8,640]{2,1,0:T(8,128)(2,1)}, u32[]{:S(2)}, u32[]{:S(2)}) async-start(bf16[64,8,640]{2,1,0:T(8,128)(2,1)} %bitcast.16), calls=%async_computation.1 | async-start | bytes 1310720 | tf_op jit(solution)/shard_map/all_to_all | solution.py:338
  111.4 0.0 collective-permute-done.4.refs_4_
  111.4 0.0 copy-start.3
  111.4 0.0 collective-permute-done.3.refs_1_
  111.4 6.7 %collective-permute-start.6 = (bf16[4,16,32,128]{3,2,1,0:T(8,128)(2,1)}, bf16[4,16,32,128]{3,2,1,0:T(8,128)(2,1)}, u32[]{:S(2)}, u32[]{:S(2)}) collective-permute-start(bf16[4,16,32,128]{3,2,1,0:T(8,128)(2,1)} %collective-permute-done.3.refs_1_), channel_id=1, source_target_pairs={{0,12},{4,0},{8,4},{12,8},{16,28},{20,16},{24,20},{28,24},{32,44},... | collective-permute-start | bytes 1572872 | tf_op jit(solution)/shard_map/ppermute | solution.py:406
  118.2 1.9 %collective-permute-start.5 = (bf16[4,16,32,128]{3,2,1,0:T(8,128)(2,1)}, bf16[4,16,32,128]{3,2,1,0:T(8,128)(2,1)}, u32[]{:S(2)}, u32[]{:S(2)}) collective-permute-start(bf16[4,16,32,128]{3,2,1,0:T(8,128)(2,1)} %collective-permute-done.3.refs_1_), channel_id=1, source_target_pairs={{0,4},{4,8},{8,12},{12,0},{16,20},{20,24},{24,28},{28,16},{32,36},... | collective-permute-start | bytes 1572872 | tf_op jit(solution)/shard_map/ppermute | solution.py:405
  120.1 4.8 %collective-permute-start.7 = (bf16[4,16,32,128]{3,2,1,0:T(8,128)(2,1)}, bf16[4,16,32,128]{3,2,1,0:T(8,128)(2,1)}, u32[]{:S(2)}, u32[]{:S(2)}) collective-permute-start(bf16[4,16,32,128]{3,2,1,0:T(8,128)(2,1)} %bitcast.13.refs_0_), channel_id=1, source_target_pairs={{0,12},{4,0},{8,4},{12,8},{16,28},{20,16},{24,20},{28,24},{32,44},... | collective-permute-start | bytes 1572872 | tf_op jit(solution)/shard_map/ppermute | solution.py:400
  124.9 7.6 %row_before.1 = (bf16[512,512]{1,0:T(8,128)(2,1)S(1)}, bf16[512,128]{1,0:T(8,128)(2,1)S(1)}) custom-call(s32[1]{0:T(128)} %bitcast.3.parity_ref, bf16[512,512]{1,0:T(8,128)(2,1)S(1)} %copy-done.2, bf16[512,512]{1,0:T(8,128)(2,1)} %collective-permute-done.1.kp_ref, bf16[512,512]{1,0:T(8,128)(2,1)} %collective-permute-done.2.vp_ref, ...), custom_call_target="tpu_custom_call" | custom-call | flops 199999995904 | bytes 1024 | tf_op jit(solution)/shard_map/row_before/pallas_call | solution.py:156
  132.4 0.0 copy-done.3
  132.4 0.6 all-to-all-done.1
  133.0 0.0 copy-start.4
  133.0 2.1 %mix.1.refs_0_ = bf16[512,512]{1,0:T(8,128)(2,1)S(1)} custom-call(bf16[512,512]{1,0:T(8,128)(2,1)S(1)} %get-tuple-element.41.row_ref, bf16[512,128]{1,0:T(8,128)(2,1)S(1)} %get-tuple-element.42.row_stat_ref, bf16[512,640]{1,0:T(8,128)(2,1)} %bitcast.17.col_ref), custom_call_target="tpu_custom_call" | custom-call | flops 1024 | bytes 1024 | tf_op jit(solution)/shard_map/mix/pallas_call | solution.py:246
  135.1 2.7 %collective-permute-start.9 = (bf16[512,512]{1,0:T(8,128)(2,1)S(1)}, bf16[512,512]{1,0:T(8,128)(2,1)S(1)}, u32[]{:S(2)}, u32[]{:S(2)}) collective-permute-start(bf16[512,512]{1,0:T(8,128)(2,1)S(1)} %mix.1.refs_0_), channel_id=1, source_target_pairs={{0,2},{1,3},{2,0},{3,1},{4,6},{5,7},{6,4},{7,5},{8,10},{9,11},{10,... | collective-permute-start | bytes 1572872 | tf_op jit(solution)/shard_map/ppermute | solution.py:412
  137.9 0.1 pad_add_fusion.place_ref
  138.0 3.5 %collective-permute-start.11 = (bf16[4,16,32,128]{3,2,1,0:T(8,128)(2,1)}, bf16[4,16,32,128]{3,2,1,0:T(8,128)(2,1)S(1)}, u32[]{:S(2)}, u32[]{:S(2)}) collective-permute-start(bf16[4,16,32,128]{3,2,1,0:T(8,128)(2,1)} %copy-done.3), channel_id=1, source_target_pairs={{0,4},{4,8},{8,12},{12,0},{16,20},{20,24},{24,28},{28,16},{32,36},... | collective-permute-start | bytes 1572872 | tf_op jit(solution)/shard_map/ppermute | solution.py:414
  141.5 0.0 collective-permute-done.6.refs_3_
  141.5 0.0 collective-permute-done.5.refs_5_
  141.5 3.0 %collective-permute-start.12 = (bf16[4,16,32,128]{3,2,1,0:T(8,128)(2,1)}, bf16[4,16,32,128]{3,2,1,0:T(8,128)(2,1)S(1)}, u32[]{:S(2)}, u32[]{:S(2)}) collective-permute-start(bf16[4,16,32,128]{3,2,1,0:T(8,128)(2,1)} %collective-permute-done.6.refs_3_), channel_id=1, source_target_pairs={{0,12},{4,0},{8,4},{12,8},{16,28},{20,16},{24,20},{28,24},{32,44},... | collective-permute-start | bytes 1572872 | tf_op jit(solution)/shard_map/ppermute | solution.py:415
  144.5 1.0 collective-permute-done.7.refs_2_
  145.5 0.0 copy-done.4
  145.5 2.5 %arrange.1.refs_6_ = bf16[4,1024,512]{2,1,0:T(8,128)(2,1)S(1)} custom-call(s32[3]{0:T(128)S(1)} %pad_add_fusion.place_ref, bf16[4,16,32,128]{3,2,1,0:T(8,128)(2,1)} %bitcast.13.refs_0_, bf16[4,16,32,128]{3,2,1,0:T(8,128)(2,1)} %collective-permute-done.3.refs_1_, bf16[4,16,32,128]{3,2,1,0:T(8,128)(2,1)} %collective-permute-done.7.refs_2_, ...), custom_call_target="tpu_custom_call" | custom-call | flops 1024 | bytes 1024 | tf_op jit(solution)/shard_map/arrange/pallas_call | solution.py:279
  148.0 6.2 %collective-permute-start.8 = (bf16[512,512]{1,0:T(8,128)(2,1)S(1)}, bf16[512,512]{1,0:T(8,128)(2,1)S(1)}, u32[]{:S(2)}, u32[]{:S(2)}) collective-permute-start(bf16[512,512]{1,0:T(8,128)(2,1)S(1)} %mix.1.refs_0_), channel_id=1, source_target_pairs={{0,1},{1,0},{2,3},{3,2},{4,5},{5,4},{6,7},{7,6},{8,9},{9,8},{10,11... | collective-permute-start | bytes 1572872 | tf_op jit(solution)/shard_map/ppermute | solution.py:419
  154.2 0.0 collective-permute-done.9.refs_2_
  154.2 1.9 %collective-permute-start.10 = (bf16[512,512]{1,0:T(8,128)(2,1)S(1)}, bf16[512,512]{1,0:T(8,128)(2,1)S(1)}, u32[]{:S(2)}, u32[]{:S(2)}) collective-permute-start(bf16[512,512]{1,0:T(8,128)(2,1)S(1)} %collective-permute-done.9.refs_2_), channel_id=1, source_target_pairs={{0,1},{1,0},{2,3},{3,2},{4,5},{5,4},{6,7},{7,6},{8,9},{9,8},{10,11... | collective-permute-start | bytes 1572872 | tf_op jit(solution)/shard_map/ppermute | solution.py:420
  156.1 0.0 collective-permute-done.11.refs_4_
  156.1 0.5 collective-permute-done.12.refs_5_
  156.6 0.0 collective-permute-done.8.refs_1_
  156.6 1.4 collective-permute-done.10.refs_3_
  158.0 3.9 %finish.1 = (bf16[512,1024]{1,0:T(8,128)(2,1)}, bf16[4,1024,512]{2,1,0:T(8,128)(2,1)S(1)}) custom-call(s32[3]{0:T(128)S(1)} %pad_add_fusion.place_ref, bf16[512,512]{1,0:T(8,128)(2,1)S(1)} %mix.1.refs_0_, bf16[512,512]{1,0:T(8,128)(2,1)S(1)} %collective-permute-done.8.refs_1_, ...), custom_call_target="tpu_custom_call", output_to_operand_aliasing={{1}: (7, {})} | custom-call | flops 1024 | bytes 1024 | tf_op jit(solution)/shard_map/finish/pallas_call | solution.py:316
  (4 shorter events, 0.1 us)
Async XLA Ops:
  0.0 15.0 %collective-permute-start = (bf16[32,512]{1,0:T(8,128)(2,1)}, bf16[32,512]{1,0:T(8,128)(2,1)S(1)}, u32[]{:S(2)}, u32[]{:S(2)}) collective-permute-start(bf16[32,512]{1,0:T(8,128)(2,1)} %bitcast.24), channel_id=1, source_target_pairs={{0,0},{1,128},{2,256},{3,384},{4,4},{5,132},{6,260},{7,388},{8,8},... | collective-permute-start | bytes 98312 | tf_op jit(solution)/shard_map/ppermute | solution.py:357
  7.2 82.8 %collective-permute-start.1 = (bf16[512,512]{1,0:T(8,128)(2,1)}, bf16[512,512]{1,0:T(8,128)(2,1)}, u32[]{:S(2)}, u32[]{:S(2)}) collective-permute-start(bf16[512,512]{1,0:T(8,128)(2,1)} %k_ref.1), channel_id=1, source_target_pairs={{0,4},{8,12},{16,20},{24,28},{32,36},{40,44},{48,52},{56,60},{64,6... | collective-permute-start | bytes 1572872 | tf_op jit(solution)/shard_map/ppermute | solution.py:384
  11.1 78.8 %collective-permute-start.2 = (bf16[512,512]{1,0:T(8,128)(2,1)}, bf16[512,512]{1,0:T(8,128)(2,1)}, u32[]{:S(2)}, u32[]{:S(2)}) collective-permute-start(bf16[512,512]{1,0:T(8,128)(2,1)} %v_ref.1), channel_id=1, source_target_pairs={{0,4},{8,12},{16,20},{24,28},{32,36},{40,44},{48,52},{56,60},{64,6... | collective-permute-start | bytes 1572872 | tf_op jit(solution)/shard_map/ppermute | solution.py:385
  15.1 1.3 copy-start.5
  16.5 14.4 %copy-start = (bf16[512,512]{1,0:T(8,128)(2,1)S(1)}, bf16[512,512]{1,0:T(8,128)(2,1)}, u32[]{:S(2)}) copy-start(bf16[512,512]{1,0:T(8,128)(2,1)} %k_ref.1) | copy-start | bytes 1572868
  16.5 14.4 %copy-start.1 = (bf16[512,512]{1,0:T(8,128)(2,1)S(1)}, bf16[512,512]{1,0:T(8,128)(2,1)}, u32[]{:S(2)}) copy-start(bf16[512,512]{1,0:T(8,128)(2,1)} %v_ref.1) | copy-start | bytes 1572868
  16.5 14.4 %copy-start.2 = (bf16[512,512]{1,0:T(8,128)(2,1)S(1)}, bf16[512,512]{1,0:T(8,128)(2,1)}, u32[]{:S(2)}) copy-start(bf16[512,512]{1,0:T(8,128)(2,1)} %q_ref.3) | copy-start | bytes 1572868
  16.5 66.9 %all-to-all-start = ((bf16[64,8,2048]{2,1,0:T(8,128)(2,1)}), bf16[64,8,2048]{2,1,0:T(8,128)(2,1)}, u32[]{:S(2)}, u32[]{:S(2)}) async-start(bf16[64,8,2048]{2,1,0:T(8,128)(2,1)} %bitcast.22), calls=%async_computation | async-start | bytes 4194304 | tf_op jit(solution)/shard_map/all_to_all | solution.py:338
  90.0 21.4 %collective-permute-start.4 = (bf16[4,16,32,128]{3,2,1,0:T(8,128)(2,1)}, bf16[4,16,32,128]{3,2,1,0:T(8,128)(2,1)S(1)}, u32[]{:S(2)}, u32[]{:S(2)}) collective-permute-start(bf16[4,16,32,128]{3,2,1,0:T(8,128)(2,1)} %bitcast.13.refs_0_), channel_id=1, source_target_pairs={{0,4},{4,8},{8,12},{12,0},{16,20},{20,24},{24,28},{28,16},{32,36},... | collective-permute-start | bytes 1572872 | tf_op jit(solution)/shard_map/ppermute | solution.py:396
  91.9 19.5 %collective-permute-start.3 = (bf16[4,16,32,128]{3,2,1,0:T(8,128)(2,1)}, bf16[4,16,32,128]{3,2,1,0:T(8,128)(2,1)}, u32[]{:S(2)}, u32[]{:S(2)}) collective-permute-start(bf16[4,16,32,128]{3,2,1,0:T(8,128)(2,1)} %bitcast.13.refs_0_), channel_id=1, source_target_pairs={{0,16},{4,20},{8,24},{12,28},{16,0},{20,4},{24,8},{28,12},{32,48},... | collective-permute-start | bytes 1572872 | tf_op jit(solution)/shard_map/ppermute | solution.py:390
  93.8 39.2 %all-to-all-start.1 = ((bf16[64,8,640]{2,1,0:T(8,128)(2,1)}), bf16[64,8,640]{2,1,0:T(8,128)(2,1)}, u32[]{:S(2)}, u32[]{:S(2)}) async-start(bf16[64,8,640]{2,1,0:T(8,128)(2,1)} %bitcast.16), calls=%async_computation.1 | async-start | bytes 1310720 | tf_op jit(solution)/shard_map/all_to_all | solution.py:338
  111.4 21.0 %copy-start.3 = (bf16[4,16,32,128]{3,2,1,0:T(8,128)(2,1)}, bf16[4,16,32,128]{3,2,1,0:T(8,128)(2,1)S(1)}, u32[]{:S(2)}) copy-start(bf16[4,16,32,128]{3,2,1,0:T(8,128)(2,1)S(1)} %collective-permute-done.4.refs_4_) | copy-start | bytes 1572868
  111.4 30.1 %collective-permute-start.6 = (bf16[4,16,32,128]{3,2,1,0:T(8,128)(2,1)}, bf16[4,16,32,128]{3,2,1,0:T(8,128)(2,1)}, u32[]{:S(2)}, u32[]{:S(2)}) collective-permute-start(bf16[4,16,32,128]{3,2,1,0:T(8,128)(2,1)} %collective-permute-done.3.refs_1_), channel_id=1, source_target_pairs={{0,12},{4,0},{8,4},{12,8},{16,28},{20,16},{24,20},{28,24},{32,44},... | collective-permute-start | bytes 1572872 | tf_op jit(solution)/shard_map/ppermute | solution.py:406
  118.2 23.3 %collective-permute-start.5 = (bf16[4,16,32,128]{3,2,1,0:T(8,128)(2,1)}, bf16[4,16,32,128]{3,2,1,0:T(8,128)(2,1)}, u32[]{:S(2)}, u32[]{:S(2)}) collective-permute-start(bf16[4,16,32,128]{3,2,1,0:T(8,128)(2,1)} %collective-permute-done.3.refs_1_), channel_id=1, source_target_pairs={{0,4},{4,8},{8,12},{12,0},{16,20},{20,24},{24,28},{28,16},{32,36},... | collective-permute-start | bytes 1572872 | tf_op jit(solution)/shard_map/ppermute | solution.py:405
  120.1 25.4 %collective-permute-start.7 = (bf16[4,16,32,128]{3,2,1,0:T(8,128)(2,1)}, bf16[4,16,32,128]{3,2,1,0:T(8,128)(2,1)}, u32[]{:S(2)}, u32[]{:S(2)}) collective-permute-start(bf16[4,16,32,128]{3,2,1,0:T(8,128)(2,1)} %bitcast.13.refs_0_), channel_id=1, source_target_pairs={{0,12},{4,0},{8,4},{12,8},{16,28},{20,16},{24,20},{28,24},{32,44},... | collective-permute-start | bytes 1572872 | tf_op jit(solution)/shard_map/ppermute | solution.py:400
  133.0 12.5 %copy-start.4 = (bf16[4,16,32,128]{3,2,1,0:T(8,128)(2,1)S(1)}, bf16[4,16,32,128]{3,2,1,0:T(8,128)(2,1)}, u32[]{:S(2)}) copy-start(bf16[4,16,32,128]{3,2,1,0:T(8,128)(2,1)} %copy-done.3) | copy-start | bytes 1572868
  135.1 19.1 %collective-permute-start.9 = (bf16[512,512]{1,0:T(8,128)(2,1)S(1)}, bf16[512,512]{1,0:T(8,128)(2,1)S(1)}, u32[]{:S(2)}, u32[]{:S(2)}) collective-permute-start(bf16[512,512]{1,0:T(8,128)(2,1)S(1)} %mix.1.refs_0_), channel_id=1, source_target_pairs={{0,2},{1,3},{2,0},{3,1},{4,6},{5,7},{6,4},{7,5},{8,10},{9,11},{10,... | collective-permute-start | bytes 1572872 | tf_op jit(solution)/shard_map/ppermute | solution.py:412
  138.0 18.2 %collective-permute-start.11 = (bf16[4,16,32,128]{3,2,1,0:T(8,128)(2,1)}, bf16[4,16,32,128]{3,2,1,0:T(8,128)(2,1)S(1)}, u32[]{:S(2)}, u32[]{:S(2)}) collective-permute-start(bf16[4,16,32,128]{3,2,1,0:T(8,128)(2,1)} %copy-done.3), channel_id=1, source_target_pairs={{0,4},{4,8},{8,12},{12,0},{16,20},{20,24},{24,28},{28,16},{32,36},... | collective-permute-start | bytes 1572872 | tf_op jit(solution)/shard_map/ppermute | solution.py:414
  141.5 15.1 %collective-permute-start.12 = (bf16[4,16,32,128]{3,2,1,0:T(8,128)(2,1)}, bf16[4,16,32,128]{3,2,1,0:T(8,128)(2,1)S(1)}, u32[]{:S(2)}, u32[]{:S(2)}) collective-permute-start(bf16[4,16,32,128]{3,2,1,0:T(8,128)(2,1)} %collective-permute-done.6.refs_3_), channel_id=1, source_target_pairs={{0,12},{4,0},{8,4},{12,8},{16,28},{20,16},{24,20},{28,24},{32,44},... | collective-permute-start | bytes 1572872 | tf_op jit(solution)/shard_map/ppermute | solution.py:415
  148.0 8.6 %collective-permute-start.8 = (bf16[512,512]{1,0:T(8,128)(2,1)S(1)}, bf16[512,512]{1,0:T(8,128)(2,1)S(1)}, u32[]{:S(2)}, u32[]{:S(2)}) collective-permute-start(bf16[512,512]{1,0:T(8,128)(2,1)S(1)} %mix.1.refs_0_), channel_id=1, source_target_pairs={{0,1},{1,0},{2,3},{3,2},{4,5},{5,4},{6,7},{7,6},{8,9},{9,8},{10,11... | collective-permute-start | bytes 1572872 | tf_op jit(solution)/shard_map/ppermute | solution.py:419
  154.2 3.8 %collective-permute-start.10 = (bf16[512,512]{1,0:T(8,128)(2,1)S(1)}, bf16[512,512]{1,0:T(8,128)(2,1)S(1)}, u32[]{:S(2)}, u32[]{:S(2)}) collective-permute-start(bf16[512,512]{1,0:T(8,128)(2,1)S(1)} %collective-permute-done.9.refs_2_), channel_id=1, source_target_pairs={{0,1},{1,0},{2,3},{3,2},{4,5},{5,4},{6,7},{7,6},{8,9},{9,8},{10,11... | collective-permute-start | bytes 1572872 | tf_op jit(solution)/shard_map/ppermute | solution.py:420
